TPU v7x, 1024 devices: a whole 4x4x32 slice. The times are simulated.
1024 devices in a mesh: ep: 64 (over z, core), etp: 16 (over y, x).
Axes of the slice: x: 4, y: 4, z: 32, core: 2. Of those that a mesh axis runs over, the one named last changes fastest.
Arguments:
- tokens: bfloat16 [1024, 7168], P('ep', 'etp'), may hold values from -6 to 6
- grad_out: bfloat16 [1024, 7168], P('ep', 'etp'), may hold values from -6 to 6
- routes: int32 [1024, 8], P('ep'), may hold values from 0 to 31, all different within a row; in each aligned block of 16 rows (0 to 15, 16 to 31, ...) at most 5 rows name the same one
- route_gates: float32 [1024, 8], P('ep'), may hold values from 0.05 to 1
- gate_weight: bfloat16 [64, 3584, 2048], P('ep', None, 'etp'), may hold values from -0.0625 to 0.0625
- up_weight: bfloat16 [64, 3584, 2048], P('ep', None, 'etp'), may hold values from -0.0625 to 0.0625
- down_weight: bfloat16 [64, 2048, 3584], P('ep', 'etp'), may hold values from -0.125 to 0.125
Outputs:
- grad_tokens: bfloat16 [1024, 7168], P('ep', 'etp')
Inputs may be any that keep to these rules, and one draw needn't show every extreme that they name: `routes`: each row names 8 different experts. In each aligned block of 16 rows (the tokens of one ep index) no expert is named by more than 5 rows, and in some block one expert is named by exactly 5 rows.
All inputs are finite; a program needn't handle non-finite values.
Results may differ from a plain program's by a relative error of at most 0.024.
Values may be sent and summed in bfloat16 or wider, within the bound.
No kernel may reach another device: no remote copies, remote signals or barrier semaphores. Data moves between devices by JAX's collectives and lax.ppermute only.
A program may use at most 32 MiB of HBM per device.

v0:
```python
import jax
import jax.numpy as jnp
from jax import lax
from jax.sharding import PartitionSpec as P

CONTRACT = (((1,), (1,)), ((), ()))


def from_partner(block, axis, apart):
    count = lax.axis_size(axis)
    route = []
    for low in range(count):
        high = low | 1 << apart
        if high != low and high < count:
            route += [(low, high), (high, low)]
    return lax.ppermute(block, axis, route)


def slot_tables(routes, route_gates, experts, capacity):
    group_rows, top_count = routes.shape
    route_flat = routes.reshape(group_rows * top_count)
    gate_flat = route_gates.reshape(group_rows * top_count)
    expert_ids = jnp.arange(experts, dtype=jnp.int32)
    one_hot = (route_flat[:, None] == expert_ids[None, :]).astype(jnp.int32)
    earlier = jnp.cumsum(one_hot, axis=0) - one_hot
    route_rank = jnp.sum(earlier * one_hot, axis=1)
    slot_ids = jnp.arange(capacity, dtype=jnp.int32)
    chosen = (route_flat[None, None, :] == expert_ids[:, None, None]) & (
        route_rank[None, None, :] == slot_ids[None, :, None]
    )
    chosen = chosen.reshape(experts, capacity, group_rows, top_count)
    picker = jnp.any(chosen, axis=3)
    scaled = jnp.sum(jnp.where(chosen, gate_flat.reshape(1, 1, group_rows, top_count), 0.0), axis=3)
    return (picker, scaled)


def on_device(tokens, grad_out, routes, route_gates, gate_weight, up_weight, down_weight):
    ep_count = lax.axis_size("ep")
    experts = ep_count // 2
    group_rows, top_count = routes.shape
    capacity = min(group_rows, 5 * group_rows * top_count // (4 * experts))
    half_block = tokens.shape[1] // 2
    rows_all = ep_count * capacity
    picker, scaled = slot_tables(routes, route_gates, experts, capacity)
    picker_float = picker.astype(jnp.float32)
    picker = picker.astype(jnp.bfloat16)
    token_halves = tokens.reshape(group_rows, 2, half_block)
    grad_halves = grad_out.astype(jnp.float32).reshape(group_rows, 2, half_block)
    input_slots = jnp.einsum(
        "ecg,ghq->ehcq", picker, token_halves, preferred_element_type=jnp.float32
    ).astype(jnp.bfloat16)
    grad_slots = jnp.einsum(
        "ecg,ghq->ehcq", scaled, grad_halves, precision=lax.Precision.HIGHEST
    ).astype(jnp.bfloat16)
    sent_inputs, sent_grads = (
        lax.all_to_all(
            input_slots.reshape(ep_count, capacity * half_block),
            "ep",
            split_axis=0,
            concat_axis=0,
            tiled=True,
        ),
        lax.all_to_all(
            grad_slots.reshape(ep_count, capacity * half_block),
            "ep",
            split_axis=0,
            concat_axis=0,
            tiled=True,
        ),
    )
    row_inputs = sent_inputs.reshape(rows_all, half_block)
    row_grads = sent_grads.reshape(rows_all, half_block)
    gate_local = gate_weight[0]
    up_local = up_weight[0]
    down_local = down_weight[0]
    full_inputs, full_grads = (
        lax.all_gather(row_inputs, "etp", axis=1, tiled=True),
        lax.all_gather(row_grads, "etp", axis=1, tiled=True),
    )
    pre_gate = jnp.dot(full_inputs, gate_local, preferred_element_type=jnp.float32)
    pre_up = jnp.dot(full_inputs, up_local, preferred_element_type=jnp.float32)
    d_hidden = lax.dot_general(full_grads, down_local, CONTRACT, preferred_element_type=jnp.float32)
    partner = (
        from_partner(pre_gate.astype(jnp.bfloat16), "ep", 0).astype(pre_gate.dtype),
        from_partner(pre_up.astype(jnp.bfloat16), "ep", 0).astype(pre_up.dtype),
        from_partner(d_hidden.astype(jnp.bfloat16), "ep", 0).astype(d_hidden.dtype),
    )
    pre_gate = pre_gate + partner[0]
    pre_up = pre_up + partner[1]
    d_hidden = d_hidden + partner[2]
    sigma = jax.nn.sigmoid(pre_gate)
    d_up = (d_hidden * pre_gate * sigma).astype(jnp.bfloat16)
    d_gate = (d_hidden * pre_up * sigma * (1.0 + pre_gate * (1.0 - sigma))).astype(jnp.bfloat16)
    summed = lax.psum_scatter(
        (
            lax.dot_general(gate_local, d_gate, CONTRACT, preferred_element_type=jnp.float32)
            + lax.dot_general(up_local, d_up, CONTRACT, preferred_element_type=jnp.float32)
        ).astype(jnp.bfloat16),
        "etp",
        scatter_dimension=0,
        tiled=True,
    ).astype(jnp.float32)
    returned = lax.all_to_all(
        summed.astype(jnp.bfloat16), "ep", split_axis=1, concat_axis=1, tiled=True
    ).astype(summed.dtype)
    share = returned.shape[0]
    returned = returned.reshape(share, experts, 2, capacity)
    result = jnp.einsum("qehc,ecg->ghq", returned, picker_float, precision=lax.Precision.HIGHEST)
    return result.reshape(group_rows, 2 * share).astype(jnp.bfloat16)


def solution(mesh):
    return jax.shard_map(
        on_device,
        mesh=mesh,
        in_specs=(
            P("ep", "etp"),
            P("ep", "etp"),
            P("ep", None),
            P("ep", None),
            P("ep", None, "etp"),
            P("ep", None, "etp"),
            P("ep", "etp", None),
        ),
        out_specs=P("ep", "etp"),
        check_vma=False,
    )
```

profile of v0, /device:TPU:1, one launch (start us, length us, event | category | flops | bytes accessed | tf_op | source)
XLA Modules:
  0.0 436.2 jit_solution(6248996012681880160)
XLA Ops:
  6.5 0.8 copy.39
  7.6 0.8 copy.41
  8.3 0.8 reshape.88
  9.2 0.2 reduce_window_sum.11
  9.4 0.2 select_reduce_fusion
  9.7 0.2 fusion.15
  9.9 0.3 fusion.3
  10.4 0.3 all_to_all.24
  10.7 0.5 broadcast.53
  11.2 1.5 reduce.3
  12.8 0.2 reshape.108
  13.0 63.8 %all_to_all.29 = bf16[64,2,560]{2,1,0:T(2,128)(2,1)S(1)} all-to-all(bf16[64,2,560]{2,1,0:T(2,128)(2,1)S(1)} %reshape.108), channel_id=1, replica_groups=mesh['ep'=64,'etp'=16] {'ep'}, dimensions={0} | all-to-all | bytes 286720 | tf_op jit(solution)/shard_map/all_to_all | solution.py:63
  76.8 0.2 reshape.109
  77.0 0.9 reduce
  77.9 0.9 reshape.89
  79.0 0.2 and_reduce_fusion
  79.2 0.2 fusion.2
  79.4 0.1 copy.47
  79.5 0.3 all_to_all.25
  79.9 1.5 reduce.2
  81.4 0.2 reshape.106
  81.6 39.1 %all_to_all.30 = bf16[64,2,560]{2,1,0:T(2,128)(2,1)S(1)} all-to-all(bf16[64,2,560]{2,1,0:T(2,128)(2,1)S(1)} %reshape.106), channel_id=1, replica_groups=mesh['ep'=64,'etp'=16] {'ep'}, dimensions={0} | all-to-all | bytes 286720 | tf_op jit(solution)/shard_map/all_to_all | solution.py:56
  120.7 0.2 reshape.107
  120.9 0.9 reduce.1
  121.8 0.9 reshape.91
  122.7 0.2 reduce-scatter.4.cloned.1.call-start
  123.0 19.9 %all-gather.5.cloned.1.call-done = bf16[16,224,320]{1,2,0:T(8,128)(2,1)} async-done(((bf16[1,224,320]{1,2,0:T(8,128)(2,1)}), bf16[16,224,320]{1,2,0:T(8,128)(2,1)}) %all-gather.5.cloned.1.call-update) | async-done | bytes 2293776 | tf_op jit(solution)/shard_map/all_gather | solution.py:78
  142.8 4.7 %copy.45 = bf16[16,224,320]{1,0,2:T(8,128)(2,1)} copy(bf16[16,224,320]{1,2,0:T(8,128)(2,1)} %all-gather.5.cloned.1.call-done) | data formatting | bytes 4587520 | tf_op jit(solution)/shard_map/all_gather | solution.py:78
  147.6 5.2 %reshape.94 = bf16[3584,320]{0,1:T(8,128)(2,1)S(1)} reshape(bf16[16,224,320]{1,0,2:T(8,128)(2,1)} %copy.45) | data formatting | bytes 4587520
  152.7 1.9 fusion.30
  154.7 3.0 collective-permute-start
  157.6 71.1 %all-gather.7.cloned.1.call-done = bf16[16,224,320]{1,2,0:T(8,128)(2,1)} async-done(((bf16[1,224,320]{1,2,0:T(8,128)(2,1)}), bf16[16,224,320]{1,2,0:T(8,128)(2,1)}) %all-gather.7.cloned.1.call-update) | async-done | bytes 2293776 | tf_op jit(solution)/shard_map/all_gather | solution.py:77
  228.8 4.7 %copy.49 = bf16[16,224,320]{1,0,2:T(8,128)(2,1)} copy(bf16[16,224,320]{1,2,0:T(8,128)(2,1)} %all-gather.7.cloned.1.call-done) | data formatting | bytes 4587520 | tf_op jit(solution)/shard_map/all_gather | solution.py:77
  233.5 5.2 %reshape.96 = bf16[3584,320]{0,1:T(8,128)(2,1)S(1)} reshape(bf16[16,224,320]{1,0,2:T(8,128)(2,1)} %copy.49) | data formatting | bytes 4587520
  238.7 1.9 fusion.29
  240.6 0.8 fusion.31
  241.4 3.0 collective-permute-start.1
  244.4 1.9 collective-permute-start.2
  246.3 1.2 collective-permute-done.2
  247.5 0.8 fusion.6
  248.3 0.4 copy-done.1
  248.7 0.8 fusion.1
  249.5 2.7 copy.58
  252.2 108.8 %reduce-scatter.4.cloned.1.call-done = bf16[224,320]{1,0:T(8,128)(2,1)} async-done(((bf16[3584,320]{1,0:T(8,128)(2,1)}), bf16[224,320]{1,0:T(8,128)(2,1)}) %reduce-scatter.4.cloned.1.call-update) | async-done | bytes 143376
  361.0 1.0 copy.59
  362.1 66.6 %all_to_all.31 = bf16[224,64,5]{0,2,1:T(8,128)(2,1)S(1)} all-to-all(bf16[224,64,5]{0,2,1:T(8,128)(2,1)S(1)} %all_to_all.22), channel_id=1, replica_groups=mesh['ep'=64,'etp'=16] {'ep'}, dimensions={1} | all-to-all | bytes 286720 | tf_op jit(solution)/shard_map/all_to_all | solution.py:103
  428.7 0.2 fusion.5
  428.9 0.7 convert_element_type.77
  (21 shorter events, 0.8 us)
Async XLA Ops:
  6.5 234.1 %copy-start = (bf16[1,3584,128]{2,1,0:T(8,128)(2,1)S(1)}, bf16[1,3584,128]{2,1,0:T(8,128)(2,1)}, u32[]{:S(2)}) copy-start(bf16[1,3584,128]{2,1,0:T(8,128)(2,1)} %param.11) | copy-start | bytes 2752516
  6.5 72.4 %copy-start.2 = (bf16[16,448]{1,0:T(8,128)(2,1)S(1)}, bf16[16,448]{1,0:T(8,128)(2,1)}, u32[]{:S(2)}) copy-start(bf16[16,448]{1,0:T(8,128)(2,1)} %param.7) | copy-start | bytes 43012
  6.5 136.3 %all-gather.5.cloned.1.call-start = ((), (), s32[]{:S(2)}) async-start(), calls=%async_computation.4 | async-start | bytes 2785280 | tf_op jit(solution)/shard_map/all_gather | solution.py:78
  78.8 149.9 %all-gather.7.cloned.1.call-start = ((), (), s32[]{:S(2)}) async-start(), calls=%async_computation.5 | async-start | bytes 2785280 | tf_op jit(solution)/shard_map/all_gather | solution.py:77
  122.7 238.3 %reduce-scatter.4.cloned.1.call-start = ((), (), s32[]{:S(2)}) async-start(), calls=%async_computation.6 | async-start | bytes 2924544
  154.7 91.6 %collective-permute-start = (bf16[320,128]{1,0:T(8,128)(2,1)S(1)}, bf16[320,128]{1,0:T(8,128)(2,1)S(1)}, u32[]{:S(2)}, u32[]{:S(2)}) collective-permute-start(bf16[320,128]{1,0:T(8,128)(2,1)S(1)} %get-tuple-element.7), channel_id=1, source_target_pairs={{0,16},{16,0},{32,48},{48,32},{64,80},{80,64},{96,112},{112,96},{1... | collective-permute-start | bytes 245768 | tf_op jit(solution)/shard_map/ppermute | solution.py:16
  241.4 4.9 %collective-permute-start.1 = (bf16[320,128]{1,0:T(8,128)(2,1)S(1)}, bf16[320,128]{1,0:T(8,128)(2,1)S(1)}, u32[]{:S(2)}, u32[]{:S(2)}) collective-permute-start(bf16[320,128]{1,0:T(8,128)(2,1)S(1)} %get-tuple-element.5), channel_id=1, source_target_pairs={{0,16},{16,0},{32,48},{48,32},{64,80},{80,64},{96,112},{112,96},{1... | collective-permute-start | bytes 245768 | tf_op jit(solution)/shard_map/ppermute | solution.py:16
  244.4 3.2 collective-permute-start.2
  247.5 1.2 copy-start.1
Sparse Core Ops, SparseCore 0:
  79.0 63.8 all-gather.4
  147.0 81.6 all-gather.6
  252.3 108.6 reduce-scatter.3
where the time goes:
time: 437 us; the launch traced here: 436 us
  waiting for transfers between devices  201 us (46%)
  blocking collectives  169 us (39%)
  local copies, waits for them, and re-layouts  31.4 us (7%)
  between operations  13.4 us (3%)
  starting transfers between devices  8.11 us (2%)
  matrix products  6.93 us (2%)
  other arithmetic  5.8 us (1%)
    unnamed x4, waiting for transfers between devices  109 us
    all_gather x1, waiting for transfers between devices, on_device(): lax.all_gather(row_inputs, 'etp', axis=1, tiled=True)  71.1 us
    all_to_all x1, blocking collectives, on_device(): lax.all_to_all(summed.astype(jnp.bfloat16), 'ep', split_axis=1, concat_ax...  66.6 us
    all_to_all x1, blocking collectives, on_device(): lax.all_to_all(grad_slots.reshape(ep_count, capacity * half_block), 'ep',...  63.8 us
    all_to_all x1, blocking collectives, on_device(): lax.all_to_all(input_slots.reshape(ep_count, capacity * half_block), 'ep'...  39.1 us
    all_gather x1, waiting for transfers between devices, on_device(): lax.all_gather(row_grads, 'etp', axis=1, tiled=True)  19.9 us
    unnamed x16, local copies, waits for them, and re-layouts  17 us
  transfers between devices with their start and end apart: 6, of which 4 were waited for; matrix products, arithmetic and copies ran while one was open for 7% of the time, Pallas kernels for 0%

commit v1 on v0

v1 whole, which is shorter than its diff:
```python
import functools

import jax
import jax.numpy as jnp
from jax import lax
from jax.experimental import pallas as pl
from jax.experimental.pallas import tpu as pltpu
from jax.sharding import PartitionSpec as P

SIDE = 4
STEPS = (0, 1, 3, 2)
NT = (((1,), (1,)), ((), ()))
NN = (((1,), (0,)), ((), ()))
VMEM_BYTES = 48 * 1024 * 1024


def mm(a, b, dims):
    return lax.dot_general(a, b, dims, preferred_element_type=jnp.float32)


def pack_kernel(gate_ref, up_ref, down_ref, o0, o1, o2, o3, sems):
    quarter = gate_ref.shape[0] // SIDE
    lanes = gate_ref.shape[1]
    chunks = quarter // lanes
    mine = lax.axis_index("etp") // SIDE
    copies = []

    def go(src, dst):
        copy = pltpu.make_async_copy(src, dst, sems.at[len(copies)])
        copy.start()
        copies.append(copy)

    for step, out in zip(STEPS, (o0, o1, o2, o3)):
        first = lax.rem(mine + step, SIDE) * quarter
        go(gate_ref.at[pl.ds(first, quarter)], out.at[pl.ds(0, quarter)])
        go(up_ref.at[pl.ds(first, quarter)], out.at[pl.ds(quarter, quarter)])
        for j in range(chunks):
            go(
                down_ref.at[:, pl.ds(pl.multiple_of(first + j * lanes, lanes), lanes)],
                out.at[pl.ds(2 * quarter + j * lanes, lanes)],
            )
    for copy in copies:
        copy.wait()


def pack_weights(gate, up, down):
    rows, lanes = gate.shape
    quarter = rows // SIDE
    shape = jax.ShapeDtypeStruct((3 * quarter, lanes), gate.dtype)
    count = SIDE * (2 + quarter // lanes)
    return pl.pallas_call(
        pack_kernel,
        out_shape=[shape] * SIDE,
        in_specs=[pl.BlockSpec(memory_space=pl.ANY)] * 3,
        out_specs=[pl.BlockSpec(memory_space=pl.ANY)] * SIDE,
        scratch_shapes=[pltpu.SemaphoreType.DMA((count,))],
        name="pack_weights",
    )(gate, up, down)


def forward_kernel(x_ref, w0, w1, w2, w3, out_ref):
    share = x_ref.shape[3]
    quarter = SIDE * share
    lanes = w0.shape[1]
    mine = lax.axis_index("etp") // SIDE
    for step, w in zip(STEPS, (w0, w1, w2, w3)):
        place = lax.rem(mine + step, SIDE)
        down = jnp.concatenate(
            [w[pl.ds(2 * quarter + j * lanes, lanes), :] for j in range(quarter // lanes)], axis=1
        )
        both = None
        hidden = None
        for x in range(SIDE):
            pair = jnp.concatenate(
                [w[pl.ds(x * share, share), :], w[pl.ds(quarter + x * share, share), :]], axis=1
            )
            one = mm(x_ref[x, 0], pair, NN)
            two = mm(x_ref[x, 1], down[:, x * share : (x + 1) * share], NT)
            both = one if both is None else both + one
            hidden = two if hidden is None else hidden + two
        out_ref[place, 0] = both[:, :lanes].astype(out_ref.dtype)
        out_ref[place, 1] = both[:, lanes:].astype(out_ref.dtype)
        out_ref[place, 2] = hidden.astype(out_ref.dtype)


def backward_kernel(d_ref, w0, w1, w2, w3, out_ref):
    share = out_ref.shape[2]
    quarter = SIDE * share
    mine = lax.axis_index("etp") // SIDE
    for x in range(SIDE):
        total = None
        for step, w in zip(STEPS, (w0, w1, w2, w3)):
            place = lax.rem(mine + step, SIDE)
            grads = jnp.concatenate([d_ref[place, 0], d_ref[place, 1]], axis=1)
            pair = jnp.concatenate(
                [w[pl.ds(x * share, share), :], w[pl.ds(quarter + x * share, share), :]], axis=1
            )
            one = mm(grads, pair, NT)
            total = one if total is None else total + one
        out_ref[x] = total.astype(out_ref.dtype)


def local_call(kernel, shape, count, flops, name):
    return pl.pallas_call(
        kernel,
        out_shape=jax.ShapeDtypeStruct(shape, jnp.bfloat16),
        in_specs=[pl.BlockSpec(memory_space=pltpu.VMEM)] * count,
        out_specs=pl.BlockSpec(memory_space=pltpu.VMEM),
        compiler_params=pltpu.CompilerParams(vmem_limit_bytes=VMEM_BYTES),
        cost_estimate=pl.CostEstimate(flops=flops, bytes_accessed=5_000_000, transcendentals=0),
        name=name,
    )


def on_device(tokens, grad_out, routes, route_gates, gate_weight, up_weight, down_weight):
    ep_count = lax.axis_size("ep")
    experts = ep_count // 2
    group_rows, top_count = routes.shape
    capacity = min(group_rows, 5 * group_rows * top_count // (4 * experts))
    half = tokens.shape[1] // 2
    rows_all = ep_count * capacity
    lanes = gate_weight.shape[2]
    along_x = [[SIDE * y + x for x in range(SIDE)] for y in range(SIDE)]
    along_y = [[SIDE * y + x for y in range(SIDE)] for x in range(SIDE)]

    packed = pack_weights(gate_weight[0], up_weight[0], down_weight[0])
    routes, route_gates, tokens, grad_out, *packed = lax.optimization_barrier(
        (routes, route_gates, tokens, grad_out, *packed)
    )
    weights = [packed[0]]
    for step, block in zip(STEPS[1:], packed[1:]):
        pairs = [
            (SIDE * y + x, SIDE * ((y + step) % SIDE) + x) for y in range(SIDE) for x in range(SIDE)
        ]
        weights.append(lax.ppermute(block, "etp", pairs))
    weights = [weights[0], weights[2], weights[1], weights[3]]

    expert_ids = jnp.arange(experts, dtype=jnp.int32)
    hit = routes[:, :, None] == expert_ids
    member = jnp.any(hit, axis=1).astype(jnp.int32)
    scale = jnp.sum(jnp.where(hit, route_gates[:, :, None], 0.0), axis=1)
    rank = jnp.cumsum(member, axis=0) - member
    slots = jnp.arange(capacity, dtype=jnp.int32)
    chosen = (member.T[:, None, :] == 1) & (rank.T[:, None, :] == slots[None, :, None])
    picker = chosen.astype(jnp.bfloat16)
    scaled = jnp.sum(jnp.where(chosen, scale.T[:, None, :], 0.0), axis=2)

    input_slots = jnp.einsum(
        "ecg,ghq->ehcq",
        picker,
        tokens.reshape(group_rows, 2, half),
        preferred_element_type=jnp.float32,
    ).astype(jnp.bfloat16)
    grad_slots = jnp.einsum(
        "ecg,ghq->ehcq",
        picker,
        grad_out.reshape(group_rows, 2, half),
        preferred_element_type=jnp.float32,
    )
    grad_slots = (grad_slots * scaled[:, None, :, None]).astype(jnp.bfloat16)
    sent = jnp.stack([input_slots, grad_slots], axis=2).reshape(ep_count, 2 * capacity * half)
    came = lax.all_to_all(sent, "ep", split_axis=0, concat_axis=0, tiled=True)
    rows = (
        came.reshape(ep_count, 2, capacity, half)
        .transpose(1, 0, 2, 3)
        .reshape(2, rows_all, half)
    )

    rows, *weights = lax.optimization_barrier((rows, *weights))
    wide = jnp.broadcast_to(rows[None], (SIDE, *rows.shape))
    gathered = lax.all_to_all(wide, "etp", 0, 0, tiled=True, axis_index_groups=along_x)
    flops = 2 * 3 * rows_all * half * SIDE * lanes * SIDE
    partial = local_call(
        forward_kernel, (SIDE, 3, rows_all, lanes), 5, flops, "forward_parts"
    )(gathered, *weights)
    partial = lax.all_to_all(partial, "etp", 0, 0, tiled=True, axis_index_groups=along_y)
    mine = jnp.sum(partial.astype(jnp.float32), axis=0)
    other = lax.ppermute(
        mine.astype(jnp.bfloat16), "ep", [(i, i ^ 1) for i in range(ep_count)]
    ).astype(jnp.float32)
    pre_gate, pre_up, d_hidden = mine + other
    sigma = jax.nn.sigmoid(pre_gate)
    d_up = (d_hidden * pre_gate * sigma).astype(jnp.bfloat16)
    d_gate = (d_hidden * pre_up * sigma * (1.0 + pre_gate * (1.0 - sigma))).astype(jnp.bfloat16)
    grads = lax.all_gather(jnp.stack([d_gate, d_up]), "etp", axis_index_groups=along_y)
    back = local_call(
        backward_kernel, (SIDE, rows_all, half), 5, flops * 2 // 3, "backward_parts"
    )(grads, *weights)
    back = lax.all_to_all(back, "etp", 0, 0, tiled=True, axis_index_groups=along_x)
    summed = jnp.sum(back.astype(jnp.float32), axis=0).astype(jnp.bfloat16)
    returned = lax.all_to_all(
        summed.reshape(ep_count, capacity * half), "ep", split_axis=0, concat_axis=0, tiled=True
    ).reshape(experts, 2, capacity, half)
    result = jnp.einsum(
        "ehcq,ecg->ghq", returned, picker, preferred_element_type=jnp.float32
    )
    return result.reshape(group_rows, 2 * half).astype(jnp.bfloat16)


def solution(mesh):
    return jax.shard_map(
        on_device,
        mesh=mesh,
        in_specs=(
            P("ep", "etp"),
            P("ep", "etp"),
            P("ep", None),
            P("ep", None),
            P("ep", None, "etp"),
            P("ep", None, "etp"),
            P("ep", "etp", None),
        ),
        out_specs=P("ep", "etp"),
        check_vma=False,
    )
```

time: 437 us -> 290 us (0.66)
  waiting for transfers between devices: 201 us -> 35.9 us
  Pallas kernels: 0 us -> 87.3 us
  blocking collectives: 169 us -> 105 us
  starting transfers between devices: 8.11 us -> 46.2 us
  local copies, waits for them, and re-layouts: 31.4 us -> 5.6 us
  between operations: 13.4 us -> 0.29 us
  matrix products: 6.93 us -> 1.29 us
    unnamed x4 -> x0, waiting for transfers between devices: 109 us -> none
    all_gather x2 -> x0, waiting for transfers between devices: 91 us -> none  [the longest x1 71.1 us: on_device(): lax.all_gather(row_inputs, 'etp', axis=1, tiled=True)]
    pallas_call x0 -> x3, Pallas kernels: none -> 87.3 us  [the longest x1 84.8 us: pack_weights(): pl.pallas_call(pack_kernel, out_shape=[shape] * SIDE, in_specs=[pl.BlockS...]
    all_to_all x3 -> x4, blocking collectives: 169 us -> 94.3 us  [the longest x1 48.5 us: on_device(): lax.all_to_all(summed.reshape(ep_count, capacity * half), 'ep', split_axi...]
    all_to_all x0 -> x1, waiting for transfers between devices: none -> 34.7 us  [on_device(): came = lax.all_to_all(sent, 'ep', split_axis=0, concat_axis=0, tiled=True)]
    all_to_all x0 -> x1, starting transfers between devices: none -> 30.4 us  [on_device(): came = lax.all_to_all(sent, 'ep', split_axis=0, concat_axis=0, tiled=True)]
    unnamed x16 -> x14, local copies, waits for them, and re-layouts: 17 us -> 1.92 us
    all_gather x0 -> x1, blocking collectives: none -> 10.5 us  [on_device(): lax.all_gather(jnp.stack([d_gate, d_up]), 'etp', axis_index_groups=along_y)]
  transfers between devices with their start and end apart: 6 -> 5, of which waited for: 4 -> 2; matrix products, arithmetic and copies ran while one was open for 7% -> 1% of each run, Pallas kernels for 0% -> 0%
where the time goes in v1:
time: 290 us; the launch traced here: 289 us
  blocking collectives  105 us (36%)
  Pallas kernels  87.3 us (30%)
  starting transfers between devices  46.2 us (16%)
  waiting for transfers between devices  35.9 us (12%)
  other arithmetic  7.81 us (3%)
  local copies, waits for them, and re-layouts  5.6 us (2%)
    pallas_call x1, Pallas kernels, pack_weights(): pl.pallas_call(pack_kernel, out_shape=[shape] * SIDE, in_specs=[pl.BlockS...  84.8 us
    all_to_all x1, blocking collectives, on_device(): lax.all_to_all(summed.reshape(ep_count, capacity * half), 'ep', split_axi...  48.5 us
    all_to_all x1, waiting for transfers between devices, on_device(): came = lax.all_to_all(sent, 'ep', split_axis=0, concat_axis=0, tiled=True)  34.7 us
    all_to_all x1, starting transfers between devices, on_device(): came = lax.all_to_all(sent, 'ep', split_axis=0, concat_axis=0, tiled=True)  30.4 us
    all_to_all x1, blocking collectives, on_device(): lax.all_to_all(wide, 'etp', 0, 0, tiled=True, axis_index_groups=along_x)  20.2 us
    all_to_all x1, blocking collectives, on_device(): lax.all_to_all(partial, 'etp', 0, 0, tiled=True, axis_index_groups=along_y)  15.5 us
    all_gather x1, blocking collectives, on_device(): lax.all_gather(jnp.stack([d_gate, d_up]), 'etp', axis_index_groups=along_y)  10.5 us
    ppermute x3, starting transfers between devices, on_device(): weights.append(lax.ppermute(block, 'etp', pairs))  10.1 us
  transfers between devices with their start and end apart: 5, of which 2 were waited for; matrix products, arithmetic and copies ran while one was open for 1% of the time, Pallas kernels for 0%

profile of v1, /device:TPU:1, one launch (start us, length us, event | category | flops | bytes accessed | tf_op | source)
XLA Modules:
  0.0 289.1 jit_solution(16246845851226374079)
XLA Ops:
  0.0 84.8 %pack_weights.1 = (bf16[2688,128]{1,0:T(8,128)(2,1)}, bf16[2688,128]{1,0:T(8,128)(2,1)}, bf16[2688,128]{1,0:T(8,128)(2,1)}, bf16[2688,128]{1,0:T(8,128)(2,1)}) custom-call(bf16[3584,128]{1,0:T(8,128)(2,1)} %bitcast.37, bf16[3584,128]{1,0:T(8,128)(2,1)} %bitcast.38, bf16[128,3584]{1,0:T(8,128)(2,1)} %bitcast.39), custom_call_target="tpu_custom_call" | custom-call | tf_op jit(solution)/shard_map/pack_weights/pallas_call | solution.py:51
  84.9 0.1 copy.39
  84.9 0.1 fusion.7
  85.0 0.1 copy.42
  85.1 0.1 select_reduce_fusion
  85.3 0.1 reshape.35
  85.4 0.1 reshape.36
  85.5 0.2 fusion.1
  85.8 0.2 fusion.2
  86.0 0.1 pad_maximum_fusion
  86.1 0.2 copy.43
  86.3 0.8 all_to_all.28
  87.0 0.5 broadcast.25
  87.5 2.6 reduce.3
  90.1 1.0 reshape.47
  91.1 30.4 %all-to-all-start = ((bf16[64,2,1120]{2,1,0:T(2,128)(2,1)}), bf16[64,2,1120]{2,1,0:T(2,128)(2,1)S(1)}, u32[]{:S(2)}, u32[]{:S(2)}) async-start(bf16[64,2,1120]{2,1,0:T(2,128)(2,1)} %reshape.47), calls=%async_computation | async-start | bytes 589824 | tf_op jit(solution)/shard_map/all_to_all | solution.py:162
  121.5 4.6 %collective-permute-start = (bf16[2688,128]{1,0:T(8,128)(2,1)}, bf16[2688,128]{1,0:T(8,128)(2,1)S(1)}, u32[]{:S(2)}, u32[]{:S(2)}) collective-permute-start(bf16[2688,128]{1,0:T(8,128)(2,1)} %get-tuple-element.31), channel_id=1, source_target_pairs={{0,12},{1,13},{2,14},{3,15},{4,0},{5,1},{6,2},{7,3},{8,4},{9,5},{1... | collective-permute-start | bytes 2064392 | tf_op jit(solution)/shard_map/ppermute | solution.py:135
  126.2 1.9 collective-permute-start.1
  128.1 3.5 %collective-permute-start.2 = (bf16[2688,128]{1,0:T(8,128)(2,1)}, bf16[2688,128]{1,0:T(8,128)(2,1)S(1)}, u32[]{:S(2)}, u32[]{:S(2)}) collective-permute-start(bf16[2688,128]{1,0:T(8,128)(2,1)} %get-tuple-element.33), channel_id=1, source_target_pairs={{0,8},{1,9},{2,10},{3,11},{4,12},{5,13},{6,14},{7,15},{8,0},{9,1},... | collective-permute-start | bytes 2064392 | tf_op jit(solution)/shard_map/ppermute | solution.py:135
  131.7 34.7 %all-to-all-done = bf16[64,2,1120]{2,1,0:T(2,128)(2,1)S(1)} async-done(((bf16[64,2,1120]{2,1,0:T(2,128)(2,1)}), bf16[64,2,1120]{2,1,0:T(2,128)(2,1)S(1)}, u32[]{:S(2)}, u32[]{:S(2)}) %all-to-all-start) | async-done | bytes 286752 | tf_op jit(solution)/shard_map/all_to_all | solution.py:162
  166.4 0.4 reshape.48
  166.9 1.9 reduce.1
  168.8 0.7 reshape.37
  169.5 0.3 copy.45
  169.7 0.0 collective-permute-done.w1
  169.8 0.0 collective-permute-done.1.w2
  169.8 0.1 broadcast_in_dim.42
  169.9 20.2 %all_to_all.35.x_ref = bf16[4,2,320,224]{3,2,1,0:T(8,128)(2,1)S(1)} all-to-all(bf16[4,2,320,224]{3,2,1,0:T(8,128)(2,1)S(1)} %broadcast_in_dim.42), channel_id=1, replica_groups={{0,1,2,3},{4,5,6,7},{8,9,10,11},{12,13,14,15},{16,17,18,19},{20,21,22,2..., dimensions={0} | all-to-all | bytes 2293760 | tf_op jit(solution)/shard_map/all_to_all | solution.py:171
  190.1 1.6 forward_parts.1
  191.7 15.5 %all_to_all.36 = bf16[4,3,320,128]{3,2,1,0:T(8,128)(2,1)S(1)} all-to-all(bf16[4,3,320,128]{3,2,1,0:T(8,128)(2,1)S(1)} %forward_parts.1), channel_id=1, replica_groups={{0,4,8,12},{1,5,9,13},{2,6,10,14},{3,7,11,15},{16,20,24,28},{17,21,25,2..., dimensions={0} | all-to-all | bytes 1966080 | tf_op jit(solution)/shard_map/all_to_all | solution.py:176
  207.2 0.2 convert_reduce_fusion
  207.4 5.7 %collective-permute-start.3 = (bf16[3,320,128]{2,1,0:T(8,128)(2,1)S(1)}, bf16[3,320,128]{2,1,0:T(8,128)(2,1)S(1)}, u32[]{:S(2)}, u32[]{:S(2)}) collective-permute-start(bf16[3,320,128]{2,1,0:T(8,128)(2,1)S(1)} %convert_element_type.47), channel_id=1, source_target_pairs={{0,16},{16,0},{32,48},{48,32},{64,80},{80,64},{96,112},{112,96},{1... | collective-permute-start | bytes 737288 | tf_op jit(solution)/shard_map/ppermute | solution.py:178
  213.2 1.1 collective-permute-done.3
  214.3 0.1 fusion.6
  214.4 10.5 %all-gather = bf16[8,320,128]{2,1,0:T(8,128)(2,1)S(1)} all-gather(bf16[2,320,128]{2,1,0:T(8,128)(2,1)S(1)} %pad_maximum_fusion.1), channel_id=2, replica_groups={{0,4,8,12},{1,5,9,13},{2,6,10,14},{3,7,11,15},{16,20,24,28},{17,21,25,2..., dimensions={0}, use_global_device_ids=true | all-gather | bytes 819200 | tf_op jit(solution)/shard_map/all_gather | solution.py:185
  225.0 0.9 backward_parts.1
  225.8 10.0 %all_to_all.37 = bf16[4,320,224]{2,1,0:T(8,128)(2,1)S(1)} all-to-all(bf16[4,320,224]{2,1,0:T(8,128)(2,1)S(1)} %backward_parts.1), channel_id=1, replica_groups={{0,1,2,3},{4,5,6,7},{8,9,10,11},{12,13,14,15},{16,17,18,19},{20,21,22,2..., dimensions={0} | all-to-all | bytes 1146880 | tf_op jit(solution)/shard_map/all_to_all | solution.py:189
  235.9 0.1 reduce_sum.42
  236.0 0.3 all_to_all.29
  236.3 1.6 reduce.4
  237.9 0.2 reshape.49
  238.1 48.5 %all_to_all.38 = bf16[64,2,560]{2,1,0:T(2,128)(2,1)S(1)} all-to-all(bf16[64,2,560]{2,1,0:T(2,128)(2,1)S(1)} %reshape.49), channel_id=1, replica_groups=mesh['ep'=64,'etp'=16] {'ep'}, dimensions={0} | all-to-all | bytes 286720 | tf_op jit(solution)/shard_map/all_to_all | solution.py:191
  286.6 0.2 reshape.50
  286.9 0.9 reduce.2
  287.8 0.2 reshape.39
  288.1 0.1 copy.48
  288.2 0.1 dot_general.16
  288.3 0.8 fusion.3
  (19 shorter events, 0.2 us)
Async XLA Ops:
  0.0 84.8 %copy-start.3 = (s32[16,8]{0,1:T(8,128)S(1)}, s32[16,8]{0,1:T(8,128)}, u32[]{:S(2)}) copy-start(s32[16,8]{0,1:T(8,128)} %param.9) | copy-start | bytes 1540
  0.0 85.0 %copy-start.4 = (f32[16,8]{0,1:T(8,128)S(1)}, f32[16,8]{0,1:T(8,128)}, u32[]{:S(2)}) copy-start(f32[16,8]{0,1:T(8,128)} %param.10) | copy-start | bytes 1540
  0.0 85.3 %copy-start.1 = (bf16[16,448]{1,0:T(8,128)(2,1)S(1)}, bf16[16,448]{1,0:T(8,128)(2,1)}, u32[]{:S(2)}) copy-start(bf16[16,448]{1,0:T(8,128)(2,1)} %param.7) | copy-start | bytes 43012
  0.0 85.4 %copy-start.2 = (bf16[16,448]{1,0:T(8,128)(2,1)S(1)}, bf16[16,448]{1,0:T(8,128)(2,1)}, u32[]{:S(2)}) copy-start(bf16[16,448]{1,0:T(8,128)(2,1)} %param.8) | copy-start | bytes 43012
  91.1 75.3 %all-to-all-start = ((bf16[64,2,1120]{2,1,0:T(2,128)(2,1)}), bf16[64,2,1120]{2,1,0:T(2,128)(2,1)S(1)}, u32[]{:S(2)}, u32[]{:S(2)}) async-start(bf16[64,2,1120]{2,1,0:T(2,128)(2,1)} %reshape.47), calls=%async_computation | async-start | bytes 589824 | tf_op jit(solution)/shard_map/all_to_all | solution.py:162
  121.5 48.2 %collective-permute-start = (bf16[2688,128]{1,0:T(8,128)(2,1)}, bf16[2688,128]{1,0:T(8,128)(2,1)S(1)}, u32[]{:S(2)}, u32[]{:S(2)}) collective-permute-start(bf16[2688,128]{1,0:T(8,128)(2,1)} %get-tuple-element.31), channel_id=1, source_target_pairs={{0,12},{1,13},{2,14},{3,15},{4,0},{5,1},{6,2},{7,3},{8,4},{9,5},{1... | collective-permute-start | bytes 2064392 | tf_op jit(solution)/shard_map/ppermute | solution.py:135
  126.2 43.6 %collective-permute-start.1 = (bf16[2688,128]{1,0:T(8,128)(2,1)}, bf16[2688,128]{1,0:T(8,128)(2,1)S(1)}, u32[]{:S(2)}, u32[]{:S(2)}) collective-permute-start(bf16[2688,128]{1,0:T(8,128)(2,1)} %get-tuple-element.32), channel_id=1, source_target_pairs={{0,4},{1,5},{2,6},{3,7},{4,8},{5,9},{6,10},{7,11},{8,12},{9,13},{1... | collective-permute-start | bytes 2064392 | tf_op jit(solution)/shard_map/ppermute | solution.py:135
  128.1 41.7 %collective-permute-start.2 = (bf16[2688,128]{1,0:T(8,128)(2,1)}, bf16[2688,128]{1,0:T(8,128)(2,1)S(1)}, u32[]{:S(2)}, u32[]{:S(2)}) collective-permute-start(bf16[2688,128]{1,0:T(8,128)(2,1)} %get-tuple-element.33), channel_id=1, source_target_pairs={{0,8},{1,9},{2,10},{3,11},{4,12},{5,13},{6,14},{7,15},{8,0},{9,1},... | collective-permute-start | bytes 2064392 | tf_op jit(solution)/shard_map/ppermute | solution.py:135
  169.9 20.2 %copy-start = (bf16[2688,128]{1,0:T(8,128)(2,1)S(1)}, bf16[2688,128]{1,0:T(8,128)(2,1)}, u32[]{:S(2)}) copy-start(bf16[2688,128]{1,0:T(8,128)(2,1)} %get-tuple-element.35.w0) | copy-start | bytes 2064388
  207.4 6.8 %collective-permute-start.3 = (bf16[3,320,128]{2,1,0:T(8,128)(2,1)S(1)}, bf16[3,320,128]{2,1,0:T(8,128)(2,1)S(1)}, u32[]{:S(2)}, u32[]{:S(2)}) collective-permute-start(bf16[3,320,128]{2,1,0:T(8,128)(2,1)S(1)} %convert_element_type.47), channel_id=1, source_target_pairs={{0,16},{16,0},{32,48},{48,32},{64,80},{80,64},{96,112},{112,96},{1... | collective-permute-start | bytes 737288 | tf_op jit(solution)/shard_map/ppermute | solution.py:178

commit v2 on v1

v2 whole, which is shorter than its diff:
```python
import jax
import jax.numpy as jnp
from jax import lax
from jax.experimental import pallas as pl
from jax.experimental.pallas import tpu as pltpu
from jax.sharding import PartitionSpec as P

SIDE = 4
STEPS = (0, 1, 3, 2)
NT = (((1,), (1,)), ((), ()))
NN = (((1,), (0,)), ((), ()))
TN = (((0,), (0,)), ((), ()))
LANES = 128
VMEM_BYTES = 48 * 1024 * 1024


def mm(a, b, dims, precision=None):
    return lax.dot_general(a, b, dims, precision=precision, preferred_element_type=jnp.float32)


def in_vmem(kernel, shapes, count, flops, name):
    return pl.pallas_call(
        kernel,
        out_shape=[jax.ShapeDtypeStruct(*shape) for shape in shapes],
        in_specs=[pl.BlockSpec(memory_space=pltpu.VMEM)] * count,
        out_specs=[pl.BlockSpec(memory_space=pltpu.VMEM)] * len(shapes),
        compiler_params=pltpu.CompilerParams(vmem_limit_bytes=VMEM_BYTES),
        cost_estimate=pl.CostEstimate(flops=flops, bytes_accessed=2_000_000, transcendentals=0),
        name=name,
    )


def pack_kernel(gate_ref, up_ref, down_ref, *outs):
    quarter = gate_ref.shape[0] // SIDE
    lanes = gate_ref.shape[1]
    mine = lax.axis_index("etp") // SIDE
    for step, out in zip(STEPS, outs):
        first = pl.multiple_of(lax.rem(mine + step, SIDE) * quarter, lanes)
        out[pl.ds(0, quarter), :] = gate_ref[pl.ds(first, quarter), :]
        out[pl.ds(quarter, quarter), :] = up_ref[pl.ds(first, quarter), :]
        for j in range(quarter // lanes):
            at = pl.multiple_of(first + j * lanes, lanes)
            out[pl.ds(2 * quarter + j * lanes, lanes), :] = down_ref[:, pl.ds(at, lanes)]


def dispatch_kernel(routes_ref, gates_ref, tokens_ref, grads_ref, inputs_out, grads_out, picks_out):
    group, top = routes_ref.shape
    capacity = picks_out.shape[0]
    width = picks_out.shape[2]
    sides = inputs_out.shape[0]
    half = tokens_ref.shape[1] // 2
    expert = lax.broadcasted_iota(jnp.int32, (group, width), 1) // 2
    member = jnp.zeros((group, width), jnp.float32)
    weight = jnp.zeros((group, width), jnp.float32)
    for k in range(top):
        named = expert == routes_ref[:, k : k + 1]
        member = jnp.where(named, 1.0, member)
        weight = jnp.where(named, gates_ref[:, k : k + 1], weight)
    earlier = lax.broadcasted_iota(jnp.int32, (group, group), 0) > lax.broadcasted_iota(
        jnp.int32, (group, group), 1
    )
    rank = mm(earlier.astype(jnp.float32), member, NN)
    even = lax.broadcasted_iota(jnp.int32, (width, half), 0) % 2 == 0
    tokens = tokens_ref[...].astype(jnp.float32)
    grads = grads_ref[...].astype(jnp.float32)
    input_parts, grad_parts = [], []
    for s in range(capacity):
        pick = jnp.where((rank > s - 0.5) & (rank < s + 0.5), member, 0.0)
        picks_out[s] = pick.astype(picks_out.dtype)
        one = mm(pick, tokens, TN)
        two = mm(pick * weight, grads, TN, lax.Precision.HIGHEST)
        input_parts.append(jnp.where(even, one[:, :half], one[:, half:]))
        grad_parts.append(jnp.where(even, two[:, :half], two[:, half:]))
    fill = jnp.zeros((width, inputs_out.shape[1] - capacity * half), jnp.float32)
    one = jnp.concatenate([*input_parts, fill], axis=1)[:sides]
    two = jnp.concatenate([*grad_parts, fill], axis=1)[:sides]
    inputs_out[...] = one.astype(inputs_out.dtype)
    grads_out[...] = two.astype(grads_out.dtype)


def spread_kernel(inputs_ref, grads_ref, out_ref):
    groups = inputs_ref.shape[0]
    half = out_ref.shape[3]
    for which, ref in enumerate((inputs_ref, grads_ref)):
        for s in range(out_ref.shape[2] // groups):
            block = ref[:, s * half : (s + 1) * half]
            for x in range(SIDE):
                out_ref[x, which, pl.ds(s * groups, groups), :] = block


def forward_kernel(x_ref, w0, w1, w2, w3, keep_ref, send_ref):
    share = x_ref.shape[3]
    quarter = SIDE * share
    lanes = w0.shape[1]
    rows = keep_ref.shape[2]
    mine = lax.axis_index("etp") // SIDE
    core = lax.rem(lax.axis_index("ep"), 2)
    for step, w in zip(STEPS, (w0, w1, w2, w3)):
        place = lax.rem(mine + step, SIDE)
        down = jnp.concatenate(
            [w[pl.ds(2 * quarter + j * lanes, lanes), :] for j in range(quarter // lanes)], axis=1
        )
        for out_ref, side in ((keep_ref, core), (send_ref, 1 - core)):
            here = pl.ds(pl.multiple_of(side * rows, 32), rows)
            both = None
            hidden = None
            for x in range(SIDE):
                pair = jnp.concatenate(
                    [w[pl.ds(x * share, share), :], w[pl.ds(quarter + x * share, share), :]],
                    axis=1,
                )
                one = mm(x_ref[x, 0, here, :], pair, NN)
                two = mm(x_ref[x, 1, here, :], down[:, x * share : (x + 1) * share], NT)
                both = one if both is None else both + one
                hidden = two if hidden is None else hidden + two
            out_ref[place, 0] = both[:, :lanes].astype(out_ref.dtype)
            out_ref[place, 1] = both[:, lanes:].astype(out_ref.dtype)
            out_ref[place, 2] = hidden.astype(out_ref.dtype)


def backward_kernel(d_ref, w0, w1, w2, w3, out_ref):
    share = out_ref.shape[2]
    rows = d_ref.shape[3]
    quarter = SIDE * share
    mine = lax.axis_index("etp") // SIDE
    for x in range(SIDE):
        for side in range(2):
            total = None
            for step, w in zip(STEPS, (w0, w1, w2, w3)):
                place = lax.rem(mine + step, SIDE)
                grads = jnp.concatenate([d_ref[side, place, 0], d_ref[side, place, 1]], axis=1)
                pair = jnp.concatenate(
                    [w[pl.ds(x * share, share), :], w[pl.ds(quarter + x * share, share), :]],
                    axis=1,
                )
                one = mm(grads, pair, NT)
                total = one if total is None else total + one
            out_ref[x, pl.ds(side * rows, rows), :] = total.astype(out_ref.dtype)


def gather_kernel(parts_ref, out_ref):
    groups = out_ref.shape[0]
    half = parts_ref.shape[2]
    capacity = parts_ref.shape[1] // groups
    blocks = []
    for s in range(capacity):
        here = pl.ds(s * groups, groups)
        total = parts_ref[0, here, :].astype(jnp.float32)
        for x in range(1, SIDE):
            total = total + parts_ref[x, here, :].astype(jnp.float32)
        blocks.append(total)
    blocks.append(jnp.zeros((groups, out_ref.shape[1] - capacity * half), jnp.float32))
    out_ref[...] = jnp.concatenate(blocks, axis=1).astype(out_ref.dtype)


def combine_kernel(came_ref, picks_ref, out_ref):
    sides = came_ref.shape[0]
    group = picks_ref.shape[1]
    half = out_ref.shape[1] // 2
    odd = lax.broadcasted_iota(jnp.int32, (group, sides), 1) % 2
    totals = [None, None]
    for s in range(picks_ref.shape[0]):
        block = came_ref[:, s * half : (s + 1) * half]
        pick = picks_ref[s].astype(jnp.float32)[:, :sides]
        for side in range(2):
            one = mm(jnp.where(odd == side, pick, 0.0).astype(block.dtype), block, NN)
            totals[side] = one if totals[side] is None else totals[side] + one
    out_ref[...] = jnp.concatenate(totals, axis=1).astype(out_ref.dtype)


def on_device(tokens, grad_out, routes, route_gates, gate_weight, up_weight, down_weight):
    bf16 = jnp.bfloat16
    ep_count = lax.axis_size("ep")
    experts = ep_count // 2
    group_rows, top_count = routes.shape
    capacity = min(group_rows, 5 * group_rows * top_count // (4 * experts))
    half = tokens.shape[1] // 2
    rows_all = ep_count * capacity
    lanes = gate_weight.shape[2]
    quarter = gate_weight.shape[1] // SIDE
    line = -(-capacity * half // LANES) * LANES
    back_line = -(-capacity * half // (2 * LANES)) * 2 * LANES
    along_x = [[SIDE * y + x for x in range(SIDE)] for y in range(SIDE)]
    along_y = [[SIDE * y + x for y in range(SIDE)] for x in range(SIDE)]
    cores = [[2 * z, 2 * z + 1] for z in range(experts)]

    packed = in_vmem(pack_kernel, [((3 * quarter, lanes), bf16)] * SIDE, 3, 0, "pack_weights")(
        gate_weight[0], up_weight[0], down_weight[0]
    )
    routes, route_gates, tokens, grad_out, *packed = lax.optimization_barrier(
        (routes, route_gates, tokens, grad_out, *packed)
    )
    weights = [packed[0]]
    for step, block in zip(STEPS[1:], packed[1:]):
        pairs = [
            (SIDE * y + x, SIDE * ((y + step) % SIDE) + x) for y in range(SIDE) for x in range(SIDE)
        ]
        weights.append(lax.ppermute(block, "etp", pairs))
    weights = [weights[0], weights[2], weights[1], weights[3]]

    sent_inputs, sent_grads, picks = in_vmem(
        dispatch_kernel,
        [
            ((ep_count, line), bf16),
            ((ep_count, line), bf16),
            ((capacity, group_rows, LANES), bf16),
        ],
        4,
        0,
        "dispatch_rows",
    )(routes, route_gates, tokens, grad_out)
    came = lax.all_to_all(
        jnp.stack([sent_inputs, sent_grads], axis=1), "ep", split_axis=0, concat_axis=0, tiled=True
    )
    came, *weights = lax.optimization_barrier((came, *weights))
    (wide,) = in_vmem(
        spread_kernel, [((SIDE, 2, rows_all, half), bf16)], 2, 0, "spread_rows"
    )(came[:, 0], came[:, 1])
    gathered = lax.all_to_all(wide, "etp", 0, 0, tiled=True, axis_index_groups=along_x)

    flops = 2 * 3 * rows_all * quarter * lanes * SIDE
    part = (SIDE, 3, rows_all // 2, lanes)
    keep, send = in_vmem(
        forward_kernel, [(part, jnp.float32), (part, bf16)], 5, flops, "forward_parts"
    )(gathered, *weights)
    other = lax.ppermute(send, "ep", [(i, i ^ 1) for i in range(ep_count)])
    partial = (keep + other.astype(jnp.float32)).astype(bf16)
    partial = lax.all_to_all(partial, "etp", 0, 0, tiled=True, axis_index_groups=along_y)
    pre_gate, pre_up, d_hidden = jnp.sum(partial.astype(jnp.float32), axis=0)
    sigma = jax.nn.sigmoid(pre_gate)
    d_up = (d_hidden * pre_gate * sigma).astype(bf16)
    d_gate = (d_hidden * pre_up * sigma * (1.0 + pre_gate * (1.0 - sigma))).astype(bf16)
    grads = lax.all_gather(jnp.stack([d_gate, d_up]), "etp", axis_index_groups=along_y)
    grads = lax.all_gather(grads, "ep", axis_index_groups=cores)
    (back,) = in_vmem(
        backward_kernel, [((SIDE, rows_all, half), bf16)], 5, flops * 2 // 3, "backward_parts"
    )(grads, *weights)
    back = lax.all_to_all(back, "etp", 0, 0, tiled=True, axis_index_groups=along_x)
    (summed,) = in_vmem(gather_kernel, [((ep_count, back_line), bf16)], 1, 0, "gather_rows")(back)
    returned = lax.all_to_all(summed, "ep", split_axis=0, concat_axis=0, tiled=True)
    (result,) = in_vmem(
        combine_kernel, [((group_rows, 2 * half), bf16)], 2, 0, "combine_rows"
    )(returned, picks)
    return result


def solution(mesh):
    return jax.shard_map(
        on_device,
        mesh=mesh,
        in_specs=(
            P("ep", "etp"),
            P("ep", "etp"),
            P("ep", None),
            P("ep", None),
            P("ep", None, "etp"),
            P("ep", None, "etp"),
            P("ep", "etp", None),
        ),
        out_specs=P("ep", "etp"),
        check_vma=False,
    )
```

time: 290 us -> 207 us (0.71)
  Pallas kernels: 87.3 us -> 7.23 us
  other arithmetic: 7.81 us -> 0.95 us
  blocking collectives: 105 us -> 110 us
    pallas_call x3 -> x7, Pallas kernels: 87.3 us -> 7.23 us  [the longest x1 1.71 us: on_device(): in_vmem(dispatch_kernel, [((ep_count, line), bf16), ((ep_count, line), bf...]
    all_to_all x1, waiting for transfers between devices: 34.7 us -> 6.82 us  [on_device(): lax.all_to_all(jnp.stack([sent_inputs, sent_grads], axis=1), 'ep', split_...]
    ppermute x3, waiting for transfers between devices: 0.01 us -> 27.9 us  [on_device(): weights.append(lax.ppermute(block, 'etp', pairs))]
    all_to_all x4 -> x1, other arithmetic: 6.98 us -> 0.69 us  [on_device(): lax.all_to_all(summed, 'ep', split_axis=0, concat_axis=0, tiled=True)]
    all_gather x0 -> x1, blocking collectives: none -> 6.18 us  [on_device(): grads = lax.all_gather(grads, 'ep', axis_index_groups=cores)]
    all_to_all x1, blocking collectives: 15.5 us -> 12.3 us  [on_device(): lax.all_to_all(partial, 'etp', 0, 0, tiled=True, axis_index_groups=along_y)]
    all_to_all x1, blocking collectives: 10 us -> 13 us  [on_device(): lax.all_to_all(back, 'etp', 0, 0, tiled=True, axis_index_groups=along_x)]
  transfers between devices with their start and end apart: 5 -> 5, of which waited for: 2 -> 4; matrix products, arithmetic and copies ran while one was open for 1% -> 0% of each run, Pallas kernels for 0% -> 0%
where the time goes in v2:
time: 207 us; the launch traced here: 206 us
  blocking collectives  110 us (53%)
  starting transfers between devices  45.2 us (22%)
  waiting for transfers between devices  36.2 us (17%)
  Pallas kernels  7.23 us (3%)
  local copies, waits for them, and re-layouts  6.43 us (3%)
    all_to_all x1, blocking collectives, on_device(): lax.all_to_all(summed, 'ep', split_axis=0, concat_axis=0, tiled=True)  48.5 us
    all_to_all x1, starting transfers between devices, on_device(): lax.all_to_all(jnp.stack([sent_inputs, sent_grads], axis=1), 'ep', split_...  30.6 us
    ppermute x3, waiting for transfers between devices, on_device(): weights.append(lax.ppermute(block, 'etp', pairs))  27.9 us
    all_to_all x1, blocking collectives, on_device(): lax.all_to_all(wide, 'etp', 0, 0, tiled=True, axis_index_groups=along_x)  20.1 us
    all_to_all x1, blocking collectives, on_device(): lax.all_to_all(back, 'etp', 0, 0, tiled=True, axis_index_groups=along_x)  13 us
    all_to_all x1, blocking collectives, on_device(): lax.all_to_all(partial, 'etp', 0, 0, tiled=True, axis_index_groups=along_y)  12.3 us
    ppermute x3, starting transfers between devices, on_device(): weights.append(lax.ppermute(block, 'etp', pairs))  10.1 us
    all_gather x1, blocking collectives, on_device(): lax.all_gather(jnp.stack([d_gate, d_up]), 'etp', axis_index_groups=along_y)  10 us
  transfers between devices with their start and end apart: 5, of which 4 were waited for; matrix products, arithmetic and copies ran while one was open for 0% of the time, Pallas kernels for 0%

profile of v2, /device:TPU:1, one launch (start us, length us, event | category | flops | bytes accessed | tf_op | source)
XLA Modules:
  0.0 206.2 jit_solution(8513237114829092926)
XLA Ops:
  0.0 0.0 copy-start
  0.0 1.2 copy-done
  1.2 0.0 copy-start.1
  1.2 1.2 copy-done.1
  2.4 0.0 copy-start.2
  2.4 1.2 copy-done.2
  3.5 0.0 copy-start.5
  3.5 0.0 copy-start.6
  3.5 0.0 copy-start.3
  3.5 0.0 copy-start.4
  3.5 1.4 pack_weights.1
  4.9 0.0 copy-done.5
  4.9 0.1 copy.16.routes_ref
  5.0 0.0 copy-done.6
  5.0 0.1 copy.17.gates_ref
  5.1 0.0 copy-done.3
  5.1 0.0 copy-done.4
  5.1 1.7 dispatch_rows.1
  6.9 1.0 copy.18
  7.9 30.6 %all-to-all-start = ((bf16[64,2,1152]{2,1,0:T(2,128)(2,1)}), bf16[64,2,1152]{2,1,0:T(2,128)(2,1)}, u32[]{:S(2)}, u32[]{:S(2)}) async-start(bf16[64,2,1152]{2,1,0:T(2,128)(2,1)} %copy.18), calls=%async_computation | async-start | bytes 589824 | tf_op jit(solution)/shard_map/all_to_all | solution.py:212
  38.4 4.6 %collective-permute-start = (bf16[2688,128]{1,0:T(8,128)(2,1)}, bf16[2688,128]{1,0:T(8,128)(2,1)S(1)}, u32[]{:S(2)}, u32[]{:S(2)}) collective-permute-start(bf16[2688,128]{1,0:T(8,128)(2,1)} %get-tuple-element.38), channel_id=1, source_target_pairs={{0,12},{1,13},{2,14},{3,15},{4,0},{5,1},{6,2},{7,3},{8,4},{9,5},{1... | collective-permute-start | bytes 2064392 | tf_op jit(solution)/shard_map/ppermute | solution.py:198
  43.1 1.9 collective-permute-start.1
  45.0 3.5 %collective-permute-start.2 = (bf16[2688,128]{1,0:T(8,128)(2,1)S(1)}, bf16[2688,128]{1,0:T(8,128)(2,1)S(1)}, u32[]{:S(2)}, u32[]{:S(2)}) collective-permute-start(bf16[2688,128]{1,0:T(8,128)(2,1)S(1)} %get-tuple-element.40), channel_id=1, source_target_pairs={{0,8},{1,9},{2,10},{3,11},{4,12},{5,13},{6,14},{7,15},{8,0},{9,1},... | collective-permute-start | bytes 2064392 | tf_op jit(solution)/shard_map/ppermute | solution.py:198
  48.6 23.7 %collective-permute-done.w1 = bf16[2688,128]{1,0:T(8,128)(2,1)S(1)} collective-permute-done((bf16[2688,128]{1,0:T(8,128)(2,1)}, bf16[2688,128]{1,0:T(8,128)(2,1)S(1)}, u32[]{:S(2)}, u32[]{:S(2)}) %collective-permute-start) | collective-permute-done | bytes 688160 | tf_op jit(solution)/shard_map/ppermute | solution.py:198
  72.3 0.0 collective-permute-done.1.w2
  72.3 4.2 %collective-permute-done.2.w3 = bf16[2688,128]{1,0:T(8,128)(2,1)S(1)} collective-permute-done((bf16[2688,128]{1,0:T(8,128)(2,1)S(1)}, bf16[2688,128]{1,0:T(8,128)(2,1)S(1)}, u32[]{:S(2)}, u32[]{:S(2)}) %collective-permute-start.2) | collective-permute-done | bytes 688160 | tf_op jit(solution)/shard_map/ppermute | solution.py:198
  76.4 6.8 %all-to-all-done = bf16[64,2,1152]{2,1,0:T(2,128)(2,1)} async-done(((bf16[64,2,1152]{2,1,0:T(2,128)(2,1)}), bf16[64,2,1152]{2,1,0:T(2,128)(2,1)}, u32[]{:S(2)}, u32[]{:S(2)}) %all-to-all-start) | async-done | bytes 294944 | tf_op jit(solution)/shard_map/all_to_all | solution.py:212
  83.3 1.0 copy.19
  84.3 0.2 spread_rows.1
  84.5 20.1 %all_to_all.31.x_ref = bf16[4,2,320,224]{3,2,1,0:T(8,128)(2,1)S(1)} all-to-all(bf16[4,2,320,224]{3,2,1,0:T(8,128)(2,1)S(1)} %spread_rows.1), channel_id=1, replica_groups={{0,1,2,3},{4,5,6,7},{8,9,10,11},{12,13,14,15},{16,17,18,19},{20,21,22,2..., dimensions={0} | all-to-all | bytes 2293760 | tf_op jit(solution)/shard_map/all_to_all | solution.py:219
  104.5 1.6 forward_parts.1
  106.1 4.5 %collective-permute-start.3 = (bf16[4,3,160,128]{3,2,1,0:T(8,128)(2,1)S(1)}, bf16[4,3,160,128]{3,2,1,0:T(8,128)(2,1)S(1)}, u32[]{:S(2)}, u32[]{:S(2)}) collective-permute-start(bf16[4,3,160,128]{3,2,1,0:T(8,128)(2,1)S(1)} %get-tuple-element.47), channel_id=1, source_target_pairs={{0,16},{16,0},{32,48},{48,32},{64,80},{80,64},{96,112},{112,96},{1... | collective-permute-start | bytes 1474568 | tf_op jit(solution)/shard_map/ppermute | solution.py:226
  110.6 1.5 collective-permute-done.3
  112.1 0.1 add_convert_fusion
  112.2 12.3 %all_to_all.32 = bf16[4,3,160,128]{3,2,1,0:T(8,128)(2,1)S(1)} all-to-all(bf16[4,3,160,128]{3,2,1,0:T(8,128)(2,1)S(1)} %add_convert_fusion), channel_id=1, replica_groups={{0,4,8,12},{1,5,9,13},{2,6,10,14},{3,7,11,15},{16,20,24,28},{17,21,25,2..., dimensions={0} | all-to-all | bytes 983040 | tf_op jit(solution)/shard_map/all_to_all | solution.py:228
  124.5 0.1 convert_reduce_fusion
  124.6 0.1 fusion.2
  124.7 10.0 %all-gather = bf16[8,160,128]{2,1,0:T(8,128)(2,1)S(1)} all-gather(bf16[2,160,128]{2,1,0:T(8,128)(2,1)S(1)} %pad_maximum_fusion.1), channel_id=2, replica_groups={{0,4,8,12},{1,5,9,13},{2,6,10,14},{3,7,11,15},{16,20,24,28},{17,21,25,2..., dimensions={0}, use_global_device_ids=true | all-gather | bytes 409600 | tf_op jit(solution)/shard_map/all_gather | solution.py:233
  134.7 6.2 %all-gather.1 = bf16[8,2,160,128]{3,2,1,0:T(8,128)(2,1)S(1)} all-gather(bf16[4,2,160,128]{3,2,1,0:T(8,128)(2,1)S(1)} %bitcast.23), channel_id=3, replica_groups={{0,16},{32,48},{64,80},{96,112},{128,144},{160,176},{192,208},{224,240}..., dimensions={0}, use_global_device_ids=true | all-gather | bytes 983040 | tf_op jit(solution)/shard_map/all_gather | solution.py:234
  140.9 1.4 backward_parts.1
  142.2 13.0 %all_to_all.33.parts_ref = bf16[4,320,224]{2,1,0:T(8,128)(2,1)S(1)} all-to-all(bf16[4,320,224]{2,1,0:T(8,128)(2,1)S(1)} %backward_parts.1), channel_id=1, replica_groups={{0,1,2,3},{4,5,6,7},{8,9,10,11},{12,13,14,15},{16,17,18,19},{20,21,22,2..., dimensions={0} | all-to-all | bytes 1146880 | tf_op jit(solution)/shard_map/all_to_all | solution.py:238
  155.3 0.1 gather_rows.1
  155.4 0.5 broadcast.12
  155.9 0.7 reduce
  156.7 48.5 %all_to_all.34 = bf16[64,2,640]{2,1,0:T(2,128)(2,1)S(1)} all-to-all(bf16[64,2,640]{2,1,0:T(2,128)(2,1)S(1)} %reshape.4), channel_id=1, replica_groups=mesh['ep'=64,'etp'=16] {'ep'}, dimensions={0} | all-to-all | bytes 327680 | tf_op jit(solution)/shard_map/all_to_all | solution.py:240
  205.2 0.1 reshape.5
  205.3 0.9 combine_rows.1
  (5 shorter events, 0.1 us)
Async XLA Ops:
  0.0 1.2 copy-start
  1.2 1.2 copy-start.1
  2.4 1.2 copy-start.2
  3.5 1.4 copy-start.5
  3.5 1.5 copy-start.6
  3.5 1.6 copy-start.3
  3.5 1.6 copy-start.4
  7.9 75.4 %all-to-all-start = ((bf16[64,2,1152]{2,1,0:T(2,128)(2,1)}), bf16[64,2,1152]{2,1,0:T(2,128)(2,1)}, u32[]{:S(2)}, u32[]{:S(2)}) async-start(bf16[64,2,1152]{2,1,0:T(2,128)(2,1)} %copy.18), calls=%async_computation | async-start | bytes 589824 | tf_op jit(solution)/shard_map/all_to_all | solution.py:212
  38.4 33.8 %collective-permute-start = (bf16[2688,128]{1,0:T(8,128)(2,1)}, bf16[2688,128]{1,0:T(8,128)(2,1)S(1)}, u32[]{:S(2)}, u32[]{:S(2)}) collective-permute-start(bf16[2688,128]{1,0:T(8,128)(2,1)} %get-tuple-element.38), channel_id=1, source_target_pairs={{0,12},{1,13},{2,14},{3,15},{4,0},{5,1},{6,2},{7,3},{8,4},{9,5},{1... | collective-permute-start | bytes 2064392 | tf_op jit(solution)/shard_map/ppermute | solution.py:198
  43.1 29.2 %collective-permute-start.1 = (bf16[2688,128]{1,0:T(8,128)(2,1)}, bf16[2688,128]{1,0:T(8,128)(2,1)S(1)}, u32[]{:S(2)}, u32[]{:S(2)}) collective-permute-start(bf16[2688,128]{1,0:T(8,128)(2,1)} %get-tuple-element.39), channel_id=1, source_target_pairs={{0,4},{1,5},{2,6},{3,7},{4,8},{5,9},{6,10},{7,11},{8,12},{9,13},{1... | collective-permute-start | bytes 2064392 | tf_op jit(solution)/shard_map/ppermute | solution.py:198
  45.0 31.4 %collective-permute-start.2 = (bf16[2688,128]{1,0:T(8,128)(2,1)S(1)}, bf16[2688,128]{1,0:T(8,128)(2,1)S(1)}, u32[]{:S(2)}, u32[]{:S(2)}) collective-permute-start(bf16[2688,128]{1,0:T(8,128)(2,1)S(1)} %get-tuple-element.40), channel_id=1, source_target_pairs={{0,8},{1,9},{2,10},{3,11},{4,12},{5,13},{6,14},{7,15},{8,0},{9,1},... | collective-permute-start | bytes 2064392 | tf_op jit(solution)/shard_map/ppermute | solution.py:198
  106.1 6.0 %collective-permute-start.3 = (bf16[4,3,160,128]{3,2,1,0:T(8,128)(2,1)S(1)}, bf16[4,3,160,128]{3,2,1,0:T(8,128)(2,1)S(1)}, u32[]{:S(2)}, u32[]{:S(2)}) collective-permute-start(bf16[4,3,160,128]{3,2,1,0:T(8,128)(2,1)S(1)} %get-tuple-element.47), channel_id=1, source_target_pairs={{0,16},{16,0},{32,48},{48,32},{64,80},{80,64},{96,112},{112,96},{1... | collective-permute-start | bytes 1474568 | tf_op jit(solution)/shard_map/ppermute | solution.py:226

commit v3 on v2

--- a/solution.py
+++ b/solution.py
@@ -30,24 +30,52 @@
     )
 
 
-def pack_kernel(gate_ref, up_ref, down_ref, *outs):
+def pack_kernel(gate_ref, up_ref, down_ref, *rest):
+    outs, sems = rest[:SIDE], rest[SIDE]
     quarter = gate_ref.shape[0] // SIDE
     lanes = gate_ref.shape[1]
     mine = lax.axis_index("etp") // SIDE
+    copies = []
     for step, out in zip(STEPS, outs):
         first = pl.multiple_of(lax.rem(mine + step, SIDE) * quarter, lanes)
-        out[pl.ds(0, quarter), :] = gate_ref[pl.ds(first, quarter), :]
-        out[pl.ds(quarter, quarter), :] = up_ref[pl.ds(first, quarter), :]
+        pairs = [
+            (gate_ref.at[pl.ds(first, quarter)], out.at[pl.ds(0, quarter)]),
+            (up_ref.at[pl.ds(first, quarter)], out.at[pl.ds(quarter, quarter)]),
+        ]
         for j in range(quarter // lanes):
             at = pl.multiple_of(first + j * lanes, lanes)
-            out[pl.ds(2 * quarter + j * lanes, lanes), :] = down_ref[:, pl.ds(at, lanes)]
-
-
-def dispatch_kernel(routes_ref, gates_ref, tokens_ref, grads_ref, inputs_out, grads_out, picks_out):
+            pairs.append(
+                (down_ref.at[:, pl.ds(at, lanes)], out.at[pl.ds(2 * quarter + j * lanes, lanes)])
+            )
+        for source, target in pairs:
+            copy = pltpu.make_async_copy(source, target, sems.at[len(copies)])
+            copy.start()
+            copies.append(copy)
+    for copy in copies:
+        copy.wait()
+
+
+def pack_weights(gate, up, down):
+    quarter = gate.shape[0] // SIDE
+    lanes = gate.shape[1]
+    shape = jax.ShapeDtypeStruct((3 * quarter, lanes), gate.dtype)
+    return pl.pallas_call(
+        pack_kernel,
+        out_shape=[shape] * SIDE,
+        in_specs=[pl.BlockSpec(memory_space=pl.ANY)] * 3,
+        out_specs=[pl.BlockSpec(memory_space=pltpu.VMEM)] * SIDE,
+        scratch_shapes=[pltpu.SemaphoreType.DMA((SIDE * (2 + quarter // lanes),))],
+        compiler_params=pltpu.CompilerParams(vmem_limit_bytes=VMEM_BYTES),
+        cost_estimate=pl.CostEstimate(flops=0, bytes_accessed=6_000_000, transcendentals=0),
+        name="pack_weights",
+    )(gate, up, down)
+
+
+def dispatch_kernel(routes_ref, gates_ref, tokens_ref, grads_ref, sent_out, picks_out):
     group, top = routes_ref.shape
     capacity = picks_out.shape[0]
     width = picks_out.shape[2]
-    sides = inputs_out.shape[0]
+    sides = sent_out.shape[0]
     half = tokens_ref.shape[1] // 2
     expert = lax.broadcasted_iota(jnp.int32, (group, width), 1) // 2
     member = jnp.zeros((group, width), jnp.float32)
@@ -71,11 +99,11 @@
         two = mm(pick * weight, grads, TN, lax.Precision.HIGHEST)
         input_parts.append(jnp.where(even, one[:, :half], one[:, half:]))
         grad_parts.append(jnp.where(even, two[:, :half], two[:, half:]))
-    fill = jnp.zeros((width, inputs_out.shape[1] - capacity * half), jnp.float32)
+    fill = jnp.zeros((width, sent_out.shape[2] - capacity * half), jnp.float32)
     one = jnp.concatenate([*input_parts, fill], axis=1)[:sides]
     two = jnp.concatenate([*grad_parts, fill], axis=1)[:sides]
-    inputs_out[...] = one.astype(inputs_out.dtype)
-    grads_out[...] = two.astype(grads_out.dtype)
+    sent_out[:, 0, :] = one.astype(sent_out.dtype)
+    sent_out[:, 1, :] = two.astype(sent_out.dtype)
 
 
 def spread_kernel(inputs_ref, grads_ref, out_ref):
@@ -120,26 +148,34 @@
 
 def backward_kernel(d_ref, w0, w1, w2, w3, out_ref):
     share = out_ref.shape[2]
-    rows = d_ref.shape[3]
     quarter = SIDE * share
     mine = lax.axis_index("etp") // SIDE
+    grads = []
+    for step in STEPS:
+        place = lax.rem(mine + step, SIDE)
+        grads.append(
+            jnp.concatenate(
+                [
+                    jnp.concatenate([d_ref[side, place, 0], d_ref[side, place, 1]], axis=1)
+                    for side in range(2)
+                ],
+                axis=0,
+            )
+        )
     for x in range(SIDE):
-        for side in range(2):
-            total = None
-            for step, w in zip(STEPS, (w0, w1, w2, w3)):
-                place = lax.rem(mine + step, SIDE)
-                grads = jnp.concatenate([d_ref[side, place, 0], d_ref[side, place, 1]], axis=1)
-                pair = jnp.concatenate(
-                    [w[pl.ds(x * share, share), :], w[pl.ds(quarter + x * share, share), :]],
-                    axis=1,
-                )
-                one = mm(grads, pair, NT)
-                total = one if total is None else total + one
-            out_ref[x, pl.ds(side * rows, rows), :] = total.astype(out_ref.dtype)
+        total = None
+        for grad, w in zip(grads, (w0, w1, w2, w3)):
+            pair = jnp.concatenate(
+                [w[pl.ds(x * share, share), :], w[pl.ds(quarter + x * share, share), :]], axis=1
+            )
+            one = mm(grad, pair, NT)
+            total = one if total is None else total + one
+        out_ref[x] = total.astype(out_ref.dtype)
 
 
 def gather_kernel(parts_ref, out_ref):
     groups = out_ref.shape[0]
+    width = out_ref.shape[2]
     half = parts_ref.shape[2]
     capacity = parts_ref.shape[1] // groups
     blocks = []
@@ -149,8 +185,10 @@
         for x in range(1, SIDE):
             total = total + parts_ref[x, here, :].astype(jnp.float32)
         blocks.append(total)
-    blocks.append(jnp.zeros((groups, out_ref.shape[1] - capacity * half), jnp.float32))
-    out_ref[...] = jnp.concatenate(blocks, axis=1).astype(out_ref.dtype)
+    blocks.append(jnp.zeros((groups, 2 * width - capacity * half), jnp.float32))
+    line = jnp.concatenate(blocks, axis=1).astype(out_ref.dtype)
+    out_ref[:, 0, :] = line[:, :width]
+    out_ref[:, 1, :] = line[:, width:]
 
 
 def combine_kernel(came_ref, picks_ref, out_ref):
@@ -184,12 +222,7 @@
     along_y = [[SIDE * y + x for y in range(SIDE)] for x in range(SIDE)]
     cores = [[2 * z, 2 * z + 1] for z in range(experts)]
 
-    packed = in_vmem(pack_kernel, [((3 * quarter, lanes), bf16)] * SIDE, 3, 0, "pack_weights")(
-        gate_weight[0], up_weight[0], down_weight[0]
-    )
-    routes, route_gates, tokens, grad_out, *packed = lax.optimization_barrier(
-        (routes, route_gates, tokens, grad_out, *packed)
-    )
+    packed = pack_weights(gate_weight[0], up_weight[0], down_weight[0])
     weights = [packed[0]]
     for step, block in zip(STEPS[1:], packed[1:]):
         pairs = [
@@ -198,20 +231,17 @@
         weights.append(lax.ppermute(block, "etp", pairs))
     weights = [weights[0], weights[2], weights[1], weights[3]]
 
-    sent_inputs, sent_grads, picks = in_vmem(
+    sent, picks = in_vmem(
         dispatch_kernel,
         [
-            ((ep_count, line), bf16),
-            ((ep_count, line), bf16),
+            ((ep_count, 2, line), bf16),
             ((capacity, group_rows, LANES), bf16),
         ],
         4,
         0,
         "dispatch_rows",
     )(routes, route_gates, tokens, grad_out)
-    came = lax.all_to_all(
-        jnp.stack([sent_inputs, sent_grads], axis=1), "ep", split_axis=0, concat_axis=0, tiled=True
-    )
+    came = lax.all_to_all(sent, "ep", split_axis=0, concat_axis=0, tiled=True)
     came, *weights = lax.optimization_barrier((came, *weights))
     (wide,) = in_vmem(
         spread_kernel, [((SIDE, 2, rows_all, half), bf16)], 2, 0, "spread_rows"
@@ -230,17 +260,18 @@
     sigma = jax.nn.sigmoid(pre_gate)
     d_up = (d_hidden * pre_gate * sigma).astype(bf16)
     d_gate = (d_hidden * pre_up * sigma * (1.0 + pre_gate * (1.0 - sigma))).astype(bf16)
-    grads = lax.all_gather(jnp.stack([d_gate, d_up]), "etp", axis_index_groups=along_y)
+    grads = jnp.broadcast_to(jnp.stack([d_gate, d_up])[None], (SIDE, 2, *d_up.shape))
+    grads = lax.all_to_all(grads, "etp", 0, 0, tiled=True, axis_index_groups=along_y)
     grads = lax.all_gather(grads, "ep", axis_index_groups=cores)
     (back,) = in_vmem(
         backward_kernel, [((SIDE, rows_all, half), bf16)], 5, flops * 2 // 3, "backward_parts"
     )(grads, *weights)
     back = lax.all_to_all(back, "etp", 0, 0, tiled=True, axis_index_groups=along_x)
-    (summed,) = in_vmem(gather_kernel, [((ep_count, back_line), bf16)], 1, 0, "gather_rows")(back)
+    (summed,) = in_vmem(gather_kernel, [((ep_count, 2, back_line // 2), bf16)], 1, 0, "gather_rows")(back)
     returned = lax.all_to_all(summed, "ep", split_axis=0, concat_axis=0, tiled=True)
     (result,) = in_vmem(
         combine_kernel, [((group_rows, 2 * half), bf16)], 2, 0, "combine_rows"
-    )(returned, picks)
+    )(returned.reshape(ep_count, back_line), picks)
     return result
 
 

time: 207 us -> 205 us (level)
  waiting for transfers between devices: 36.2 us -> 29.7 us
  blocking collectives: 110 us -> 113 us
    all_gather x1 -> x0, blocking collectives: 10 us -> none  [on_device(): lax.all_gather(jnp.stack([d_gate, d_up]), 'etp', axis_index_groups=along_y)]
    all_to_all x0 -> x1, blocking collectives: none -> 8.25 us  [on_device(): lax.all_to_all(grads, 'etp', 0, 0, tiled=True, axis_index_groups=along_y)]
    all_to_all x1, blocking collectives: 48.5 us -> 54.7 us  [on_device(): lax.all_to_all(summed, 'ep', split_axis=0, concat_axis=0, tiled=True)]
    all_to_all x1, waiting for transfers between devices: 6.82 us -> 0.63 us  [on_device(): came = lax.all_to_all(sent, 'ep', split_axis=0, concat_axis=0, tiled=True)]
    unnamed x17 -> x13, local copies, waits for them, and re-layouts: 3.74 us -> 6.5 us
    pallas_call x3, Pallas kernels: 3.23 us -> 5.62 us  [the longest x1 2.94 us: pack_weights(): pl.pallas_call(pack_kernel, out_shape=[shape] * SIDE, in_specs=[pl.BlockS...]
  transfers between devices with their start and end apart: 5 -> 5, of which waited for: 4 -> 4; matrix products, arithmetic and copies ran while one was open for 0% -> 0% of each run, Pallas kernels for 0% -> 1%
where the time goes in v3:
time: 205 us; the launch traced here: 204 us
  blocking collectives  113 us (55%)
  starting transfers between devices  45.6 us (22%)
  waiting for transfers between devices  29.7 us (14%)
  Pallas kernels  9.13 us (4%)
  local copies, waits for them, and re-layouts  6.6 us (3%)
    all_to_all x1, blocking collectives, on_device(): lax.all_to_all(summed, 'ep', split_axis=0, concat_axis=0, tiled=True)  54.7 us
    all_to_all x1, starting transfers between devices, on_device(): came = lax.all_to_all(sent, 'ep', split_axis=0, concat_axis=0, tiled=True)  30.4 us
    ppermute x3, waiting for transfers between devices, on_device(): weights.append(lax.ppermute(block, 'etp', pairs))  27.6 us
    all_to_all x1, blocking collectives, on_device(): lax.all_to_all(wide, 'etp', 0, 0, tiled=True, axis_index_groups=along_x)  19.4 us
    all_to_all x1, blocking collectives, on_device(): lax.all_to_all(back, 'etp', 0, 0, tiled=True, axis_index_groups=along_x)  13 us
    all_to_all x1, blocking collectives, on_device(): lax.all_to_all(partial, 'etp', 0, 0, tiled=True, axis_index_groups=along_y)  12.4 us
    ppermute x3, starting transfers between devices, on_device(): weights.append(lax.ppermute(block, 'etp', pairs))  10.1 us
    all_to_all x1, blocking collectives, on_device(): lax.all_to_all(grads, 'etp', 0, 0, tiled=True, axis_index_groups=along_y)  8.25 us
  transfers between devices with their start and end apart: 5, of which 4 were waited for; matrix products, arithmetic and copies ran while one was open for 0% of the time, Pallas kernels for 1%

profile of v3, /device:TPU:1, one launch (start us, length us, event | category | flops | bytes accessed | tf_op | source)
XLA Modules:
  0.0 204.0 jit_solution(1348963734029890309)
XLA Ops:
  0.0 0.8 copy.11.routes_ref
  0.8 0.8 copy.12.gates_ref
  1.5 0.0 copy-start.3
  1.5 0.7 copy-done.3
  2.2 0.0 copy-start.4
  2.2 0.7 copy-done.4
  3.0 2.5 %dispatch_rows.1 = (bf16[64,2,1152]{2,1,0:T(2,128)(2,1)}, bf16[5,16,128]{2,1,0:T(8,128)(2,1)S(1)}) custom-call(s32[16,8]{1,0:T(8,128)S(1)} %copy.11.routes_ref, f32[16,8]{1,0:T(8,128)S(1)} %copy.12.gates_ref, bf16[16,448]{1,0:T(8,128)(2,1)S(1)} %copy-done.3, bf16[16,448]{1,0:T(8,128)(2,1)S(1)} %copy-done.4), custom_call_target="tpu_custom_call" | custom-call | bytes 2000000 | tf_op jit(solution)/shard_map/dispatch_rows/pallas_call | solution.py:234
  5.4 30.4 %all-to-all-start = ((bf16[64,2,1152]{2,1,0:T(2,128)(2,1)}), bf16[64,2,1152]{2,1,0:T(2,128)(2,1)S(1)}, u32[]{:S(2)}, u32[]{:S(2)}) async-start(bf16[64,2,1152]{2,1,0:T(2,128)(2,1)} %get-tuple-element.18), calls=%async_computation | async-start | bytes 589824 | tf_op jit(solution)/shard_map/all_to_all | solution.py:244
  35.9 0.0 copy-start
  35.9 1.2 copy-done
  37.0 0.0 copy-start.1
  37.0 1.2 copy-done.1
  38.2 0.0 copy-start.2
  38.2 1.2 copy-done.2
  39.4 2.9 %pack_weights.1 = (bf16[2688,128]{1,0:T(8,128)(2,1)S(1)}, bf16[2688,128]{1,0:T(8,128)(2,1)S(1)}, bf16[2688,128]{1,0:T(8,128)(2,1)S(1)}, bf16[2688,128]{1,0:T(8,128)(2,1)S(1)}) custom-call(bf16[3584,128]{1,0:T(8,128)(2,1)S(1)} %bitcast.11, bf16[3584,128]{1,0:T(8,128)(2,1)S(1)} %bitcast.12, bf16[128,3584]{1,0:T(8,128)(2,1)S(1)} %bitcast.13), custom_call_target="tpu_custom_call" | custom-call | bytes 6000000 | tf_op jit(solution)/shard_map/pack_weights/pallas_call | solution.py:62
  42.3 4.6 %collective-permute-start = (bf16[2688,128]{1,0:T(8,128)(2,1)S(1)}, bf16[2688,128]{1,0:T(8,128)(2,1)S(1)}, u32[]{:S(2)}, u32[]{:S(2)}) collective-permute-start(bf16[2688,128]{1,0:T(8,128)(2,1)S(1)} %get-tuple-element.20), channel_id=1, source_target_pairs={{0,12},{1,13},{2,14},{3,15},{4,0},{5,1},{6,2},{7,3},{8,4},{9,5},{1... | collective-permute-start | bytes 2064392 | tf_op jit(solution)/shard_map/ppermute | solution.py:231
  47.0 1.9 collective-permute-start.1
  48.9 3.5 %collective-permute-start.2 = (bf16[2688,128]{1,0:T(8,128)(2,1)S(1)}, bf16[2688,128]{1,0:T(8,128)(2,1)S(1)}, u32[]{:S(2)}, u32[]{:S(2)}) collective-permute-start(bf16[2688,128]{1,0:T(8,128)(2,1)S(1)} %get-tuple-element.22), channel_id=1, source_target_pairs={{0,8},{1,9},{2,10},{3,11},{4,12},{5,13},{6,14},{7,15},{8,0},{9,1},... | collective-permute-start | bytes 2064392 | tf_op jit(solution)/shard_map/ppermute | solution.py:231
  52.5 23.5 %collective-permute-done.w1 = bf16[2688,128]{1,0:T(8,128)(2,1)S(1)} collective-permute-done((bf16[2688,128]{1,0:T(8,128)(2,1)S(1)}, bf16[2688,128]{1,0:T(8,128)(2,1)S(1)}, u32[]{:S(2)}, u32[]{:S(2)}) %collective-permute-start) | collective-permute-done | bytes 688160 | tf_op jit(solution)/shard_map/ppermute | solution.py:231
  75.9 0.0 collective-permute-done.1.w2
  75.9 4.2 %collective-permute-done.2.w3 = bf16[2688,128]{1,0:T(8,128)(2,1)S(1)} collective-permute-done((bf16[2688,128]{1,0:T(8,128)(2,1)S(1)}, bf16[2688,128]{1,0:T(8,128)(2,1)S(1)}, u32[]{:S(2)}, u32[]{:S(2)}) %collective-permute-start.2) | collective-permute-done | bytes 688160 | tf_op jit(solution)/shard_map/ppermute | solution.py:231
  80.1 0.6 all-to-all-done
  80.8 0.2 spread_rows.1
  81.0 19.4 %all_to_all.30.x_ref = bf16[4,2,320,224]{3,2,1,0:T(8,128)(2,1)S(1)} all-to-all(bf16[4,2,320,224]{3,2,1,0:T(8,128)(2,1)S(1)} %spread_rows.1), channel_id=1, replica_groups={{0,1,2,3},{4,5,6,7},{8,9,10,11},{12,13,14,15},{16,17,18,19},{20,21,22,2..., dimensions={0} | all-to-all | bytes 2293760 | tf_op jit(solution)/shard_map/all_to_all | solution.py:249
  100.4 1.6 forward_parts.1
  102.0 5.1 %collective-permute-start.3 = (bf16[4,3,160,128]{3,2,1,0:T(8,128)(2,1)S(1)}, bf16[4,3,160,128]{3,2,1,0:T(8,128)(2,1)S(1)}, u32[]{:S(2)}, u32[]{:S(2)}) collective-permute-start(bf16[4,3,160,128]{3,2,1,0:T(8,128)(2,1)S(1)} %get-tuple-element.29), channel_id=1, source_target_pairs={{0,16},{16,0},{32,48},{48,32},{64,80},{80,64},{96,112},{112,96},{1... | collective-permute-start | bytes 1474568 | tf_op jit(solution)/shard_map/ppermute | solution.py:256
  107.1 1.5 collective-permute-done.3
  108.6 0.1 add_convert_fusion
  108.7 12.4 %all_to_all.31 = bf16[4,3,160,128]{3,2,1,0:T(8,128)(2,1)S(1)} all-to-all(bf16[4,3,160,128]{3,2,1,0:T(8,128)(2,1)S(1)} %add_convert_fusion), channel_id=1, replica_groups={{0,4,8,12},{1,5,9,13},{2,6,10,14},{3,7,11,15},{16,20,24,28},{17,21,25,2..., dimensions={0} | all-to-all | bytes 983040 | tf_op jit(solution)/shard_map/all_to_all | solution.py:258
  121.0 0.1 convert_reduce_fusion
  121.1 0.1 fusion.2
  121.2 8.3 %all_to_all.32 = bf16[4,2,160,128]{3,2,1,0:T(8,128)(2,1)S(1)} all-to-all(bf16[4,2,160,128]{3,2,1,0:T(8,128)(2,1)S(1)} %broadcast_in_dim.2), channel_id=1, replica_groups={{0,4,8,12},{1,5,9,13},{2,6,10,14},{3,7,11,15},{16,20,24,28},{17,21,25,2..., dimensions={0} | all-to-all | bytes 655360 | tf_op jit(solution)/shard_map/all_to_all | solution.py:264
  129.5 4.8 %all-gather = bf16[8,2,160,128]{3,2,1,0:T(8,128)(2,1)S(1)} all-gather(bf16[4,2,160,128]{3,2,1,0:T(8,128)(2,1)S(1)} %all_to_all.32), channel_id=2, replica_groups={{0,16},{32,48},{64,80},{96,112},{128,144},{160,176},{192,208},{224,240}..., dimensions={0}, use_global_device_ids=true | all-gather | bytes 983040 | tf_op jit(solution)/shard_map/all_gather | solution.py:265
  134.3 0.9 backward_parts.1
  135.1 13.0 %all_to_all.33.parts_ref = bf16[4,320,224]{2,1,0:T(8,128)(2,1)S(1)} all-to-all(bf16[4,320,224]{2,1,0:T(8,128)(2,1)S(1)} %backward_parts.1), channel_id=1, replica_groups={{0,1,2,3},{4,5,6,7},{8,9,10,11},{12,13,14,15},{16,17,18,19},{20,21,22,2..., dimensions={0} | all-to-all | bytes 1146880 | tf_op jit(solution)/shard_map/all_to_all | solution.py:269
  148.2 0.2 gather_rows.1
  148.4 54.7 %all_to_all.34 = bf16[64,2,640]{2,1,0:T(2,128)(2,1)S(1)} all-to-all(bf16[64,2,640]{2,1,0:T(2,128)(2,1)S(1)} %gather_rows.1), channel_id=1, replica_groups=mesh['ep'=64,'etp'=16] {'ep'}, dimensions={0} | all-to-all | bytes 327680 | tf_op jit(solution)/shard_map/all_to_all | solution.py:271
  203.1 0.9 combine_rows.1
  (5 shorter events, 0.1 us)
Async XLA Ops:
  1.5 0.7 copy-start.3
  2.2 0.7 copy-start.4
  5.4 75.3 %all-to-all-start = ((bf16[64,2,1152]{2,1,0:T(2,128)(2,1)}), bf16[64,2,1152]{2,1,0:T(2,128)(2,1)S(1)}, u32[]{:S(2)}, u32[]{:S(2)}) async-start(bf16[64,2,1152]{2,1,0:T(2,128)(2,1)} %get-tuple-element.18), calls=%async_computation | async-start | bytes 589824 | tf_op jit(solution)/shard_map/all_to_all | solution.py:244
  35.9 1.2 copy-start
  37.0 1.2 copy-start.1
  38.2 1.2 copy-start.2
  42.3 33.6 %collective-permute-start = (bf16[2688,128]{1,0:T(8,128)(2,1)S(1)}, bf16[2688,128]{1,0:T(8,128)(2,1)S(1)}, u32[]{:S(2)}, u32[]{:S(2)}) collective-permute-start(bf16[2688,128]{1,0:T(8,128)(2,1)S(1)} %get-tuple-element.20), channel_id=1, source_target_pairs={{0,12},{1,13},{2,14},{3,15},{4,0},{5,1},{6,2},{7,3},{8,4},{9,5},{1... | collective-permute-start | bytes 2064392 | tf_op jit(solution)/shard_map/ppermute | solution.py:231
  47.0 28.9 %collective-permute-start.1 = (bf16[2688,128]{1,0:T(8,128)(2,1)S(1)}, bf16[2688,128]{1,0:T(8,128)(2,1)S(1)}, u32[]{:S(2)}, u32[]{:S(2)}) collective-permute-start(bf16[2688,128]{1,0:T(8,128)(2,1)S(1)} %get-tuple-element.21), channel_id=1, source_target_pairs={{0,4},{1,5},{2,6},{3,7},{4,8},{5,9},{6,10},{7,11},{8,12},{9,13},{1... | collective-permute-start | bytes 2064392 | tf_op jit(solution)/shard_map/ppermute | solution.py:231
  48.9 31.2 %collective-permute-start.2 = (bf16[2688,128]{1,0:T(8,128)(2,1)S(1)}, bf16[2688,128]{1,0:T(8,128)(2,1)S(1)}, u32[]{:S(2)}, u32[]{:S(2)}) collective-permute-start(bf16[2688,128]{1,0:T(8,128)(2,1)S(1)} %get-tuple-element.22), channel_id=1, source_target_pairs={{0,8},{1,9},{2,10},{3,11},{4,12},{5,13},{6,14},{7,15},{8,0},{9,1},... | collective-permute-start | bytes 2064392 | tf_op jit(solution)/shard_map/ppermute | solution.py:231
  102.0 6.6 %collective-permute-start.3 = (bf16[4,3,160,128]{3,2,1,0:T(8,128)(2,1)S(1)}, bf16[4,3,160,128]{3,2,1,0:T(8,128)(2,1)S(1)}, u32[]{:S(2)}, u32[]{:S(2)}) collective-permute-start(bf16[4,3,160,128]{3,2,1,0:T(8,128)(2,1)S(1)} %get-tuple-element.29), channel_id=1, source_target_pairs={{0,16},{16,0},{32,48},{48,32},{64,80},{80,64},{96,112},{112,96},{1... | collective-permute-start | bytes 1474568 | tf_op jit(solution)/shard_map/ppermute | solution.py:256

commit v4 on v3

v4 whole, which is shorter than its diff:
```python
import jax
import jax.numpy as jnp
from jax import lax
from jax.experimental import pallas as pl
from jax.experimental.pallas import tpu as pltpu
from jax.sharding import PartitionSpec as P

SIDE = 4
STEPS = (0, 1, 3, 2)
NT = (((1,), (1,)), ((), ()))
NN = (((1,), (0,)), ((), ()))
TN = (((0,), (0,)), ((), ()))
LANES = 128
VMEM_BYTES = 48 * 1024 * 1024


def mm(a, b, dims, precision=None):
    return lax.dot_general(a, b, dims, precision=precision, preferred_element_type=jnp.float32)


def in_vmem(kernel, shapes, count, flops, name):
    return pl.pallas_call(
        kernel,
        out_shape=[jax.ShapeDtypeStruct(*shape) for shape in shapes],
        in_specs=[pl.BlockSpec(memory_space=pltpu.VMEM)] * count,
        out_specs=[pl.BlockSpec(memory_space=pltpu.VMEM)] * len(shapes),
        compiler_params=pltpu.CompilerParams(vmem_limit_bytes=VMEM_BYTES),
        cost_estimate=pl.CostEstimate(flops=flops, bytes_accessed=2_000_000, transcendentals=0),
        name=name,
    )


def start_kernel(routes_any, gates_any, tokens_any, grads_any, gate_any, up_any, down_any, *rest):
    sent_out, picks_out = rest[:2]
    own, ahead, behind, far_low, far_high = rest[2:7]
    routes_ref, gates_ref, tokens_ref, grads_ref, small_sems, sems = rest[7:]
    quarter = gate_any.shape[0] // SIDE
    lanes = gate_any.shape[1]
    small = []
    for which, (source, target) in enumerate(
        (
            (routes_any, routes_ref),
            (gates_any, gates_ref),
            (tokens_any, tokens_ref),
            (grads_any, grads_ref),
        )
    ):
        copy = pltpu.make_async_copy(source, target, small_sems.at[which])
        copy.start()
        small.append(copy)
    mine = lax.axis_index("etp") // SIDE
    copies = []

    def go(source, target):
        copy = pltpu.make_async_copy(source, target, sems.at[len(copies)])
        copy.start()
        copies.append(copy)

    for step, outs in ((2, (far_low, far_high)), (1, (ahead,)), (3, (behind,)), (0, (own,))):
        first = pl.multiple_of(lax.rem(mine + step, SIDE) * quarter, lanes)
        cut = outs[0].shape[0] - quarter
        go(gate_any.at[pl.ds(first, quarter)], outs[0].at[pl.ds(0, quarter)])
        if len(outs) == 1:
            go(up_any.at[pl.ds(first, quarter)], outs[0].at[pl.ds(quarter, quarter)])
            base = 2 * quarter
        else:
            go(up_any.at[pl.ds(first, cut)], outs[0].at[pl.ds(quarter, cut)])
            go(up_any.at[pl.ds(first + cut, quarter - cut)], outs[1].at[pl.ds(0, quarter - cut)])
            base = quarter - cut
        for j in range(quarter // lanes):
            at = pl.multiple_of(first + j * lanes, lanes)
            go(down_any.at[:, pl.ds(at, lanes)], outs[-1].at[pl.ds(base + j * lanes, lanes)])

    for copy in small:
        copy.wait()
    top, group = routes_ref.shape
    capacity, sides, _ = picks_out.shape
    half = tokens_ref.shape[1] // 2
    expert = lax.broadcasted_iota(jnp.int32, (sides, group), 0) // 2
    member = jnp.zeros((sides, group), jnp.float32)
    weight = jnp.zeros((sides, group), jnp.float32)
    for k in range(top):
        named = expert == routes_ref[k : k + 1, :]
        member = jnp.where(named, 1.0, member)
        weight = jnp.where(named, gates_ref[k : k + 1, :], weight)
    earlier = lax.broadcasted_iota(jnp.int32, (group, group), 0) < lax.broadcasted_iota(
        jnp.int32, (group, group), 1
    )
    rank = mm(member, earlier.astype(jnp.float32), NN)
    even = lax.broadcasted_iota(jnp.int32, (sides, half), 0) % 2 == 0
    tokens = tokens_ref[...].astype(jnp.float32)
    grads = grads_ref[...].astype(jnp.float32)
    input_parts, grad_parts = [], []
    for s in range(capacity):
        pick = jnp.where((rank > s - 0.5) & (rank < s + 0.5), member, 0.0)
        picks_out[s] = pick
        one = mm(pick, tokens, NN)
        two = mm(pick * weight, grads, NN, lax.Precision.HIGHEST)
        input_parts.append(jnp.where(even, one[:, :half], one[:, half:]))
        grad_parts.append(jnp.where(even, two[:, :half], two[:, half:]))
    fill = jnp.zeros((sides, sent_out.shape[2] - capacity * half), jnp.float32)
    sent_out[:, 0, :] = jnp.concatenate([*input_parts, fill], axis=1).astype(sent_out.dtype)
    sent_out[:, 1, :] = jnp.concatenate([*grad_parts, fill], axis=1).astype(sent_out.dtype)
    for copy in copies:
        copy.wait()


def start(routes, gates, tokens, grads, gate, up, down, capacity, sides, line):
    quarter = gate.shape[0] // SIDE
    lanes = gate.shape[1]
    whole = jax.ShapeDtypeStruct((3 * quarter, lanes), gate.dtype)
    part = jax.ShapeDtypeStruct((3 * quarter // 2, lanes), gate.dtype)
    shapes = [
        jax.ShapeDtypeStruct((sides, 2, line), tokens.dtype),
        jax.ShapeDtypeStruct((capacity, sides, routes.shape[1]), jnp.float32),
        whole,
        whole,
        whole,
        part,
        part,
    ]
    small = (routes, gates, tokens, grads)
    return pl.pallas_call(
        start_kernel,
        out_shape=shapes,
        in_specs=[pl.BlockSpec(memory_space=pl.ANY)] * 7,
        out_specs=[pl.BlockSpec(memory_space=pltpu.VMEM)] * len(shapes),
        scratch_shapes=[
            *[pltpu.VMEM(array.shape, array.dtype) for array in small],
            pltpu.SemaphoreType.DMA((len(small),)),
            pltpu.SemaphoreType.DMA((SIDE * (2 + quarter // lanes) + 1,)),
        ],
        compiler_params=pltpu.CompilerParams(vmem_limit_bytes=60 * 1024 * 1024),
        cost_estimate=pl.CostEstimate(flops=0, bytes_accessed=6_000_000, transcendentals=0),
        name="start_rows",
    )(*small, gate, up, down)


def rows_of(parts, first, count):
    for part in parts:
        if first < part.shape[0]:
            return part[pl.ds(first, count), :]
        first -= part.shape[0]
    return None


def spread_kernel(inputs_ref, grads_ref, out_ref):
    groups = inputs_ref.shape[0]
    half = out_ref.shape[3]
    for which, ref in enumerate((inputs_ref, grads_ref)):
        for s in range(out_ref.shape[2] // groups):
            block = ref[:, s * half : (s + 1) * half]
            for x in range(SIDE):
                out_ref[x, which, pl.ds(s * groups, groups), :] = block


def forward_kernel(x_ref, own, ahead, behind, far_low, far_high, keep_ref, send_ref):
    share = x_ref.shape[3]
    quarter = SIDE * share
    lanes = own.shape[1]
    rows = keep_ref.shape[2]
    mine = lax.axis_index("etp") // SIDE
    core = lax.rem(lax.axis_index("ep"), 2)
    for step, w in zip(STEPS, ((own,), (ahead,), (behind,), (far_low, far_high))):
        place = lax.rem(mine + step, SIDE)
        down = jnp.concatenate(
            [rows_of(w, 2 * quarter + j * lanes, lanes) for j in range(quarter // lanes)], axis=1
        )
        for out_ref, side in ((keep_ref, core), (send_ref, 1 - core)):
            here = pl.ds(pl.multiple_of(side * rows, 32), rows)
            both = None
            hidden = None
            for x in range(SIDE):
                pair = jnp.concatenate(
                    [rows_of(w, x * share, share), rows_of(w, quarter + x * share, share)],
                    axis=1,
                )
                one = mm(x_ref[x, 0, here, :], pair, NN)
                two = mm(x_ref[x, 1, here, :], down[:, x * share : (x + 1) * share], NT)
                both = one if both is None else both + one
                hidden = two if hidden is None else hidden + two
            out_ref[place, 0] = both[:, :lanes].astype(out_ref.dtype)
            out_ref[place, 1] = both[:, lanes:].astype(out_ref.dtype)
            out_ref[place, 2] = hidden.astype(out_ref.dtype)


def backward_kernel(d_ref, own, ahead, behind, far_low, far_high, out_ref):
    share = out_ref.shape[2]
    quarter = SIDE * share
    mine = lax.axis_index("etp") // SIDE
    grads = []
    for step in STEPS:
        place = lax.rem(mine + step, SIDE)
        grads.append(
            jnp.concatenate(
                [
                    jnp.concatenate([d_ref[side, place, 0], d_ref[side, place, 1]], axis=1)
                    for side in range(2)
                ],
                axis=0,
            )
        )
    for x in range(SIDE):
        total = None
        for grad, w in zip(grads, ((own,), (ahead,), (behind,), (far_low, far_high))):
            pair = jnp.concatenate(
                [rows_of(w, x * share, share), rows_of(w, quarter + x * share, share)], axis=1
            )
            one = mm(grad, pair, NT)
            total = one if total is None else total + one
        out_ref[x] = total.astype(out_ref.dtype)


def gather_kernel(parts_ref, out_ref):
    groups = out_ref.shape[0]
    width = out_ref.shape[2]
    half = parts_ref.shape[2]
    capacity = parts_ref.shape[1] // groups
    blocks = []
    for s in range(capacity):
        here = pl.ds(s * groups, groups)
        total = parts_ref[0, here, :].astype(jnp.float32)
        for x in range(1, SIDE):
            total = total + parts_ref[x, here, :].astype(jnp.float32)
        blocks.append(total)
    blocks.append(jnp.zeros((groups, 2 * width - capacity * half), jnp.float32))
    line = jnp.concatenate(blocks, axis=1).astype(out_ref.dtype)
    out_ref[:, 0, :] = line[:, :width]
    out_ref[:, 1, :] = line[:, width:]


def combine_kernel(came_ref, picks_ref, out_ref):
    capacity, sides, group = picks_ref.shape
    half = out_ref.shape[1] // 2
    odd = lax.broadcasted_iota(jnp.int32, (sides, group), 0) % 2
    totals = [None, None]
    for s in range(capacity):
        block = came_ref[:, s * half : (s + 1) * half].astype(jnp.float32)
        for side in range(2):
            one = mm(jnp.where(odd == side, picks_ref[s], 0.0), block, TN)
            totals[side] = one if totals[side] is None else totals[side] + one
    out_ref[...] = jnp.concatenate(totals, axis=1).astype(out_ref.dtype)


def on_device(tokens, grad_out, routes, route_gates, gate_weight, up_weight, down_weight):
    bf16 = jnp.bfloat16
    ep_count = lax.axis_size("ep")
    experts = ep_count // 2
    group_rows, top_count = routes.shape
    capacity = min(group_rows, 5 * group_rows * top_count // (4 * experts))
    half = tokens.shape[1] // 2
    rows_all = ep_count * capacity
    lanes = gate_weight.shape[2]
    quarter = gate_weight.shape[1] // SIDE
    line = -(-capacity * half // LANES) * LANES
    back_line = -(-capacity * half // (2 * LANES)) * 2 * LANES
    along_x = [[SIDE * y + x for x in range(SIDE)] for y in range(SIDE)]
    along_y = [[SIDE * y + x for y in range(SIDE)] for x in range(SIDE)]
    cores = [[2 * z, 2 * z + 1] for z in range(experts)]

    sent, picks, own, to_ahead, to_behind, to_far_low, to_far_high = start(
        routes.T,
        route_gates.T,
        tokens,
        grad_out,
        gate_weight[0],
        up_weight[0],
        down_weight[0],
        capacity,
        ep_count,
        line,
    )

    def shift(block, step):
        pairs = [
            (SIDE * y + x, SIDE * ((y + step) % SIDE) + x) for y in range(SIDE) for x in range(SIDE)
        ]
        return lax.ppermute(block, "etp", pairs)

    far_low = shift(shift(to_far_low, 1), 1)
    far_high = shift(shift(to_far_high, -1), -1)
    weights = [own, shift(to_behind, -1), shift(to_ahead, 1), far_low, far_high]

    came = lax.all_to_all(sent, "ep", split_axis=0, concat_axis=0, tiled=True)
    came, *weights = lax.optimization_barrier((came, *weights))
    (wide,) = in_vmem(
        spread_kernel, [((SIDE, 2, rows_all, half), bf16)], 2, 0, "spread_rows"
    )(came[:, 0], came[:, 1])
    gathered = lax.all_to_all(wide, "etp", 0, 0, tiled=True, axis_index_groups=along_x)

    flops = 2 * 3 * rows_all * quarter * lanes * SIDE
    part = (SIDE, 3, rows_all // 2, lanes)
    keep, send = in_vmem(
        forward_kernel, [(part, jnp.float32), (part, bf16)], 6, flops, "forward_parts"
    )(gathered, *weights)
    other = lax.ppermute(send, "ep", [(i, i ^ 1) for i in range(ep_count)])
    partial = (keep + other.astype(jnp.float32)).astype(bf16)
    partial = lax.all_to_all(partial, "etp", 0, 0, tiled=True, axis_index_groups=along_y)
    pre_gate, pre_up, d_hidden = jnp.sum(partial.astype(jnp.float32), axis=0)
    sigma = jax.nn.sigmoid(pre_gate)
    d_up = (d_hidden * pre_gate * sigma).astype(bf16)
    d_gate = (d_hidden * pre_up * sigma * (1.0 + pre_gate * (1.0 - sigma))).astype(bf16)
    grads = jnp.broadcast_to(jnp.stack([d_gate, d_up])[None], (SIDE, 2, *d_up.shape))
    grads = lax.all_to_all(grads, "etp", 0, 0, tiled=True, axis_index_groups=along_y)
    grads = lax.all_gather(grads, "ep", axis_index_groups=cores)
    (back,) = in_vmem(
        backward_kernel, [((SIDE, rows_all, half), bf16)], 6, flops * 2 // 3, "backward_parts"
    )(grads, *weights)
    back = lax.all_to_all(back, "etp", 0, 0, tiled=True, axis_index_groups=along_x)
    (summed,) = in_vmem(gather_kernel, [((ep_count, 2, back_line // 2), bf16)], 1, 0, "gather_rows")(back)
    returned = lax.all_to_all(summed, "ep", split_axis=0, concat_axis=0, tiled=True)
    (result,) = in_vmem(
        combine_kernel, [((group_rows, 2 * half), bf16)], 2, 0, "combine_rows"
    )(returned.reshape(ep_count, back_line), picks)
    return result


def solution(mesh):
    return jax.shard_map(
        on_device,
        mesh=mesh,
        in_specs=(
            P("ep", "etp"),
            P("ep", "etp"),
            P("ep", None),
            P("ep", None),
            P("ep", None, "etp"),
            P("ep", None, "etp"),
            P("ep", "etp", None),
        ),
        out_specs=P("ep", "etp"),
        check_vma=False,
    )
```

time: 205 us -> 198 us (0.966)
  starting transfers between devices: 45.6 us -> 53.3 us
  local copies, waits for them, and re-layouts: 6.6 us -> 0.13 us
  blocking collectives: 113 us -> 107 us
    ppermute x3 -> x6, waiting for transfers between devices: 27.6 us -> 17.9 us  [shift(): return lax.ppermute(block, 'etp', pairs)]
    ppermute x3 -> x6, starting transfers between devices: 10.1 us -> 18.3 us  [shift(): return lax.ppermute(block, 'etp', pairs)]
    all_to_all x1, waiting for transfers between devices: 0.63 us -> 8.57 us  [on_device(): came = lax.all_to_all(sent, 'ep', split_axis=0, concat_axis=0, tiled=True)]
    all_to_all x1, blocking collectives: 54.7 us -> 47.9 us  [on_device(): lax.all_to_all(summed, 'ep', split_axis=0, concat_axis=0, tiled=True)]
    unnamed x13 -> x5, local copies, waits for them, and re-layouts: 6.5 us -> 0.03 us
    pallas_call x4 -> x3, Pallas kernels: 7.88 us -> 7.25 us  [the longest x1 4.81 us: start(): pl.pallas_call(start_kernel, out_shape=shapes, in_specs=[pl.BlockSpec(mem...]
  transfers between devices with their start and end apart: 5 -> 8, of which waited for: 4 -> 4; matrix products, arithmetic and copies ran while one was open for 0% -> 0% of each run, Pallas kernels for 1% -> 0%
where the time goes in v4:
time: 198 us; the launch traced here: 197 us
  blocking collectives  107 us (54%)
  starting transfers between devices  53.3 us (27%)
  waiting for transfers between devices  28 us (14%)
  Pallas kernels  8.53 us (4%)
    all_to_all x1, blocking collectives, on_device(): lax.all_to_all(summed, 'ep', split_axis=0, concat_axis=0, tiled=True)  47.9 us
    all_to_all x1, starting transfers between devices, on_device(): came = lax.all_to_all(sent, 'ep', split_axis=0, concat_axis=0, tiled=True)  30.4 us
    all_to_all x1, blocking collectives, on_device(): lax.all_to_all(wide, 'etp', 0, 0, tiled=True, axis_index_groups=along_x)  20.2 us
    ppermute x6, starting transfers between devices, shift(): return lax.ppermute(block, 'etp', pairs)  18.3 us
    ppermute x6, waiting for transfers between devices, shift(): return lax.ppermute(block, 'etp', pairs)  17.9 us
    all_to_all x1, blocking collectives, on_device(): lax.all_to_all(back, 'etp', 0, 0, tiled=True, axis_index_groups=along_x)  13.2 us
    all_to_all x1, blocking collectives, on_device(): lax.all_to_all(partial, 'etp', 0, 0, tiled=True, axis_index_groups=along_y)  12.3 us
    all_to_all x1, waiting for transfers between devices, on_device(): came = lax.all_to_all(sent, 'ep', split_axis=0, concat_axis=0, tiled=True)  8.57 us
  transfers between devices with their start and end apart: 8, of which 4 were waited for; matrix products, arithmetic and copies ran while one was open for 0% of the time, Pallas kernels for 0%

profile of v4, /device:TPU:1, one launch (start us, length us, event | category | flops | bytes accessed | tf_op | source)
XLA Modules:
  0.0 196.9 jit_solution(6928269465742394193)
XLA Ops:
  0.0 4.8 %start_rows.1 = (bf16[64,2,1152]{2,1,0:T(2,128)(2,1)}, f32[5,64,16]{2,1,0:T(8,128)}, bf16[2688,128]{1,0:T(8,128)(2,1)}, bf16[2688,128]{1,0:T(8,128)(2,1)}, bf16[...) custom-call(s32[8,16]{1,0:T(8,128)} %bitcast.18, f32[8,16]{1,0:T(8,128)} %bitcast.19, ...), custom_call_target="tpu_custom_call" | custom-call | bytes 6000000 | tf_op jit(solution)/shard_map/start_rows/pallas_call | solution.py:123
  4.8 30.4 %all-to-all-start = ((bf16[64,2,1152]{2,1,0:T(2,128)(2,1)}), bf16[64,2,1152]{2,1,0:T(2,128)(2,1)S(1)}, u32[]{:S(2)}, u32[]{:S(2)}) async-start(bf16[64,2,1152]{2,1,0:T(2,128)(2,1)} %get-tuple-element.20), calls=%async_computation | async-start | bytes 589824 | tf_op jit(solution)/shard_map/all_to_all | solution.py:284
  35.2 3.2 %collective-permute-start.2 = (bf16[1344,128]{1,0:T(8,128)(2,1)}, bf16[1344,128]{1,0:T(8,128)(2,1)S(1)}, u32[]{:S(2)}, u32[]{:S(2)}) collective-permute-start(bf16[1344,128]{1,0:T(8,128)(2,1)} %get-tuple-element.24), channel_id=1, source_target_pairs={{0,4},{1,5},{2,6},{3,7},{4,8},{5,9},{6,10},{7,11},{8,12},{9,13},{1... | collective-permute-start | bytes 1032200 | tf_op jit(solution)/shard_map/ppermute | solution.py:278
  38.5 3.4 %collective-permute-start.4 = (bf16[1344,128]{1,0:T(8,128)(2,1)}, bf16[1344,128]{1,0:T(8,128)(2,1)S(1)}, u32[]{:S(2)}, u32[]{:S(2)}) collective-permute-start(bf16[1344,128]{1,0:T(8,128)(2,1)} %get-tuple-element.25), channel_id=1, source_target_pairs={{0,12},{1,13},{2,14},{3,15},{4,0},{5,1},{6,2},{7,3},{8,4},{9,5},{1... | collective-permute-start | bytes 1032200 | tf_op jit(solution)/shard_map/ppermute | solution.py:278
  41.8 3.4 %collective-permute-start = (bf16[2688,128]{1,0:T(8,128)(2,1)}, bf16[2688,128]{1,0:T(8,128)(2,1)S(1)}, u32[]{:S(2)}, u32[]{:S(2)}) collective-permute-start(bf16[2688,128]{1,0:T(8,128)(2,1)} %get-tuple-element.22), channel_id=1, source_target_pairs={{0,12},{1,13},{2,14},{3,15},{4,0},{5,1},{6,2},{7,3},{8,4},{9,5},{1... | collective-permute-start | bytes 2064392 | tf_op jit(solution)/shard_map/ppermute | solution.py:278
  45.2 1.9 collective-permute-start.1
  47.1 0.8 collective-permute-done.2
  47.9 1.9 collective-permute-start.3
  49.8 0.0 collective-permute-done.4
  49.8 4.6 %collective-permute-start.5 = (bf16[1344,128]{1,0:T(8,128)(2,1)S(1)}, bf16[1344,128]{1,0:T(8,128)(2,1)S(1)}, u32[]{:S(2)}, u32[]{:S(2)}) collective-permute-start(bf16[1344,128]{1,0:T(8,128)(2,1)S(1)} %collective-permute-done.4), channel_id=1, source_target_pairs={{0,12},{1,13},{2,14},{3,15},{4,0},{5,1},{6,2},{7,3},{8,4},{9,5},{1... | collective-permute-start | bytes 1032200 | tf_op jit(solution)/shard_map/ppermute | solution.py:278
  54.4 17.1 %collective-permute-done.3.far_low = bf16[1344,128]{1,0:T(8,128)(2,1)S(1)} collective-permute-done((bf16[1344,128]{1,0:T(8,128)(2,1)S(1)}, bf16[1344,128]{1,0:T(8,128)(2,1)S(1)}, u32[]{:S(2)}, u32[]{:S(2)}) %collective-permute-start.3) | collective-permute-done | bytes 344096 | tf_op jit(solution)/shard_map/ppermute | solution.py:278
  71.5 0.0 collective-permute-done.5.far_high
  71.5 0.0 collective-permute-done.ahead
  71.5 0.0 collective-permute-done.1.behind
  71.5 8.6 %all-to-all-done = bf16[64,2,1152]{2,1,0:T(2,128)(2,1)S(1)} async-done(((bf16[64,2,1152]{2,1,0:T(2,128)(2,1)}), bf16[64,2,1152]{2,1,0:T(2,128)(2,1)S(1)}, u32[]{:S(2)}, u32[]{:S(2)}) %all-to-all-start) | async-done | bytes 294944 | tf_op jit(solution)/shard_map/all_to_all | solution.py:284
  80.2 0.2 spread_rows.1
  80.3 0.0 copy-start
  80.4 20.2 %all_to_all.30.x_ref = bf16[4,2,320,224]{3,2,1,0:T(8,128)(2,1)S(1)} all-to-all(bf16[4,2,320,224]{3,2,1,0:T(8,128)(2,1)S(1)} %spread_rows.1), channel_id=1, replica_groups={{0,1,2,3},{4,5,6,7},{8,9,10,11},{12,13,14,15},{16,17,18,19},{20,21,22,2..., dimensions={0} | all-to-all | bytes 2293760 | tf_op jit(solution)/shard_map/all_to_all | solution.py:289
  100.5 0.0 copy-done
  100.6 1.6 forward_parts.1
  102.1 4.5 %collective-permute-start.6 = (bf16[4,3,160,128]{3,2,1,0:T(8,128)(2,1)S(1)}, bf16[4,3,160,128]{3,2,1,0:T(8,128)(2,1)S(1)}, u32[]{:S(2)}, u32[]{:S(2)}) collective-permute-start(bf16[4,3,160,128]{3,2,1,0:T(8,128)(2,1)S(1)} %get-tuple-element.33), channel_id=1, source_target_pairs={{0,16},{16,0},{32,48},{48,32},{64,80},{80,64},{96,112},{112,96},{1... | collective-permute-start | bytes 1474568 | tf_op jit(solution)/shard_map/ppermute | solution.py:296
  106.7 1.5 collective-permute-done.6
  108.1 0.1 add_convert_fusion
  108.2 12.3 %all_to_all.31 = bf16[4,3,160,128]{3,2,1,0:T(8,128)(2,1)S(1)} all-to-all(bf16[4,3,160,128]{3,2,1,0:T(8,128)(2,1)S(1)} %add_convert_fusion), channel_id=1, replica_groups={{0,4,8,12},{1,5,9,13},{2,6,10,14},{3,7,11,15},{16,20,24,28},{17,21,25,2..., dimensions={0} | all-to-all | bytes 983040 | tf_op jit(solution)/shard_map/all_to_all | solution.py:298
  120.6 0.1 convert_reduce_fusion
  120.6 0.1 fusion.2
  120.8 8.3 %all_to_all.32 = bf16[4,2,160,128]{3,2,1,0:T(8,128)(2,1)S(1)} all-to-all(bf16[4,2,160,128]{3,2,1,0:T(8,128)(2,1)S(1)} %broadcast_in_dim.2), channel_id=1, replica_groups={{0,4,8,12},{1,5,9,13},{2,6,10,14},{3,7,11,15},{16,20,24,28},{17,21,25,2..., dimensions={0} | all-to-all | bytes 655360 | tf_op jit(solution)/shard_map/all_to_all | solution.py:304
  129.0 4.8 %all-gather = bf16[8,2,160,128]{3,2,1,0:T(8,128)(2,1)S(1)} all-gather(bf16[4,2,160,128]{3,2,1,0:T(8,128)(2,1)S(1)} %all_to_all.32), channel_id=2, replica_groups={{0,16},{32,48},{64,80},{96,112},{128,144},{160,176},{192,208},{224,240}..., dimensions={0}, use_global_device_ids=true | all-gather | bytes 983040 | tf_op jit(solution)/shard_map/all_gather | solution.py:305
  133.8 0.9 backward_parts.1
  134.7 0.0 copy-start.1
  134.7 13.2 %all_to_all.33.parts_ref = bf16[4,320,224]{2,1,0:T(8,128)(2,1)S(1)} all-to-all(bf16[4,320,224]{2,1,0:T(8,128)(2,1)S(1)} %backward_parts.1), channel_id=1, replica_groups={{0,1,2,3},{4,5,6,7},{8,9,10,11},{12,13,14,15},{16,17,18,19},{20,21,22,2..., dimensions={0} | all-to-all | bytes 1146880 | tf_op jit(solution)/shard_map/all_to_all | solution.py:309
  147.8 0.2 gather_rows.1
  148.0 47.9 %all_to_all.34 = bf16[64,2,640]{2,1,0:T(2,128)(2,1)S(1)} all-to-all(bf16[64,2,640]{2,1,0:T(2,128)(2,1)S(1)} %gather_rows.1), channel_id=1, replica_groups=mesh['ep'=64,'etp'=16] {'ep'}, dimensions={0} | all-to-all | bytes 327680 | tf_op jit(solution)/shard_map/all_to_all | solution.py:311
  196.0 0.0 copy-done.1
  196.0 0.9 combine_rows.1
  (5 shorter events, 0.1 us)
Async XLA Ops:
  4.8 75.3 %all-to-all-start = ((bf16[64,2,1152]{2,1,0:T(2,128)(2,1)}), bf16[64,2,1152]{2,1,0:T(2,128)(2,1)S(1)}, u32[]{:S(2)}, u32[]{:S(2)}) async-start(bf16[64,2,1152]{2,1,0:T(2,128)(2,1)} %get-tuple-element.20), calls=%async_computation | async-start | bytes 589824 | tf_op jit(solution)/shard_map/all_to_all | solution.py:284
  35.2 12.6 %collective-permute-start.2 = (bf16[1344,128]{1,0:T(8,128)(2,1)}, bf16[1344,128]{1,0:T(8,128)(2,1)S(1)}, u32[]{:S(2)}, u32[]{:S(2)}) collective-permute-start(bf16[1344,128]{1,0:T(8,128)(2,1)} %get-tuple-element.24), channel_id=1, source_target_pairs={{0,4},{1,5},{2,6},{3,7},{4,8},{5,9},{6,10},{7,11},{8,12},{9,13},{1... | collective-permute-start | bytes 1032200 | tf_op jit(solution)/shard_map/ppermute | solution.py:278
  38.5 11.3 %collective-permute-start.4 = (bf16[1344,128]{1,0:T(8,128)(2,1)}, bf16[1344,128]{1,0:T(8,128)(2,1)S(1)}, u32[]{:S(2)}, u32[]{:S(2)}) collective-permute-start(bf16[1344,128]{1,0:T(8,128)(2,1)} %get-tuple-element.25), channel_id=1, source_target_pairs={{0,12},{1,13},{2,14},{3,15},{4,0},{5,1},{6,2},{7,3},{8,4},{9,5},{1... | collective-permute-start | bytes 1032200 | tf_op jit(solution)/shard_map/ppermute | solution.py:278
  41.8 29.7 %collective-permute-start = (bf16[2688,128]{1,0:T(8,128)(2,1)}, bf16[2688,128]{1,0:T(8,128)(2,1)S(1)}, u32[]{:S(2)}, u32[]{:S(2)}) collective-permute-start(bf16[2688,128]{1,0:T(8,128)(2,1)} %get-tuple-element.22), channel_id=1, source_target_pairs={{0,12},{1,13},{2,14},{3,15},{4,0},{5,1},{6,2},{7,3},{8,4},{9,5},{1... | collective-permute-start | bytes 2064392 | tf_op jit(solution)/shard_map/ppermute | solution.py:278
  45.2 26.4 %collective-permute-start.1 = (bf16[2688,128]{1,0:T(8,128)(2,1)}, bf16[2688,128]{1,0:T(8,128)(2,1)S(1)}, u32[]{:S(2)}, u32[]{:S(2)}) collective-permute-start(bf16[2688,128]{1,0:T(8,128)(2,1)} %get-tuple-element.23), channel_id=1, source_target_pairs={{0,4},{1,5},{2,6},{3,7},{4,8},{5,9},{6,10},{7,11},{8,12},{9,13},{1... | collective-permute-start | bytes 2064392 | tf_op jit(solution)/shard_map/ppermute | solution.py:278
  47.9 23.6 %collective-permute-start.3 = (bf16[1344,128]{1,0:T(8,128)(2,1)S(1)}, bf16[1344,128]{1,0:T(8,128)(2,1)S(1)}, u32[]{:S(2)}, u32[]{:S(2)}) collective-permute-start(bf16[1344,128]{1,0:T(8,128)(2,1)S(1)} %collective-permute-done.2), channel_id=1, source_target_pairs={{0,4},{1,5},{2,6},{3,7},{4,8},{5,9},{6,10},{7,11},{8,12},{9,13},{1... | collective-permute-start | bytes 1032200 | tf_op jit(solution)/shard_map/ppermute | solution.py:278
  49.8 21.7 %collective-permute-start.5 = (bf16[1344,128]{1,0:T(8,128)(2,1)S(1)}, bf16[1344,128]{1,0:T(8,128)(2,1)S(1)}, u32[]{:S(2)}, u32[]{:S(2)}) collective-permute-start(bf16[1344,128]{1,0:T(8,128)(2,1)S(1)} %collective-permute-done.4), channel_id=1, source_target_pairs={{0,12},{1,13},{2,14},{3,15},{4,0},{5,1},{6,2},{7,3},{8,4},{9,5},{1... | collective-permute-start | bytes 1032200 | tf_op jit(solution)/shard_map/ppermute | solution.py:278
  80.3 20.2 %copy-start = (bf16[2688,128]{1,0:T(8,128)(2,1)S(1)}, bf16[2688,128]{1,0:T(8,128)(2,1)}, u32[]{:S(2)}) copy-start(bf16[2688,128]{1,0:T(8,128)(2,1)} %get-tuple-element.27.own) | copy-start | bytes 2064388
  102.1 6.0 %collective-permute-start.6 = (bf16[4,3,160,128]{3,2,1,0:T(8,128)(2,1)S(1)}, bf16[4,3,160,128]{3,2,1,0:T(8,128)(2,1)S(1)}, u32[]{:S(2)}, u32[]{:S(2)}) collective-permute-start(bf16[4,3,160,128]{3,2,1,0:T(8,128)(2,1)S(1)} %get-tuple-element.33), channel_id=1, source_target_pairs={{0,16},{16,0},{32,48},{48,32},{64,80},{80,64},{96,112},{112,96},{1... | collective-permute-start | bytes 1474568 | tf_op jit(solution)/shard_map/ppermute | solution.py:296
  134.7 61.3 %copy-start.1 = (f32[5,64,16]{2,1,0:T(8,128)S(1)}, f32[5,64,16]{2,1,0:T(8,128)}, u32[]{:S(2)}) copy-start(f32[5,64,16]{2,1,0:T(8,128)} %get-tuple-element.34.picks_ref) | copy-start | bytes 61444

commit v5 on v4

--- a/solution.py
+++ b/solution.py
@@ -11,7 +11,7 @@
 NN = (((1,), (0,)), ((), ()))
 TN = (((0,), (0,)), ((), ()))
 LANES = 128
-VMEM_BYTES = 48 * 1024 * 1024
+VMEM_BYTES = 24 * 1024 * 1024
 
 
 def mm(a, b, dims, precision=None):
@@ -30,24 +30,9 @@
     )
 
 
-def start_kernel(routes_any, gates_any, tokens_any, grads_any, gate_any, up_any, down_any, *rest):
-    sent_out, picks_out = rest[:2]
-    own, ahead, behind, far_low, far_high = rest[2:7]
-    routes_ref, gates_ref, tokens_ref, grads_ref, small_sems, sems = rest[7:]
+def pack_kernel(gate_any, up_any, down_any, own, ahead, behind, far_low, far_high, sems):
     quarter = gate_any.shape[0] // SIDE
     lanes = gate_any.shape[1]
-    small = []
-    for which, (source, target) in enumerate(
-        (
-            (routes_any, routes_ref),
-            (gates_any, gates_ref),
-            (tokens_any, tokens_ref),
-            (grads_any, grads_ref),
-        )
-    ):
-        copy = pltpu.make_async_copy(source, target, small_sems.at[which])
-        copy.start()
-        small.append(copy)
     mine = lax.axis_index("etp") // SIDE
     copies = []
 
@@ -56,22 +41,54 @@
         copy.start()
         copies.append(copy)
 
-    for step, outs in ((2, (far_low, far_high)), (1, (ahead,)), (3, (behind,)), (0, (own,))):
+    for step, into in ((2, (far_low, far_high)), (1, (ahead,)), (3, (behind,)), (0, (own,))):
         first = pl.multiple_of(lax.rem(mine + step, SIDE) * quarter, lanes)
-        cut = outs[0].shape[0] - quarter
-        go(gate_any.at[pl.ds(first, quarter)], outs[0].at[pl.ds(0, quarter)])
-        if len(outs) == 1:
-            go(up_any.at[pl.ds(first, quarter)], outs[0].at[pl.ds(quarter, quarter)])
+        cut = into[0].shape[0] - quarter
+        go(gate_any.at[pl.ds(first, quarter)], into[0].at[pl.ds(0, quarter)])
+        if len(into) == 1:
+            go(up_any.at[pl.ds(first, quarter)], into[0].at[pl.ds(quarter, quarter)])
             base = 2 * quarter
         else:
-            go(up_any.at[pl.ds(first, cut)], outs[0].at[pl.ds(quarter, cut)])
-            go(up_any.at[pl.ds(first + cut, quarter - cut)], outs[1].at[pl.ds(0, quarter - cut)])
+            go(up_any.at[pl.ds(first, cut)], into[0].at[pl.ds(quarter, cut)])
+            go(up_any.at[pl.ds(first + cut, quarter - cut)], into[1].at[pl.ds(0, quarter - cut)])
             base = quarter - cut
         for j in range(quarter // lanes):
             at = pl.multiple_of(first + j * lanes, lanes)
-            go(down_any.at[:, pl.ds(at, lanes)], outs[-1].at[pl.ds(base + j * lanes, lanes)])
-
-    for copy in small:
+            go(down_any.at[:, pl.ds(at, lanes)], into[-1].at[pl.ds(base + j * lanes, lanes)])
+    for copy in copies:
+        copy.wait()
+
+
+def pack_weights(gate, up, down):
+    quarter = gate.shape[0] // SIDE
+    lanes = gate.shape[1]
+    whole = jax.ShapeDtypeStruct((3 * quarter, lanes), gate.dtype)
+    part = jax.ShapeDtypeStruct((3 * quarter // 2, lanes), gate.dtype)
+    shapes = [whole, whole, whole, part, part]
+    return pl.pallas_call(
+        pack_kernel,
+        out_shape=shapes,
+        in_specs=[pl.BlockSpec(memory_space=pl.ANY)] * 3,
+        out_specs=[pl.BlockSpec(memory_space=pltpu.VMEM)] * len(shapes),
+        scratch_shapes=[pltpu.SemaphoreType.DMA((SIDE * (2 + quarter // lanes) + 1,))],
+        compiler_params=pltpu.CompilerParams(vmem_limit_bytes=60 * 1024 * 1024),
+        cost_estimate=pl.CostEstimate(flops=0, bytes_accessed=6_000_000, transcendentals=0),
+        name="pack_weights",
+    )(gate, up, down)
+
+
+def dispatch_kernel(routes_any, gates_any, tokens_any, grads_any, sent_out, picks_out, *rest):
+    routes_ref, gates_ref, tokens_ref, grads_ref, sems = rest
+    pairs = (
+        (routes_any, routes_ref),
+        (gates_any, gates_ref),
+        (tokens_any, tokens_ref),
+        (grads_any, grads_ref),
+    )
+    copies = [pltpu.make_async_copy(*pair, sems.at[n]) for n, pair in enumerate(pairs)]
+    for copy in copies:
+        copy.start()
+    for copy in copies:
         copy.wait()
     top, group = routes_ref.shape
     capacity, sides, _ = picks_out.shape
@@ -101,39 +118,26 @@
     fill = jnp.zeros((sides, sent_out.shape[2] - capacity * half), jnp.float32)
     sent_out[:, 0, :] = jnp.concatenate([*input_parts, fill], axis=1).astype(sent_out.dtype)
     sent_out[:, 1, :] = jnp.concatenate([*grad_parts, fill], axis=1).astype(sent_out.dtype)
-    for copy in copies:
-        copy.wait()
-
-
-def start(routes, gates, tokens, grads, gate, up, down, capacity, sides, line):
-    quarter = gate.shape[0] // SIDE
-    lanes = gate.shape[1]
-    whole = jax.ShapeDtypeStruct((3 * quarter, lanes), gate.dtype)
-    part = jax.ShapeDtypeStruct((3 * quarter // 2, lanes), gate.dtype)
-    shapes = [
-        jax.ShapeDtypeStruct((sides, 2, line), tokens.dtype),
-        jax.ShapeDtypeStruct((capacity, sides, routes.shape[1]), jnp.float32),
-        whole,
-        whole,
-        whole,
-        part,
-        part,
-    ]
+
+
+def dispatch_rows(routes, gates, tokens, grads, capacity, sides, line):
     small = (routes, gates, tokens, grads)
     return pl.pallas_call(
-        start_kernel,
-        out_shape=shapes,
-        in_specs=[pl.BlockSpec(memory_space=pl.ANY)] * 7,
-        out_specs=[pl.BlockSpec(memory_space=pltpu.VMEM)] * len(shapes),
+        dispatch_kernel,
+        out_shape=[
+            jax.ShapeDtypeStruct((sides, 2, line), tokens.dtype),
+            jax.ShapeDtypeStruct((capacity, sides, routes.shape[1]), jnp.float32),
+        ],
+        in_specs=[pl.BlockSpec(memory_space=pl.ANY)] * len(small),
+        out_specs=[pl.BlockSpec(memory_space=pltpu.VMEM)] * 2,
         scratch_shapes=[
             *[pltpu.VMEM(array.shape, array.dtype) for array in small],
             pltpu.SemaphoreType.DMA((len(small),)),
-            pltpu.SemaphoreType.DMA((SIDE * (2 + quarter // lanes) + 1,)),
         ],
         compiler_params=pltpu.CompilerParams(vmem_limit_bytes=60 * 1024 * 1024),
-        cost_estimate=pl.CostEstimate(flops=0, bytes_accessed=6_000_000, transcendentals=0),
-        name="start_rows",
-    )(*small, gate, up, down)
+        cost_estimate=pl.CostEstimate(flops=0, bytes_accessed=500_000, transcendentals=0),
+        name="dispatch_rows",
+    )(*small)
 
 
 def rows_of(parts, first, count):
@@ -258,17 +262,11 @@
     along_y = [[SIDE * y + x for y in range(SIDE)] for x in range(SIDE)]
     cores = [[2 * z, 2 * z + 1] for z in range(experts)]
 
-    sent, picks, own, to_ahead, to_behind, to_far_low, to_far_high = start(
-        routes.T,
-        route_gates.T,
-        tokens,
-        grad_out,
-        gate_weight[0],
-        up_weight[0],
-        down_weight[0],
-        capacity,
-        ep_count,
-        line,
+    sent, picks = dispatch_rows(
+        routes.T, route_gates.T, tokens, grad_out, capacity, ep_count, line
+    )
+    own, to_ahead, to_behind, to_far_low, to_far_high = pack_weights(
+        gate_weight[0], up_weight[0], down_weight[0]
     )
 
     def shift(block, step):
@@ -277,12 +275,17 @@
         ]
         return lax.ppermute(block, "etp", pairs)
 
-    far_low = shift(shift(to_far_low, 1), 1)
-    far_high = shift(shift(to_far_high, -1), -1)
-    weights = [own, shift(to_behind, -1), shift(to_ahead, 1), far_low, far_high]
+    weights = [
+        own,
+        shift(to_behind, -1),
+        shift(to_ahead, 1),
+        shift(to_far_low, 1),
+        shift(to_far_high, -1),
+    ]
 
     came = lax.all_to_all(sent, "ep", split_axis=0, concat_axis=0, tiled=True)
     came, *weights = lax.optimization_barrier((came, *weights))
+    weights[3:] = [shift(weights[3], 1), shift(weights[4], -1)]
     (wide,) = in_vmem(
         spread_kernel, [((SIDE, 2, rows_all, half), bf16)], 2, 0, "spread_rows"
     )(came[:, 0], came[:, 1])

time: 198 us -> 198 us (level)
  blocking collectives: 107 us -> 85.5 us
  waiting for transfers between devices: 28 us -> 36.9 us
  starting transfers between devices: 53.3 us -> 58.7 us
  local copies, waits for them, and re-layouts: 0.13 us -> 4.42 us
  Pallas kernels: 8.53 us -> 11 us
    all_to_all x1 -> x0, blocking collectives: 20.2 us -> none  [on_device(): lax.all_to_all(wide, 'etp', 0, 0, tiled=True, axis_index_groups=along_x)]
    ppermute x6, waiting for transfers between devices: 17.9 us -> 24.1 us  [shift(): return lax.ppermute(block, 'etp', pairs)]
    unnamed x5 -> x21, local copies, waits for them, and re-layouts: 0.03 us -> 4.32 us
    all_to_all x0 -> x1, starting transfers between devices: none -> 4.14 us  [on_device(): lax.all_to_all(wide, 'etp', 0, 0, tiled=True, axis_index_groups=along_x)]
    all_to_all x0 -> x1, waiting for transfers between devices: none -> 2.61 us  [on_device(): lax.all_to_all(wide, 'etp', 0, 0, tiled=True, axis_index_groups=along_x)]
    pallas_call x1 -> x2, Pallas kernels: 4.81 us -> 6.22 us  [the longest x1 3.66 us: pack_weights(): pl.pallas_call(pack_kernel, out_shape=shapes, in_specs=[pl.BlockSpec(memo...]
  transfers between devices with their start and end apart: 8 -> 9, of which waited for: 4 -> 6; matrix products, arithmetic and copies ran while one was open for 0% -> 0% of each run, Pallas kernels for 0% -> 2%
where the time goes in v5:
time: 198 us; the launch traced here: 197 us
  blocking collectives  85.5 us (43%)
  starting transfers between devices  58.7 us (30%)
  waiting for transfers between devices  36.9 us (19%)
  Pallas kernels  11 us (6%)
  local copies, waits for them, and re-layouts  4.42 us (2%)
    all_to_all x1, blocking collectives, on_device(): lax.all_to_all(summed, 'ep', split_axis=0, concat_axis=0, tiled=True)  46.9 us
    all_to_all x1, starting transfers between devices, on_device(): came = lax.all_to_all(sent, 'ep', split_axis=0, concat_axis=0, tiled=True)  30.4 us
    ppermute x6, waiting for transfers between devices, shift(): return lax.ppermute(block, 'etp', pairs)  24.1 us
    ppermute x6, starting transfers between devices, shift(): return lax.ppermute(block, 'etp', pairs)  19.6 us
    all_to_all x1, blocking collectives, on_device(): lax.all_to_all(back, 'etp', 0, 0, tiled=True, axis_index_groups=along_x)  13.2 us
    all_to_all x1, blocking collectives, on_device(): lax.all_to_all(partial, 'etp', 0, 0, tiled=True, axis_index_groups=along_y)  12.3 us
    all_to_all x1, waiting for transfers between devices, on_device(): came = lax.all_to_all(sent, 'ep', split_axis=0, concat_axis=0, tiled=True)  8.78 us
    all_to_all x1, blocking collectives, on_device(): lax.all_to_all(grads, 'etp', 0, 0, tiled=True, axis_index_groups=along_y)  8.38 us
  transfers between devices with their start and end apart: 9, of which 6 were waited for; matrix products, arithmetic and copies ran while one was open for 0% of the time, Pallas kernels for 2%

profile of v5, /device:TPU:1, one launch (start us, length us, event | category | flops | bytes accessed | tf_op | source)
XLA Modules:
  0.0 197.0 jit_solution(16645225886176561544)
XLA Ops:
  0.0 2.6 %dispatch_rows.1 = (bf16[64,2,1152]{2,1,0:T(2,128)(2,1)}, f32[5,64,16]{2,1,0:T(8,128)}) custom-call(s32[8,16]{1,0:T(8,128)} %bitcast.18, f32[8,16]{1,0:T(8,128)} %bitcast.19, bf16[16,448]{1,0:T(8,128)(2,1)} %tokens_any.1, bf16[16,448]{1,0:T(8,128)(2,1)} %grads_any.1), custom_call_target="tpu_custom_call" | custom-call | bytes 500000 | tf_op jit(solution)/shard_map/dispatch_rows/pallas_call | solution.py:125
  2.6 30.4 %all-to-all-start = ((bf16[64,2,1152]{2,1,0:T(2,128)(2,1)}), bf16[64,2,1152]{2,1,0:T(2,128)(2,1)S(1)}, u32[]{:S(2)}, u32[]{:S(2)}) async-start(bf16[64,2,1152]{2,1,0:T(2,128)(2,1)} %get-tuple-element.20), calls=%async_computation | async-start | bytes 589824 | tf_op jit(solution)/shard_map/all_to_all | solution.py:286
  33.0 3.7 %pack_weights.1 = (bf16[2688,128]{1,0:T(8,128)(2,1)}, bf16[2688,128]{1,0:T(8,128)(2,1)}, bf16[2688,128]{1,0:T(8,128)(2,1)}, bf16[1344,128]{1,0:T(8,128)(2,1)}, bf16[1344,128]{1,0:T(8,128)(2,1)}) custom-call(bf16[3584,128]{1,0:T(8,128)(2,1)} %bitcast.14, bf16[3584,128]{1,0:T(8,128)(2,1)} %bitcast.15, bf16[128,3584]{1,0:T(8,128)(2,1)} %bitcast.16), custom_call_target="tpu_custom_call" | custom-call | bytes 6000000 | tf_op jit(solution)/shard_map/pack_weights/pallas_call | solution.py:68
  36.7 4.6 %collective-permute-start = (bf16[2688,128]{1,0:T(8,128)(2,1)}, bf16[2688,128]{1,0:T(8,128)(2,1)S(1)}, u32[]{:S(2)}, u32[]{:S(2)}) collective-permute-start(bf16[2688,128]{1,0:T(8,128)(2,1)} %get-tuple-element.22), channel_id=1, source_target_pairs={{0,12},{1,13},{2,14},{3,15},{4,0},{5,1},{6,2},{7,3},{8,4},{9,5},{1... | collective-permute-start | bytes 2064392 | tf_op jit(solution)/shard_map/ppermute | solution.py:276
  41.3 1.9 collective-permute-start.1
  43.2 1.9 collective-permute-start.2
  45.2 4.6 %collective-permute-start.3 = (bf16[1344,128]{1,0:T(8,128)(2,1)}, bf16[1344,128]{1,0:T(8,128)(2,1)S(1)}, u32[]{:S(2)}, u32[]{:S(2)}) collective-permute-start(bf16[1344,128]{1,0:T(8,128)(2,1)} %get-tuple-element.25), channel_id=1, source_target_pairs={{0,12},{1,13},{2,14},{3,15},{4,0},{5,1},{6,2},{7,3},{8,4},{9,5},{1... | collective-permute-start | bytes 1032200 | tf_op jit(solution)/shard_map/ppermute | solution.py:276
  49.7 18.5 %collective-permute-done.2 = bf16[1344,128]{1,0:T(8,128)(2,1)S(1)} collective-permute-done((bf16[1344,128]{1,0:T(8,128)(2,1)}, bf16[1344,128]{1,0:T(8,128)(2,1)S(1)}, u32[]{:S(2)}, u32[]{:S(2)}) %collective-permute-start.2) | collective-permute-done | bytes 344096 | tf_op jit(solution)/shard_map/ppermute | solution.py:276
  68.2 0.0 copy-start.8
  68.2 0.0 collective-permute-done.3
  68.2 0.0 copy-start.9
  68.2 0.0 collective-permute-done.ahead
  68.2 0.7 copy-done.8
  69.0 0.1 copy-done.9
  69.1 0.0 collective-permute-done.1.behind
  69.1 8.8 %all-to-all-done = bf16[64,2,1152]{2,1,0:T(2,128)(2,1)S(1)} async-done(((bf16[64,2,1152]{2,1,0:T(2,128)(2,1)}), bf16[64,2,1152]{2,1,0:T(2,128)(2,1)S(1)}, u32[]{:S(2)}, u32[]{:S(2)}) %all-to-all-start) | async-done | bytes 294944 | tf_op jit(solution)/shard_map/all_to_all | solution.py:286
  77.9 1.2 spread_rows.1
  79.2 4.1 %all-to-all-start.1 = ((bf16[4,2,320,224]{3,2,1,0:T(8,128)(2,1)}), bf16[4,2,320,224]{3,2,1,0:T(8,128)(2,1)S(1)}, u32[]{:S(2)}, u32[]{:S(2)}) async-start(bf16[4,2,320,224]{3,2,1,0:T(8,128)(2,1)} %spread_rows.1), calls=%async_computation.1 | async-start | bytes 2621440 | tf_op jit(solution)/shard_map/all_to_all | solution.py:292
  83.3 3.2 %collective-permute-start.4 = (bf16[1344,128]{1,0:T(8,128)(2,1)}, bf16[1344,128]{1,0:T(8,128)(2,1)S(1)}, u32[]{:S(2)}, u32[]{:S(2)}) collective-permute-start(bf16[1344,128]{1,0:T(8,128)(2,1)} %copy-done.8), channel_id=1, source_target_pairs={{0,4},{1,5},{2,6},{3,7},{4,8},{5,9},{6,10},{7,11},{8,12},{9,13},{1... | collective-permute-start | bytes 1032200 | tf_op jit(solution)/shard_map/ppermute | solution.py:276
  86.5 3.4 %collective-permute-start.5 = (bf16[1344,128]{1,0:T(8,128)(2,1)}, bf16[1344,128]{1,0:T(8,128)(2,1)S(1)}, u32[]{:S(2)}, u32[]{:S(2)}) collective-permute-start(bf16[1344,128]{1,0:T(8,128)(2,1)} %copy-done.9), channel_id=1, source_target_pairs={{0,12},{1,13},{2,14},{3,15},{4,0},{5,1},{6,2},{7,3},{8,4},{9,5},{1... | collective-permute-start | bytes 1032200 | tf_op jit(solution)/shard_map/ppermute | solution.py:276
  89.9 4.7 %collective-permute-done.4.far_low = bf16[1344,128]{1,0:T(8,128)(2,1)S(1)} collective-permute-done((bf16[1344,128]{1,0:T(8,128)(2,1)}, bf16[1344,128]{1,0:T(8,128)(2,1)S(1)}, u32[]{:S(2)}, u32[]{:S(2)}) %collective-permute-start.4) | collective-permute-done | bytes 344096 | tf_op jit(solution)/shard_map/ppermute | solution.py:276
  94.6 0.7 copy-done.1
  95.3 0.8 collective-permute-done.5.far_high
  96.2 0.7 copy-done.4
  96.9 2.6 %all-to-all-done.1.x_ref = bf16[4,2,320,224]{3,2,1,0:T(8,128)(2,1)S(1)} async-done(((bf16[4,2,320,224]{3,2,1,0:T(8,128)(2,1)}), bf16[4,2,320,224]{3,2,1,0:T(8,128)(2,1)S(1)}, u32[]{:S(2)}, u32[]{:S(2)}) %all-to-all-start.1) | async-done | bytes 1146912 | tf_op jit(solution)/shard_map/all_to_all | solution.py:292
  99.5 0.0 copy-done
  99.6 1.0 copy-done.2
  100.5 1.0 copy-done.5
  101.5 1.6 forward_parts.1
  103.1 4.5 %collective-permute-start.6 = (bf16[4,3,160,128]{3,2,1,0:T(8,128)(2,1)S(1)}, bf16[4,3,160,128]{3,2,1,0:T(8,128)(2,1)S(1)}, u32[]{:S(2)}, u32[]{:S(2)}) collective-permute-start(bf16[4,3,160,128]{3,2,1,0:T(8,128)(2,1)S(1)} %get-tuple-element.33), channel_id=1, source_target_pairs={{0,16},{16,0},{32,48},{48,32},{64,80},{80,64},{96,112},{112,96},{1... | collective-permute-start | bytes 1474568 | tf_op jit(solution)/shard_map/ppermute | solution.py:299
  107.6 1.5 collective-permute-done.6
  109.1 0.1 add_convert_fusion
  109.2 12.3 %all_to_all.30 = bf16[4,3,160,128]{3,2,1,0:T(8,128)(2,1)S(1)} all-to-all(bf16[4,3,160,128]{3,2,1,0:T(8,128)(2,1)S(1)} %add_convert_fusion), channel_id=1, replica_groups={{0,4,8,12},{1,5,9,13},{2,6,10,14},{3,7,11,15},{16,20,24,28},{17,21,25,2..., dimensions={0} | all-to-all | bytes 983040 | tf_op jit(solution)/shard_map/all_to_all | solution.py:301
  121.5 0.1 convert_reduce_fusion
  121.6 0.0 copy-start.3
  121.6 0.0 copy-start.6
  121.6 0.1 fusion.2
  121.7 8.4 %all_to_all.31 = bf16[4,2,160,128]{3,2,1,0:T(8,128)(2,1)S(1)} all-to-all(bf16[4,2,160,128]{3,2,1,0:T(8,128)(2,1)S(1)} %broadcast_in_dim.2), channel_id=1, replica_groups={{0,4,8,12},{1,5,9,13},{2,6,10,14},{3,7,11,15},{16,20,24,28},{17,21,25,2..., dimensions={0} | all-to-all | bytes 655360 | tf_op jit(solution)/shard_map/all_to_all | solution.py:307
  130.1 4.8 %all-gather = bf16[8,2,160,128]{3,2,1,0:T(8,128)(2,1)S(1)} all-gather(bf16[4,2,160,128]{3,2,1,0:T(8,128)(2,1)S(1)} %all_to_all.31), channel_id=2, replica_groups={{0,16},{32,48},{64,80},{96,112},{128,144},{160,176},{192,208},{224,240}..., dimensions={0}, use_global_device_ids=true | all-gather | bytes 983040 | tf_op jit(solution)/shard_map/all_gather | solution.py:308
  134.9 0.0 copy-done.3
  134.9 0.0 copy-done.6
  134.9 0.9 backward_parts.1
  135.8 0.0 copy-start.7
  135.8 13.2 %all_to_all.32.parts_ref = bf16[4,320,224]{2,1,0:T(8,128)(2,1)S(1)} all-to-all(bf16[4,320,224]{2,1,0:T(8,128)(2,1)S(1)} %backward_parts.1), channel_id=1, replica_groups={{0,1,2,3},{4,5,6,7},{8,9,10,11},{12,13,14,15},{16,17,18,19},{20,21,22,2..., dimensions={0} | all-to-all | bytes 1146880 | tf_op jit(solution)/shard_map/all_to_all | solution.py:312
  148.9 0.2 gather_rows.1
  149.1 46.9 %all_to_all.33 = bf16[64,2,640]{2,1,0:T(2,128)(2,1)S(1)} all-to-all(bf16[64,2,640]{2,1,0:T(2,128)(2,1)S(1)} %gather_rows.1), channel_id=1, replica_groups=mesh['ep'=64,'etp'=16] {'ep'}, dimensions={0} | all-to-all | bytes 327680 | tf_op jit(solution)/shard_map/all_to_all | solution.py:314
  196.0 0.0 copy-done.7
  196.0 0.9 combine_rows.1
  (10 shorter events, 0.1 us)
Async XLA Ops:
  2.6 75.3 %all-to-all-start = ((bf16[64,2,1152]{2,1,0:T(2,128)(2,1)}), bf16[64,2,1152]{2,1,0:T(2,128)(2,1)S(1)}, u32[]{:S(2)}, u32[]{:S(2)}) async-start(bf16[64,2,1152]{2,1,0:T(2,128)(2,1)} %get-tuple-element.20), calls=%async_computation | async-start | bytes 589824 | tf_op jit(solution)/shard_map/all_to_all | solution.py:286
  36.7 31.6 %collective-permute-start = (bf16[2688,128]{1,0:T(8,128)(2,1)}, bf16[2688,128]{1,0:T(8,128)(2,1)S(1)}, u32[]{:S(2)}, u32[]{:S(2)}) collective-permute-start(bf16[2688,128]{1,0:T(8,128)(2,1)} %get-tuple-element.22), channel_id=1, source_target_pairs={{0,12},{1,13},{2,14},{3,15},{4,0},{5,1},{6,2},{7,3},{8,4},{9,5},{1... | collective-permute-start | bytes 2064392 | tf_op jit(solution)/shard_map/ppermute | solution.py:276
  41.3 27.8 %collective-permute-start.1 = (bf16[2688,128]{1,0:T(8,128)(2,1)}, bf16[2688,128]{1,0:T(8,128)(2,1)S(1)}, u32[]{:S(2)}, u32[]{:S(2)}) collective-permute-start(bf16[2688,128]{1,0:T(8,128)(2,1)} %get-tuple-element.23), channel_id=1, source_target_pairs={{0,4},{1,5},{2,6},{3,7},{4,8},{5,9},{6,10},{7,11},{8,12},{9,13},{1... | collective-permute-start | bytes 2064392 | tf_op jit(solution)/shard_map/ppermute | solution.py:276
  43.2 25.0 %collective-permute-start.2 = (bf16[1344,128]{1,0:T(8,128)(2,1)}, bf16[1344,128]{1,0:T(8,128)(2,1)S(1)}, u32[]{:S(2)}, u32[]{:S(2)}) collective-permute-start(bf16[1344,128]{1,0:T(8,128)(2,1)} %get-tuple-element.24), channel_id=1, source_target_pairs={{0,4},{1,5},{2,6},{3,7},{4,8},{5,9},{6,10},{7,11},{8,12},{9,13},{1... | collective-permute-start | bytes 1032200 | tf_op jit(solution)/shard_map/ppermute | solution.py:276
  45.2 23.1 %collective-permute-start.3 = (bf16[1344,128]{1,0:T(8,128)(2,1)}, bf16[1344,128]{1,0:T(8,128)(2,1)S(1)}, u32[]{:S(2)}, u32[]{:S(2)}) collective-permute-start(bf16[1344,128]{1,0:T(8,128)(2,1)} %get-tuple-element.25), channel_id=1, source_target_pairs={{0,12},{1,13},{2,14},{3,15},{4,0},{5,1},{6,2},{7,3},{8,4},{9,5},{1... | collective-permute-start | bytes 1032200 | tf_op jit(solution)/shard_map/ppermute | solution.py:276
  68.2 0.7 copy-start.8
  68.2 0.8 copy-start.9
  79.2 20.4 %copy-start = (bf16[2688,128]{1,0:T(8,128)(2,1)S(1)}, bf16[2688,128]{1,0:T(8,128)(2,1)}, u32[]{:S(2)}) copy-start(bf16[2688,128]{1,0:T(8,128)(2,1)} %get-tuple-element.27.own) | copy-start | bytes 2064388
  79.2 20.4 %all-to-all-start.1 = ((bf16[4,2,320,224]{3,2,1,0:T(8,128)(2,1)}), bf16[4,2,320,224]{3,2,1,0:T(8,128)(2,1)S(1)}, u32[]{:S(2)}, u32[]{:S(2)}) async-start(bf16[4,2,320,224]{3,2,1,0:T(8,128)(2,1)} %spread_rows.1), calls=%async_computation.1 | async-start | bytes 2621440 | tf_op jit(solution)/shard_map/all_to_all | solution.py:292
  83.3 11.3 %collective-permute-start.4 = (bf16[1344,128]{1,0:T(8,128)(2,1)}, bf16[1344,128]{1,0:T(8,128)(2,1)S(1)}, u32[]{:S(2)}, u32[]{:S(2)}) collective-permute-start(bf16[1344,128]{1,0:T(8,128)(2,1)} %copy-done.8), channel_id=1, source_target_pairs={{0,4},{1,5},{2,6},{3,7},{4,8},{5,9},{6,10},{7,11},{8,12},{9,13},{1... | collective-permute-start | bytes 1032200 | tf_op jit(solution)/shard_map/ppermute | solution.py:276
  86.5 9.7 %collective-permute-start.5 = (bf16[1344,128]{1,0:T(8,128)(2,1)}, bf16[1344,128]{1,0:T(8,128)(2,1)S(1)}, u32[]{:S(2)}, u32[]{:S(2)}) collective-permute-start(bf16[1344,128]{1,0:T(8,128)(2,1)} %copy-done.9), channel_id=1, source_target_pairs={{0,12},{1,13},{2,14},{3,15},{4,0},{5,1},{6,2},{7,3},{8,4},{9,5},{1... | collective-permute-start | bytes 1032200 | tf_op jit(solution)/shard_map/ppermute | solution.py:276
  94.6 0.7 copy-start.1
  96.2 0.7 copy-start.4
  99.6 1.0 copy-start.2
  100.5 1.0 copy-start.5
  103.1 6.0 %collective-permute-start.6 = (bf16[4,3,160,128]{3,2,1,0:T(8,128)(2,1)S(1)}, bf16[4,3,160,128]{3,2,1,0:T(8,128)(2,1)S(1)}, u32[]{:S(2)}, u32[]{:S(2)}) collective-permute-start(bf16[4,3,160,128]{3,2,1,0:T(8,128)(2,1)S(1)} %get-tuple-element.33), channel_id=1, source_target_pairs={{0,16},{16,0},{32,48},{48,32},{64,80},{80,64},{96,112},{112,96},{1... | collective-permute-start | bytes 1474568 | tf_op jit(solution)/shard_map/ppermute | solution.py:299
  121.6 13.3 %copy-start.3 = (bf16[1344,128]{1,0:T(8,128)(2,1)S(1)}, bf16[1344,128]{1,0:T(8,128)(2,1)}, u32[]{:S(2)}) copy-start(bf16[1344,128]{1,0:T(8,128)(2,1)} %copy-done.1) | copy-start | bytes 1032196
  121.6 13.3 %copy-start.6 = (bf16[1344,128]{1,0:T(8,128)(2,1)S(1)}, bf16[1344,128]{1,0:T(8,128)(2,1)}, u32[]{:S(2)}) copy-start(bf16[1344,128]{1,0:T(8,128)(2,1)} %copy-done.4) | copy-start | bytes 1032196
  135.8 60.3 %copy-start.7 = (f32[5,64,16]{2,1,0:T(8,128)S(1)}, f32[5,64,16]{2,1,0:T(8,128)}, u32[]{:S(2)}) copy-start(f32[5,64,16]{2,1,0:T(8,128)} %get-tuple-element.34.picks_ref) | copy-start | bytes 61444

commit v6 on v5

--- a/solution.py
+++ b/solution.py
@@ -1,3 +1,5 @@
+import functools
+
 import jax
 import jax.numpy as jnp
 from jax import lax
@@ -148,49 +150,50 @@
     return None
 
 
-def spread_kernel(inputs_ref, grads_ref, out_ref):
-    groups = inputs_ref.shape[0]
-    half = out_ref.shape[3]
-    for which, ref in enumerate((inputs_ref, grads_ref)):
-        for s in range(out_ref.shape[2] // groups):
-            block = ref[:, s * half : (s + 1) * half]
-            for x in range(SIDE):
-                out_ref[x, which, pl.ds(s * groups, groups), :] = block
-
-
-def forward_kernel(x_ref, own, ahead, behind, far_low, far_high, keep_ref, send_ref):
-    share = x_ref.shape[3]
-    quarter = SIDE * share
+def forward_kernel(keep, x_ref, own, ahead, behind, far_low, far_high, out_ref):
+    quarter = 2 * far_low.shape[0] // 3
     lanes = own.shape[1]
-    rows = keep_ref.shape[2]
+    share = quarter // SIDE
+    groups = x_ref.shape[2] // 2
+    capacity = out_ref.shape[2] // groups
     mine = lax.axis_index("etp") // SIDE
     core = lax.rem(lax.axis_index("ep"), 2)
+    side = core if keep else 1 - core
+    here = pl.ds(pl.multiple_of(side * groups, groups), groups)
+
+    def rows(x, which):
+        return jnp.concatenate(
+            [x_ref[x, which, here, s * share : (s + 1) * share] for s in range(capacity)], axis=0
+        )
+
+    inputs = [rows(x, 0) for x in range(SIDE)]
+    grads = [rows(x, 1) for x in range(SIDE)]
     for step, w in zip(STEPS, ((own,), (ahead,), (behind,), (far_low, far_high))):
         place = lax.rem(mine + step, SIDE)
         down = jnp.concatenate(
             [rows_of(w, 2 * quarter + j * lanes, lanes) for j in range(quarter // lanes)], axis=1
         )
-        for out_ref, side in ((keep_ref, core), (send_ref, 1 - core)):
-            here = pl.ds(pl.multiple_of(side * rows, 32), rows)
-            both = None
-            hidden = None
-            for x in range(SIDE):
-                pair = jnp.concatenate(
-                    [rows_of(w, x * share, share), rows_of(w, quarter + x * share, share)],
-                    axis=1,
-                )
-                one = mm(x_ref[x, 0, here, :], pair, NN)
-                two = mm(x_ref[x, 1, here, :], down[:, x * share : (x + 1) * share], NT)
-                both = one if both is None else both + one
-                hidden = two if hidden is None else hidden + two
-            out_ref[place, 0] = both[:, :lanes].astype(out_ref.dtype)
-            out_ref[place, 1] = both[:, lanes:].astype(out_ref.dtype)
-            out_ref[place, 2] = hidden.astype(out_ref.dtype)
+        both = None
+        hidden = None
+        for x in range(SIDE):
+            pair = jnp.concatenate(
+                [rows_of(w, x * share, share), rows_of(w, quarter + x * share, share)],
+                axis=1,
+            )
+            one = mm(inputs[x], pair, NN)
+            two = mm(grads[x], down[:, x * share : (x + 1) * share], NT)
+            both = one if both is None else both + one
+            hidden = two if hidden is None else hidden + two
+        out_ref[place, 0] = both[:, :lanes].astype(out_ref.dtype)
+        out_ref[place, 1] = both[:, lanes:].astype(out_ref.dtype)
+        out_ref[place, 2] = hidden.astype(out_ref.dtype)
 
 
 def backward_kernel(d_ref, own, ahead, behind, far_low, far_high, out_ref):
-    share = out_ref.shape[2]
-    quarter = SIDE * share
+    quarter = 2 * far_low.shape[0] // 3
+    share = quarter // SIDE
+    groups = out_ref.shape[1] // 2
+    rows = d_ref.shape[3]
     mine = lax.axis_index("etp") // SIDE
     grads = []
     for step in STEPS:
@@ -204,6 +207,7 @@
                 axis=0,
             )
         )
+    fill = jnp.zeros((groups, out_ref.shape[2] - rows // groups * share), jnp.float32)
     for x in range(SIDE):
         total = None
         for grad, w in zip(grads, ((own,), (ahead,), (behind,), (far_low, far_high))):
@@ -212,23 +216,22 @@
             )
             one = mm(grad, pair, NT)
             total = one if total is None else total + one
-        out_ref[x] = total.astype(out_ref.dtype)
+        for side in range(2):
+            blocks = [
+                total[side * rows + s * groups : side * rows + (s + 1) * groups]
+                for s in range(rows // groups)
+            ]
+            line = jnp.concatenate([*blocks, fill], axis=1)
+            out_ref[x, pl.ds(side * groups, groups), :] = line.astype(out_ref.dtype)
 
 
 def gather_kernel(parts_ref, out_ref):
-    groups = out_ref.shape[0]
     width = out_ref.shape[2]
-    half = parts_ref.shape[2]
-    capacity = parts_ref.shape[1] // groups
-    blocks = []
-    for s in range(capacity):
-        here = pl.ds(s * groups, groups)
-        total = parts_ref[0, here, :].astype(jnp.float32)
-        for x in range(1, SIDE):
-            total = total + parts_ref[x, here, :].astype(jnp.float32)
-        blocks.append(total)
-    blocks.append(jnp.zeros((groups, 2 * width - capacity * half), jnp.float32))
-    line = jnp.concatenate(blocks, axis=1).astype(out_ref.dtype)
+    total = parts_ref[0].astype(jnp.float32)
+    for x in range(1, SIDE):
+        total = total + parts_ref[x].astype(jnp.float32)
+    fill = jnp.zeros((total.shape[0], 2 * width - total.shape[1]), jnp.float32)
+    line = jnp.concatenate([total, fill], axis=1).astype(out_ref.dtype)
     out_ref[:, 0, :] = line[:, :width]
     out_ref[:, 1, :] = line[:, width:]
 
@@ -279,24 +282,25 @@
         own,
         shift(to_behind, -1),
         shift(to_ahead, 1),
-        shift(to_far_low, 1),
-        shift(to_far_high, -1),
+        shift(shift(to_far_low, 1), 1),
+        shift(shift(to_far_high, -1), -1),
     ]
 
     came = lax.all_to_all(sent, "ep", split_axis=0, concat_axis=0, tiled=True)
     came, *weights = lax.optimization_barrier((came, *weights))
-    weights[3:] = [shift(weights[3], 1), shift(weights[4], -1)]
-    (wide,) = in_vmem(
-        spread_kernel, [((SIDE, 2, rows_all, half), bf16)], 2, 0, "spread_rows"
-    )(came[:, 0], came[:, 1])
+    wide = jnp.broadcast_to(came[None], (SIDE, *came.shape))
     gathered = lax.all_to_all(wide, "etp", 0, 0, tiled=True, axis_index_groups=along_x)
+    gathered = jnp.swapaxes(gathered, 1, 2)
 
     flops = 2 * 3 * rows_all * quarter * lanes * SIDE
     part = (SIDE, 3, rows_all // 2, lanes)
-    keep, send = in_vmem(
-        forward_kernel, [(part, jnp.float32), (part, bf16)], 6, flops, "forward_parts"
+    (send,) = in_vmem(
+        functools.partial(forward_kernel, False), [(part, bf16)], 6, flops // 2, "forward_send"
     )(gathered, *weights)
     other = lax.ppermute(send, "ep", [(i, i ^ 1) for i in range(ep_count)])
+    (keep,) = in_vmem(
+        functools.partial(forward_kernel, True), [(part, jnp.float32)], 6, flops // 2, "forward_keep"
+    )(gathered, *weights)
     partial = (keep + other.astype(jnp.float32)).astype(bf16)
     partial = lax.all_to_all(partial, "etp", 0, 0, tiled=True, axis_index_groups=along_y)
     pre_gate, pre_up, d_hidden = jnp.sum(partial.astype(jnp.float32), axis=0)
@@ -307,7 +311,7 @@
     grads = lax.all_to_all(grads, "etp", 0, 0, tiled=True, axis_index_groups=along_y)
     grads = lax.all_gather(grads, "ep", axis_index_groups=cores)
     (back,) = in_vmem(
-        backward_kernel, [((SIDE, rows_all, half), bf16)], 6, flops * 2 // 3, "backward_parts"
+        backward_kernel, [((SIDE, ep_count, line), bf16)], 6, flops * 2 // 3, "backward_parts"
     )(grads, *weights)
     back = lax.all_to_all(back, "etp", 0, 0, tiled=True, axis_index_groups=along_x)
     (summed,) = in_vmem(gather_kernel, [((ep_count, 2, back_line // 2), bf16)], 1, 0, "gather_rows")(back)

time: 198 us -> 196 us (0.990)
  blocking collectives: 85.5 us -> 108 us
  waiting for transfers between devices: 36.9 us -> 23.4 us
  starting transfers between devices: 58.7 us -> 53.3 us
  local copies, waits for them, and re-layouts: 4.42 us -> 0.25 us
    all_to_all x0 -> x1, blocking collectives: none -> 18.8 us  [on_device(): lax.all_to_all(wide, 'etp', 0, 0, tiled=True, axis_index_groups=along_x)]
    ppermute x6, waiting for transfers between devices: 24.1 us -> 17.9 us  [shift(): return lax.ppermute(block, 'etp', pairs)]
    all_to_all x1, blocking collectives: 46.9 us -> 51.9 us  [on_device(): lax.all_to_all(summed, 'ep', split_axis=0, concat_axis=0, tiled=True)]
    unnamed x21 -> x5, local copies, waits for them, and re-layouts: 4.32 us -> 0.03 us
    all_to_all x1 -> x0, starting transfers between devices: 4.14 us -> none  [on_device(): lax.all_to_all(wide, 'etp', 0, 0, tiled=True, axis_index_groups=along_x)]
    all_to_all x1, waiting for transfers between devices: 8.78 us -> 4.92 us  [on_device(): came = lax.all_to_all(sent, 'ep', split_axis=0, concat_axis=0, tiled=True)]
    all_to_all x1 -> x0, waiting for transfers between devices: 2.61 us -> none  [on_device(): lax.all_to_all(wide, 'etp', 0, 0, tiled=True, axis_index_groups=along_x)]
  transfers between devices with their start and end apart: 9 -> 8, of which waited for: 6 -> 4; matrix products, arithmetic and copies ran while one was open for 0% -> 0% of each run, Pallas kernels for 2% -> 2%
where the time goes in v6:
time: 196 us
  blocking collectives  108 us (55%)
  starting transfers between devices  53.3 us (27%)
  waiting for transfers between devices  23.4 us (12%)
  Pallas kernels  10.2 us (5%)
    all_to_all x1, blocking collectives, on_device(): lax.all_to_all(summed, 'ep', split_axis=0, concat_axis=0, tiled=True)  51.9 us
    all_to_all x1, starting transfers between devices, on_device(): came = lax.all_to_all(sent, 'ep', split_axis=0, concat_axis=0, tiled=True)  30.4 us
    all_to_all x1, blocking collectives, on_device(): lax.all_to_all(wide, 'etp', 0, 0, tiled=True, axis_index_groups=along_x)  18.8 us
    ppermute x6, starting transfers between devices, shift(): return lax.ppermute(block, 'etp', pairs)  18.3 us
    ppermute x6, waiting for transfers between devices, shift(): return lax.ppermute(block, 'etp', pairs)  17.9 us
    all_to_all x1, blocking collectives, on_device(): lax.all_to_all(partial, 'etp', 0, 0, tiled=True, axis_index_groups=along_y)  12.3 us
    all_to_all x1, blocking collectives, on_device(): lax.all_to_all(back, 'etp', 0, 0, tiled=True, axis_index_groups=along_x)  12.1 us
    all_to_all x1, blocking collectives, on_device(): lax.all_to_all(grads, 'etp', 0, 0, tiled=True, axis_index_groups=along_y)  8.25 us
  transfers between devices with their start and end apart: 8, of which 4 were waited for; matrix products, arithmetic and copies ran while one was open for 0% of the time, Pallas kernels for 2%

profile of v6, /device:TPU:1, one launch (start us, length us, event | category | flops | bytes accessed | tf_op | source)
XLA Modules:
  0.0 195.6 jit_solution(12155806611267327191)
XLA Ops:
  0.0 2.6 %dispatch_rows.1 = (bf16[64,2,1152]{2,1,0:T(2,128)(2,1)}, f32[5,64,16]{2,1,0:T(8,128)}) custom-call(s32[8,16]{1,0:T(8,128)} %bitcast.17, f32[8,16]{1,0:T(8,128)} %bitcast.18, bf16[16,448]{1,0:T(8,128)(2,1)} %tokens_any.1, bf16[16,448]{1,0:T(8,128)(2,1)} %grads_any.1), custom_call_target="tpu_custom_call" | custom-call | bytes 500000 | tf_op jit(solution)/shard_map/dispatch_rows/pallas_call | solution.py:127
  2.6 30.4 %all-to-all-start = ((bf16[64,2,1152]{2,1,0:T(2,128)(2,1)}), bf16[64,2,1152]{2,1,0:T(2,128)(2,1)S(1)}, u32[]{:S(2)}, u32[]{:S(2)}) async-start(bf16[64,2,1152]{2,1,0:T(2,128)(2,1)} %get-tuple-element.18), calls=%async_computation | async-start | bytes 589824 | tf_op jit(solution)/shard_map/all_to_all | solution.py:289
  33.0 3.6 %pack_weights.1 = (bf16[2688,128]{1,0:T(8,128)(2,1)}, bf16[2688,128]{1,0:T(8,128)(2,1)}, bf16[2688,128]{1,0:T(8,128)(2,1)}, bf16[1344,128]{1,0:T(8,128)(2,1)}, bf16[1344,128]{1,0:T(8,128)(2,1)}) custom-call(bf16[3584,128]{1,0:T(8,128)(2,1)} %bitcast.13, bf16[3584,128]{1,0:T(8,128)(2,1)} %bitcast.14, bf16[128,3584]{1,0:T(8,128)(2,1)} %bitcast.15), custom_call_target="tpu_custom_call" | custom-call | bytes 6000000 | tf_op jit(solution)/shard_map/pack_weights/pallas_call | solution.py:70
  36.6 3.2 %collective-permute-start.2 = (bf16[1344,128]{1,0:T(8,128)(2,1)}, bf16[1344,128]{1,0:T(8,128)(2,1)S(1)}, u32[]{:S(2)}, u32[]{:S(2)}) collective-permute-start(bf16[1344,128]{1,0:T(8,128)(2,1)} %get-tuple-element.22), channel_id=1, source_target_pairs={{0,4},{1,5},{2,6},{3,7},{4,8},{5,9},{6,10},{7,11},{8,12},{9,13},{1... | collective-permute-start | bytes 1032200 | tf_op jit(solution)/shard_map/ppermute | solution.py:279
  39.8 3.4 %collective-permute-start.4 = (bf16[1344,128]{1,0:T(8,128)(2,1)}, bf16[1344,128]{1,0:T(8,128)(2,1)S(1)}, u32[]{:S(2)}, u32[]{:S(2)}) collective-permute-start(bf16[1344,128]{1,0:T(8,128)(2,1)} %get-tuple-element.23), channel_id=1, source_target_pairs={{0,12},{1,13},{2,14},{3,15},{4,0},{5,1},{6,2},{7,3},{8,4},{9,5},{1... | collective-permute-start | bytes 1032200 | tf_op jit(solution)/shard_map/ppermute | solution.py:279
  43.2 3.4 %collective-permute-start = (bf16[2688,128]{1,0:T(8,128)(2,1)}, bf16[2688,128]{1,0:T(8,128)(2,1)S(1)}, u32[]{:S(2)}, u32[]{:S(2)}) collective-permute-start(bf16[2688,128]{1,0:T(8,128)(2,1)} %get-tuple-element.20), channel_id=1, source_target_pairs={{0,12},{1,13},{2,14},{3,15},{4,0},{5,1},{6,2},{7,3},{8,4},{9,5},{1... | collective-permute-start | bytes 2064392 | tf_op jit(solution)/shard_map/ppermute | solution.py:279
  46.6 1.9 collective-permute-start.1
  48.5 0.8 collective-permute-done.2
  49.3 1.9 collective-permute-start.3
  51.2 0.0 collective-permute-done.4
  51.2 4.6 %collective-permute-start.5 = (bf16[1344,128]{1,0:T(8,128)(2,1)S(1)}, bf16[1344,128]{1,0:T(8,128)(2,1)S(1)}, u32[]{:S(2)}, u32[]{:S(2)}) collective-permute-start(bf16[1344,128]{1,0:T(8,128)(2,1)S(1)} %collective-permute-done.4), channel_id=1, source_target_pairs={{0,12},{1,13},{2,14},{3,15},{4,0},{5,1},{6,2},{7,3},{8,4},{9,5},{1... | collective-permute-start | bytes 1032200 | tf_op jit(solution)/shard_map/ppermute | solution.py:279
  55.8 17.1 %collective-permute-done.3.far_low = bf16[1344,128]{1,0:T(8,128)(2,1)S(1)} collective-permute-done((bf16[1344,128]{1,0:T(8,128)(2,1)S(1)}, bf16[1344,128]{1,0:T(8,128)(2,1)S(1)}, u32[]{:S(2)}, u32[]{:S(2)}) %collective-permute-start.3) | collective-permute-done | bytes 344096 | tf_op jit(solution)/shard_map/ppermute | solution.py:279
  72.9 0.0 collective-permute-done.5.far_high
  72.9 0.0 collective-permute-done.ahead
  72.9 0.0 collective-permute-done.1.behind
  72.9 4.9 %all-to-all-done = bf16[64,2,1152]{2,1,0:T(2,128)(2,1)S(1)} async-done(((bf16[64,2,1152]{2,1,0:T(2,128)(2,1)}), bf16[64,2,1152]{2,1,0:T(2,128)(2,1)S(1)}, u32[]{:S(2)}, u32[]{:S(2)}) %all-to-all-start) | async-done | bytes 294944 | tf_op jit(solution)/shard_map/all_to_all | solution.py:289
  77.9 0.1 broadcast_in_dim.4
  78.0 0.0 copy-start
  78.1 18.8 %all_to_all.30 = bf16[4,64,2,1152]{3,1,2,0:T(8,128)(2,1)S(1)} all-to-all(bf16[4,64,2,1152]{3,1,2,0:T(8,128)(2,1)S(1)} %broadcast_in_dim.4), channel_id=1, replica_groups={{0,1,2,3},{4,5,6,7},{8,9,10,11},{12,13,14,15},{16,17,18,19},{20,21,22,2..., dimensions={0} | all-to-all | bytes 2359296 | tf_op jit(solution)/shard_map/all_to_all | solution.py:292
  96.8 0.0 copy-done
  96.8 0.9 forward_send.1
  97.8 4.5 %collective-permute-start.6 = (bf16[4,3,160,128]{3,2,1,0:T(8,128)(2,1)S(1)}, bf16[4,3,160,128]{3,2,1,0:T(8,128)(2,1)S(1)}, u32[]{:S(2)}, u32[]{:S(2)}) collective-permute-start(bf16[4,3,160,128]{3,2,1,0:T(8,128)(2,1)S(1)} %forward_send.1), channel_id=1, source_target_pairs={{0,16},{16,0},{32,48},{48,32},{64,80},{80,64},{96,112},{112,96},{1... | collective-permute-start | bytes 1474568 | tf_op jit(solution)/shard_map/ppermute | solution.py:300
  102.3 0.9 forward_keep.1
  103.3 0.5 collective-permute-done.6
  103.8 0.1 add_convert_fusion
  103.9 12.3 %all_to_all.31 = bf16[4,3,160,128]{3,2,1,0:T(8,128)(2,1)S(1)} all-to-all(bf16[4,3,160,128]{3,2,1,0:T(8,128)(2,1)S(1)} %add_convert_fusion), channel_id=1, replica_groups={{0,4,8,12},{1,5,9,13},{2,6,10,14},{3,7,11,15},{16,20,24,28},{17,21,25,2..., dimensions={0} | all-to-all | bytes 983040 | tf_op jit(solution)/shard_map/all_to_all | solution.py:305
  116.2 0.1 convert_reduce_fusion
  116.3 0.1 fusion.2
  116.4 8.3 %all_to_all.32 = bf16[4,2,160,128]{3,2,1,0:T(8,128)(2,1)S(1)} all-to-all(bf16[4,2,160,128]{3,2,1,0:T(8,128)(2,1)S(1)} %broadcast_in_dim.5), channel_id=1, replica_groups={{0,4,8,12},{1,5,9,13},{2,6,10,14},{3,7,11,15},{16,20,24,28},{17,21,25,2..., dimensions={0} | all-to-all | bytes 655360 | tf_op jit(solution)/shard_map/all_to_all | solution.py:311
  124.7 4.8 %all-gather = bf16[8,2,160,128]{3,2,1,0:T(8,128)(2,1)S(1)} all-gather(bf16[4,2,160,128]{3,2,1,0:T(8,128)(2,1)S(1)} %all_to_all.32), channel_id=2, replica_groups={{0,16},{32,48},{64,80},{96,112},{128,144},{160,176},{192,208},{224,240}..., dimensions={0}, use_global_device_ids=true | all-gather | bytes 983040 | tf_op jit(solution)/shard_map/all_gather | solution.py:312
  129.5 0.9 backward_parts.1
  130.4 0.0 copy-start.1
  130.4 12.1 %all_to_all.33.parts_ref = bf16[4,64,1152]{2,1,0:T(8,128)(2,1)S(1)} all-to-all(bf16[4,64,1152]{2,1,0:T(8,128)(2,1)S(1)} %backward_parts.1), channel_id=1, replica_groups={{0,1,2,3},{4,5,6,7},{8,9,10,11},{12,13,14,15},{16,17,18,19},{20,21,22,2..., dimensions={0} | all-to-all | bytes 1179648 | tf_op jit(solution)/shard_map/all_to_all | solution.py:316
  142.5 0.2 gather_rows.1
  142.7 51.9 %all_to_all.34 = bf16[64,2,640]{2,1,0:T(2,128)(2,1)S(1)} all-to-all(bf16[64,2,640]{2,1,0:T(2,128)(2,1)S(1)} %gather_rows.1), channel_id=1, replica_groups=mesh['ep'=64,'etp'=16] {'ep'}, dimensions={0} | all-to-all | bytes 327680 | tf_op jit(solution)/shard_map/all_to_all | solution.py:318
  194.6 0.0 copy-done.1
  194.7 0.9 combine_rows.1
  (4 shorter events, 0.1 us)
Async XLA Ops:
  2.6 75.3 %all-to-all-start = ((bf16[64,2,1152]{2,1,0:T(2,128)(2,1)}), bf16[64,2,1152]{2,1,0:T(2,128)(2,1)S(1)}, u32[]{:S(2)}, u32[]{:S(2)}) async-start(bf16[64,2,1152]{2,1,0:T(2,128)(2,1)} %get-tuple-element.18), calls=%async_computation | async-start | bytes 589824 | tf_op jit(solution)/shard_map/all_to_all | solution.py:289
  36.6 12.6 %collective-permute-start.2 = (bf16[1344,128]{1,0:T(8,128)(2,1)}, bf16[1344,128]{1,0:T(8,128)(2,1)S(1)}, u32[]{:S(2)}, u32[]{:S(2)}) collective-permute-start(bf16[1344,128]{1,0:T(8,128)(2,1)} %get-tuple-element.22), channel_id=1, source_target_pairs={{0,4},{1,5},{2,6},{3,7},{4,8},{5,9},{6,10},{7,11},{8,12},{9,13},{1... | collective-permute-start | bytes 1032200 | tf_op jit(solution)/shard_map/ppermute | solution.py:279
  39.8 11.3 %collective-permute-start.4 = (bf16[1344,128]{1,0:T(8,128)(2,1)}, bf16[1344,128]{1,0:T(8,128)(2,1)S(1)}, u32[]{:S(2)}, u32[]{:S(2)}) collective-permute-start(bf16[1344,128]{1,0:T(8,128)(2,1)} %get-tuple-element.23), channel_id=1, source_target_pairs={{0,12},{1,13},{2,14},{3,15},{4,0},{5,1},{6,2},{7,3},{8,4},{9,5},{1... | collective-permute-start | bytes 1032200 | tf_op jit(solution)/shard_map/ppermute | solution.py:279
  43.2 29.7 %collective-permute-start = (bf16[2688,128]{1,0:T(8,128)(2,1)}, bf16[2688,128]{1,0:T(8,128)(2,1)S(1)}, u32[]{:S(2)}, u32[]{:S(2)}) collective-permute-start(bf16[2688,128]{1,0:T(8,128)(2,1)} %get-tuple-element.20), channel_id=1, source_target_pairs={{0,12},{1,13},{2,14},{3,15},{4,0},{5,1},{6,2},{7,3},{8,4},{9,5},{1... | collective-permute-start | bytes 2064392 | tf_op jit(solution)/shard_map/ppermute | solution.py:279
  46.6 26.4 %collective-permute-start.1 = (bf16[2688,128]{1,0:T(8,128)(2,1)}, bf16[2688,128]{1,0:T(8,128)(2,1)S(1)}, u32[]{:S(2)}, u32[]{:S(2)}) collective-permute-start(bf16[2688,128]{1,0:T(8,128)(2,1)} %get-tuple-element.21), channel_id=1, source_target_pairs={{0,4},{1,5},{2,6},{3,7},{4,8},{5,9},{6,10},{7,11},{8,12},{9,13},{1... | collective-permute-start | bytes 2064392 | tf_op jit(solution)/shard_map/ppermute | solution.py:279
  49.3 23.6 %collective-permute-start.3 = (bf16[1344,128]{1,0:T(8,128)(2,1)S(1)}, bf16[1344,128]{1,0:T(8,128)(2,1)S(1)}, u32[]{:S(2)}, u32[]{:S(2)}) collective-permute-start(bf16[1344,128]{1,0:T(8,128)(2,1)S(1)} %collective-permute-done.2), channel_id=1, source_target_pairs={{0,4},{1,5},{2,6},{3,7},{4,8},{5,9},{6,10},{7,11},{8,12},{9,13},{1... | collective-permute-start | bytes 1032200 | tf_op jit(solution)/shard_map/ppermute | solution.py:279
  51.2 21.7 %collective-permute-start.5 = (bf16[1344,128]{1,0:T(8,128)(2,1)S(1)}, bf16[1344,128]{1,0:T(8,128)(2,1)S(1)}, u32[]{:S(2)}, u32[]{:S(2)}) collective-permute-start(bf16[1344,128]{1,0:T(8,128)(2,1)S(1)} %collective-permute-done.4), channel_id=1, source_target_pairs={{0,12},{1,13},{2,14},{3,15},{4,0},{5,1},{6,2},{7,3},{8,4},{9,5},{1... | collective-permute-start | bytes 1032200 | tf_op jit(solution)/shard_map/ppermute | solution.py:279
  78.0 18.8 %copy-start = (bf16[2688,128]{1,0:T(8,128)(2,1)S(1)}, bf16[2688,128]{1,0:T(8,128)(2,1)}, u32[]{:S(2)}) copy-start(bf16[2688,128]{1,0:T(8,128)(2,1)} %get-tuple-element.25.own) | copy-start | bytes 2064388
  97.8 6.0 %collective-permute-start.6 = (bf16[4,3,160,128]{3,2,1,0:T(8,128)(2,1)S(1)}, bf16[4,3,160,128]{3,2,1,0:T(8,128)(2,1)S(1)}, u32[]{:S(2)}, u32[]{:S(2)}) collective-permute-start(bf16[4,3,160,128]{3,2,1,0:T(8,128)(2,1)S(1)} %forward_send.1), channel_id=1, source_target_pairs={{0,16},{16,0},{32,48},{48,32},{64,80},{80,64},{96,112},{112,96},{1... | collective-permute-start | bytes 1474568 | tf_op jit(solution)/shard_map/ppermute | solution.py:300
  130.4 64.3 %copy-start.1 = (f32[5,64,16]{2,1,0:T(8,128)S(1)}, f32[5,64,16]{2,1,0:T(8,128)}, u32[]{:S(2)}) copy-start(f32[5,64,16]{2,1,0:T(8,128)} %get-tuple-element.30.picks_ref) | copy-start | bytes 61444

commit v7 on v6

--- a/solution.py
+++ b/solution.py
@@ -32,7 +32,8 @@
     )
 
 
-def pack_kernel(gate_any, up_any, down_any, own, ahead, behind, far_low, far_high, sems):
+def pack_kernel(steps, gate_any, up_any, down_any, *rest):
+    outs, sems = list(rest[:-1]), rest[-1]
     quarter = gate_any.shape[0] // SIDE
     lanes = gate_any.shape[1]
     mine = lax.axis_index("etp") // SIDE
@@ -43,14 +44,16 @@
         copy.start()
         copies.append(copy)
 
-    for step, into in ((2, (far_low, far_high)), (1, (ahead,)), (3, (behind,)), (0, (own,))):
+    for step in steps:
+        into = [outs.pop(0)]
         first = pl.multiple_of(lax.rem(mine + step, SIDE) * quarter, lanes)
         cut = into[0].shape[0] - quarter
         go(gate_any.at[pl.ds(first, quarter)], into[0].at[pl.ds(0, quarter)])
-        if len(into) == 1:
+        if cut == 2 * quarter:
             go(up_any.at[pl.ds(first, quarter)], into[0].at[pl.ds(quarter, quarter)])
             base = 2 * quarter
         else:
+            into.append(outs.pop(0))
             go(up_any.at[pl.ds(first, cut)], into[0].at[pl.ds(quarter, cut)])
             go(up_any.at[pl.ds(first + cut, quarter - cut)], into[1].at[pl.ds(0, quarter - cut)])
             base = quarter - cut
@@ -61,21 +64,18 @@
         copy.wait()
 
 
-def pack_weights(gate, up, down):
-    quarter = gate.shape[0] // SIDE
+def pack_weights(steps, sizes, gate, up, down):
     lanes = gate.shape[1]
-    whole = jax.ShapeDtypeStruct((3 * quarter, lanes), gate.dtype)
-    part = jax.ShapeDtypeStruct((3 * quarter // 2, lanes), gate.dtype)
-    shapes = [whole, whole, whole, part, part]
+    count = len(steps) * (2 + gate.shape[0] // SIDE // lanes) + len(sizes) - len(steps)
     return pl.pallas_call(
-        pack_kernel,
-        out_shape=shapes,
+        functools.partial(pack_kernel, steps),
+        out_shape=[jax.ShapeDtypeStruct((size, lanes), gate.dtype) for size in sizes],
         in_specs=[pl.BlockSpec(memory_space=pl.ANY)] * 3,
-        out_specs=[pl.BlockSpec(memory_space=pltpu.VMEM)] * len(shapes),
-        scratch_shapes=[pltpu.SemaphoreType.DMA((SIDE * (2 + quarter // lanes) + 1,))],
+        out_specs=[pl.BlockSpec(memory_space=pltpu.VMEM)] * len(sizes),
+        scratch_shapes=[pltpu.SemaphoreType.DMA((count,))],
         compiler_params=pltpu.CompilerParams(vmem_limit_bytes=60 * 1024 * 1024),
-        cost_estimate=pl.CostEstimate(flops=0, bytes_accessed=6_000_000, transcendentals=0),
-        name="pack_weights",
+        cost_estimate=pl.CostEstimate(flops=0, bytes_accessed=3_000_000, transcendentals=0),
+        name="pack_far" if len(sizes) > len(steps) else "pack_near",
     )(gate, up, down)
 
 
@@ -151,7 +151,7 @@
 
 
 def forward_kernel(keep, x_ref, own, ahead, behind, far_low, far_high, out_ref):
-    quarter = 2 * far_low.shape[0] // 3
+    quarter = own.shape[0] // 3
     lanes = own.shape[1]
     share = quarter // SIDE
     groups = x_ref.shape[2] // 2
@@ -190,7 +190,7 @@
 
 
 def backward_kernel(d_ref, own, ahead, behind, far_low, far_high, out_ref):
-    quarter = 2 * far_low.shape[0] // 3
+    quarter = own.shape[0] // 3
     share = quarter // SIDE
     groups = out_ref.shape[1] // 2
     rows = d_ref.shape[3]
@@ -268,9 +268,10 @@
     sent, picks = dispatch_rows(
         routes.T, route_gates.T, tokens, grad_out, capacity, ep_count, line
     )
-    own, to_ahead, to_behind, to_far_low, to_far_high = pack_weights(
-        gate_weight[0], up_weight[0], down_weight[0]
-    )
+    ours = (gate_weight[0], up_weight[0], down_weight[0])
+    low = quarter + quarter // 2
+    to_far_low, to_far_high = pack_weights((2,), (low, 3 * quarter - low), *ours)
+    to_ahead, to_behind, own = pack_weights((1, 3, 0), (3 * quarter,) * 3, *ours)
 
     def shift(block, step):
         pairs = [

time: 196 us -> 196 us (level)
    pallas_call x1 -> x2, Pallas kernels: 3.64 us -> 5.18 us  [pack_weights(): pl.pallas_call(functools.partial(pack_kernel, steps), out_shape=[jax.Shap...]
  transfers between devices with their start and end apart: 8 -> 8, of which waited for: 4 -> 3; matrix products, arithmetic and copies ran while one was open for 0% -> 0% of each run, Pallas kernels for 2% -> 3%
where the time goes in v7:
time: 196 us
  blocking collectives  108 us (55%)
  starting transfers between devices  53.3 us (27%)
  waiting for transfers between devices  21.8 us (11%)
  Pallas kernels  11.7 us (6%)
    all_to_all x1, blocking collectives, on_device(): lax.all_to_all(summed, 'ep', split_axis=0, concat_axis=0, tiled=True)  52.1 us
    all_to_all x1, starting transfers between devices, on_device(): came = lax.all_to_all(sent, 'ep', split_axis=0, concat_axis=0, tiled=True)  30.4 us
    all_to_all x1, blocking collectives, on_device(): lax.all_to_all(wide, 'etp', 0, 0, tiled=True, axis_index_groups=along_x)  18.8 us
    ppermute x6, starting transfers between devices, shift(): return lax.ppermute(block, 'etp', pairs)  18.3 us
    ppermute x6, waiting for transfers between devices, shift(): return lax.ppermute(block, 'etp', pairs)  17.9 us
    all_to_all x1, blocking collectives, on_device(): lax.all_to_all(partial, 'etp', 0, 0, tiled=True, axis_index_groups=along_y)  12.3 us
    all_to_all x1, blocking collectives, on_device(): lax.all_to_all(back, 'etp', 0, 0, tiled=True, axis_index_groups=along_x)  12.2 us
    all_to_all x1, blocking collectives, on_device(): lax.all_to_all(grads, 'etp', 0, 0, tiled=True, axis_index_groups=along_y)  8.25 us
  transfers between devices with their start and end apart: 8, of which 3 were waited for; matrix products, arithmetic and copies ran while one was open for 0% of the time, Pallas kernels for 3%

profile of v7, /device:TPU:1, one launch (start us, length us, event | category | flops | bytes accessed | tf_op | source)
XLA Modules:
  0.0 195.8 jit_solution(890263502588960056)
XLA Ops:
  0.0 2.6 %dispatch_rows.1 = (bf16[64,2,1152]{2,1,0:T(2,128)(2,1)}, f32[5,64,16]{2,1,0:T(8,128)}) custom-call(s32[8,16]{1,0:T(8,128)} %bitcast.20, f32[8,16]{1,0:T(8,128)} %bitcast.21, bf16[16,448]{1,0:T(8,128)(2,1)} %tokens_any.1, bf16[16,448]{1,0:T(8,128)(2,1)} %grads_any.1), custom_call_target="tpu_custom_call" | custom-call | bytes 500000 | tf_op jit(solution)/shard_map/dispatch_rows/pallas_call | solution.py:127
  2.6 30.4 %all-to-all-start = ((bf16[64,2,1152]{2,1,0:T(2,128)(2,1)}), bf16[64,2,1152]{2,1,0:T(2,128)(2,1)S(1)}, u32[]{:S(2)}, u32[]{:S(2)}) async-start(bf16[64,2,1152]{2,1,0:T(2,128)(2,1)} %get-tuple-element.18), calls=%async_computation | async-start | bytes 589824 | tf_op jit(solution)/shard_map/all_to_all | solution.py:290
  33.0 2.0 %pack_far.1 = (bf16[1344,128]{1,0:T(8,128)(2,1)}, bf16[1344,128]{1,0:T(8,128)(2,1)}) custom-call(bf16[3584,128]{1,0:T(8,128)(2,1)} %bitcast.13, bf16[3584,128]{1,0:T(8,128)(2,1)} %bitcast.15, bf16[128,3584]{1,0:T(8,128)(2,1)} %bitcast.17), custom_call_target="tpu_custom_call" | custom-call | bytes 3000000 | tf_op jit(solution)/shard_map/pack_far/pallas_call | solution.py:70
  35.0 3.2 %collective-permute-start.2 = (bf16[1344,128]{1,0:T(8,128)(2,1)}, bf16[1344,128]{1,0:T(8,128)(2,1)S(1)}, u32[]{:S(2)}, u32[]{:S(2)}) collective-permute-start(bf16[1344,128]{1,0:T(8,128)(2,1)} %get-tuple-element.22), channel_id=1, source_target_pairs={{0,4},{1,5},{2,6},{3,7},{4,8},{5,9},{6,10},{7,11},{8,12},{9,13},{1... | collective-permute-start | bytes 1032200 | tf_op jit(solution)/shard_map/ppermute | solution.py:280
  38.2 3.4 %collective-permute-start.4 = (bf16[1344,128]{1,0:T(8,128)(2,1)}, bf16[1344,128]{1,0:T(8,128)(2,1)S(1)}, u32[]{:S(2)}, u32[]{:S(2)}) collective-permute-start(bf16[1344,128]{1,0:T(8,128)(2,1)} %get-tuple-element.23), channel_id=1, source_target_pairs={{0,12},{1,13},{2,14},{3,15},{4,0},{5,1},{6,2},{7,3},{8,4},{9,5},{1... | collective-permute-start | bytes 1032200 | tf_op jit(solution)/shard_map/ppermute | solution.py:280
  41.6 3.1 %pack_near.1 = (bf16[2688,128]{1,0:T(8,128)(2,1)}, bf16[2688,128]{1,0:T(8,128)(2,1)}, bf16[2688,128]{1,0:T(8,128)(2,1)}) custom-call(bf16[3584,128]{1,0:T(8,128)(2,1)} %bitcast.14, bf16[3584,128]{1,0:T(8,128)(2,1)} %bitcast.16, bf16[128,3584]{1,0:T(8,128)(2,1)} %bitcast.18), custom_call_target="tpu_custom_call" | custom-call | bytes 3000000 | tf_op jit(solution)/shard_map/pack_near/pallas_call | solution.py:70
  44.8 3.4 %collective-permute-start = (bf16[2688,128]{1,0:T(8,128)(2,1)}, bf16[2688,128]{1,0:T(8,128)(2,1)S(1)}, u32[]{:S(2)}, u32[]{:S(2)}) collective-permute-start(bf16[2688,128]{1,0:T(8,128)(2,1)} %get-tuple-element.20), channel_id=1, source_target_pairs={{0,12},{1,13},{2,14},{3,15},{4,0},{5,1},{6,2},{7,3},{8,4},{9,5},{1... | collective-permute-start | bytes 2064392 | tf_op jit(solution)/shard_map/ppermute | solution.py:280
  48.1 1.9 collective-permute-start.1
  50.1 0.0 collective-permute-done.2
  50.1 1.9 collective-permute-start.3
  52.0 0.0 collective-permute-done.4
  52.0 4.6 %collective-permute-start.5 = (bf16[1344,128]{1,0:T(8,128)(2,1)S(1)}, bf16[1344,128]{1,0:T(8,128)(2,1)S(1)}, u32[]{:S(2)}, u32[]{:S(2)}) collective-permute-start(bf16[1344,128]{1,0:T(8,128)(2,1)S(1)} %collective-permute-done.4), channel_id=1, source_target_pairs={{0,12},{1,13},{2,14},{3,15},{4,0},{5,1},{6,2},{7,3},{8,4},{9,5},{1... | collective-permute-start | bytes 1032200 | tf_op jit(solution)/shard_map/ppermute | solution.py:280
  56.6 17.9 %collective-permute-done.3.far_low = bf16[1344,128]{1,0:T(8,128)(2,1)S(1)} collective-permute-done((bf16[1344,128]{1,0:T(8,128)(2,1)S(1)}, bf16[1344,128]{1,0:T(8,128)(2,1)S(1)}, u32[]{:S(2)}, u32[]{:S(2)}) %collective-permute-start.3) | collective-permute-done | bytes 344096 | tf_op jit(solution)/shard_map/ppermute | solution.py:280
  74.5 0.0 collective-permute-done.5.far_high
  74.5 0.0 collective-permute-done.ahead
  74.5 0.0 collective-permute-done.1.behind
  74.5 3.4 %all-to-all-done = bf16[64,2,1152]{2,1,0:T(2,128)(2,1)S(1)} async-done(((bf16[64,2,1152]{2,1,0:T(2,128)(2,1)}), bf16[64,2,1152]{2,1,0:T(2,128)(2,1)S(1)}, u32[]{:S(2)}, u32[]{:S(2)}) %all-to-all-start) | async-done | bytes 294944 | tf_op jit(solution)/shard_map/all_to_all | solution.py:290
  77.9 0.1 broadcast_in_dim.4
  78.1 0.0 copy-start
  78.1 18.8 %all_to_all.30 = bf16[4,64,2,1152]{3,1,2,0:T(8,128)(2,1)S(1)} all-to-all(bf16[4,64,2,1152]{3,1,2,0:T(8,128)(2,1)S(1)} %broadcast_in_dim.4), channel_id=1, replica_groups={{0,1,2,3},{4,5,6,7},{8,9,10,11},{12,13,14,15},{16,17,18,19},{20,21,22,2..., dimensions={0} | all-to-all | bytes 2359296 | tf_op jit(solution)/shard_map/all_to_all | solution.py:293
  96.8 0.0 copy-done
  96.9 0.9 forward_send.1
  97.8 4.5 %collective-permute-start.6 = (bf16[4,3,160,128]{3,2,1,0:T(8,128)(2,1)S(1)}, bf16[4,3,160,128]{3,2,1,0:T(8,128)(2,1)S(1)}, u32[]{:S(2)}, u32[]{:S(2)}) collective-permute-start(bf16[4,3,160,128]{3,2,1,0:T(8,128)(2,1)S(1)} %forward_send.1), channel_id=1, source_target_pairs={{0,16},{16,0},{32,48},{48,32},{64,80},{80,64},{96,112},{112,96},{1... | collective-permute-start | bytes 1474568 | tf_op jit(solution)/shard_map/ppermute | solution.py:301
  102.3 0.9 forward_keep.1
  103.3 0.5 collective-permute-done.6
  103.8 0.1 add_convert_fusion
  103.9 12.3 %all_to_all.31 = bf16[4,3,160,128]{3,2,1,0:T(8,128)(2,1)S(1)} all-to-all(bf16[4,3,160,128]{3,2,1,0:T(8,128)(2,1)S(1)} %add_convert_fusion), channel_id=1, replica_groups={{0,4,8,12},{1,5,9,13},{2,6,10,14},{3,7,11,15},{16,20,24,28},{17,21,25,2..., dimensions={0} | all-to-all | bytes 983040 | tf_op jit(solution)/shard_map/all_to_all | solution.py:306
  116.2 0.1 convert_reduce_fusion
  116.3 0.1 fusion.2
  116.4 8.3 %all_to_all.32 = bf16[4,2,160,128]{3,2,1,0:T(8,128)(2,1)S(1)} all-to-all(bf16[4,2,160,128]{3,2,1,0:T(8,128)(2,1)S(1)} %broadcast_in_dim.5), channel_id=1, replica_groups={{0,4,8,12},{1,5,9,13},{2,6,10,14},{3,7,11,15},{16,20,24,28},{17,21,25,2..., dimensions={0} | all-to-all | bytes 655360 | tf_op jit(solution)/shard_map/all_to_all | solution.py:312
  124.7 4.8 %all-gather = bf16[8,2,160,128]{3,2,1,0:T(8,128)(2,1)S(1)} all-gather(bf16[4,2,160,128]{3,2,1,0:T(8,128)(2,1)S(1)} %all_to_all.32), channel_id=2, replica_groups={{0,16},{32,48},{64,80},{96,112},{128,144},{160,176},{192,208},{224,240}..., dimensions={0}, use_global_device_ids=true | all-gather | bytes 983040 | tf_op jit(solution)/shard_map/all_gather | solution.py:313
  129.5 0.9 backward_parts.1
  130.4 0.0 copy-start.1
  130.4 12.2 %all_to_all.33.parts_ref = bf16[4,64,1152]{2,1,0:T(8,128)(2,1)S(1)} all-to-all(bf16[4,64,1152]{2,1,0:T(8,128)(2,1)S(1)} %backward_parts.1), channel_id=1, replica_groups={{0,1,2,3},{4,5,6,7},{8,9,10,11},{12,13,14,15},{16,17,18,19},{20,21,22,2..., dimensions={0} | all-to-all | bytes 1179648 | tf_op jit(solution)/shard_map/all_to_all | solution.py:317
  142.6 0.2 gather_rows.1
  142.8 52.1 %all_to_all.34 = bf16[64,2,640]{2,1,0:T(2,128)(2,1)S(1)} all-to-all(bf16[64,2,640]{2,1,0:T(2,128)(2,1)S(1)} %gather_rows.1), channel_id=1, replica_groups=mesh['ep'=64,'etp'=16] {'ep'}, dimensions={0} | all-to-all | bytes 327680 | tf_op jit(solution)/shard_map/all_to_all | solution.py:319
  194.8 0.0 copy-done.1
  194.9 0.9 combine_rows.1
  (4 shorter events, 0.1 us)
Async XLA Ops:
  2.6 75.3 %all-to-all-start = ((bf16[64,2,1152]{2,1,0:T(2,128)(2,1)}), bf16[64,2,1152]{2,1,0:T(2,128)(2,1)S(1)}, u32[]{:S(2)}, u32[]{:S(2)}) async-start(bf16[64,2,1152]{2,1,0:T(2,128)(2,1)} %get-tuple-element.18), calls=%async_computation | async-start | bytes 589824 | tf_op jit(solution)/shard_map/all_to_all | solution.py:290
  35.0 15.0 %collective-permute-start.2 = (bf16[1344,128]{1,0:T(8,128)(2,1)}, bf16[1344,128]{1,0:T(8,128)(2,1)S(1)}, u32[]{:S(2)}, u32[]{:S(2)}) collective-permute-start(bf16[1344,128]{1,0:T(8,128)(2,1)} %get-tuple-element.22), channel_id=1, source_target_pairs={{0,4},{1,5},{2,6},{3,7},{4,8},{5,9},{6,10},{7,11},{8,12},{9,13},{1... | collective-permute-start | bytes 1032200 | tf_op jit(solution)/shard_map/ppermute | solution.py:280
  38.2 13.8 %collective-permute-start.4 = (bf16[1344,128]{1,0:T(8,128)(2,1)}, bf16[1344,128]{1,0:T(8,128)(2,1)S(1)}, u32[]{:S(2)}, u32[]{:S(2)}) collective-permute-start(bf16[1344,128]{1,0:T(8,128)(2,1)} %get-tuple-element.23), channel_id=1, source_target_pairs={{0,12},{1,13},{2,14},{3,15},{4,0},{5,1},{6,2},{7,3},{8,4},{9,5},{1... | collective-permute-start | bytes 1032200 | tf_op jit(solution)/shard_map/ppermute | solution.py:280
  44.8 29.7 %collective-permute-start = (bf16[2688,128]{1,0:T(8,128)(2,1)}, bf16[2688,128]{1,0:T(8,128)(2,1)S(1)}, u32[]{:S(2)}, u32[]{:S(2)}) collective-permute-start(bf16[2688,128]{1,0:T(8,128)(2,1)} %get-tuple-element.20), channel_id=1, source_target_pairs={{0,12},{1,13},{2,14},{3,15},{4,0},{5,1},{6,2},{7,3},{8,4},{9,5},{1... | collective-permute-start | bytes 2064392 | tf_op jit(solution)/shard_map/ppermute | solution.py:280
  48.1 26.3 %collective-permute-start.1 = (bf16[2688,128]{1,0:T(8,128)(2,1)}, bf16[2688,128]{1,0:T(8,128)(2,1)S(1)}, u32[]{:S(2)}, u32[]{:S(2)}) collective-permute-start(bf16[2688,128]{1,0:T(8,128)(2,1)} %get-tuple-element.21), channel_id=1, source_target_pairs={{0,4},{1,5},{2,6},{3,7},{4,8},{5,9},{6,10},{7,11},{8,12},{9,13},{1... | collective-permute-start | bytes 2064392 | tf_op jit(solution)/shard_map/ppermute | solution.py:280
  50.1 24.4 %collective-permute-start.3 = (bf16[1344,128]{1,0:T(8,128)(2,1)S(1)}, bf16[1344,128]{1,0:T(8,128)(2,1)S(1)}, u32[]{:S(2)}, u32[]{:S(2)}) collective-permute-start(bf16[1344,128]{1,0:T(8,128)(2,1)S(1)} %collective-permute-done.2), channel_id=1, source_target_pairs={{0,4},{1,5},{2,6},{3,7},{4,8},{5,9},{6,10},{7,11},{8,12},{9,13},{1... | collective-permute-start | bytes 1032200 | tf_op jit(solution)/shard_map/ppermute | solution.py:280
  52.0 22.4 %collective-permute-start.5 = (bf16[1344,128]{1,0:T(8,128)(2,1)S(1)}, bf16[1344,128]{1,0:T(8,128)(2,1)S(1)}, u32[]{:S(2)}, u32[]{:S(2)}) collective-permute-start(bf16[1344,128]{1,0:T(8,128)(2,1)S(1)} %collective-permute-done.4), channel_id=1, source_target_pairs={{0,12},{1,13},{2,14},{3,15},{4,0},{5,1},{6,2},{7,3},{8,4},{9,5},{1... | collective-permute-start | bytes 1032200 | tf_op jit(solution)/shard_map/ppermute | solution.py:280
  78.1 18.8 %copy-start = (bf16[2688,128]{1,0:T(8,128)(2,1)S(1)}, bf16[2688,128]{1,0:T(8,128)(2,1)}, u32[]{:S(2)}) copy-start(bf16[2688,128]{1,0:T(8,128)(2,1)} %get-tuple-element.25.own) | copy-start | bytes 2064388
  97.8 6.0 %collective-permute-start.6 = (bf16[4,3,160,128]{3,2,1,0:T(8,128)(2,1)S(1)}, bf16[4,3,160,128]{3,2,1,0:T(8,128)(2,1)S(1)}, u32[]{:S(2)}, u32[]{:S(2)}) collective-permute-start(bf16[4,3,160,128]{3,2,1,0:T(8,128)(2,1)S(1)} %forward_send.1), channel_id=1, source_target_pairs={{0,16},{16,0},{32,48},{48,32},{64,80},{80,64},{96,112},{112,96},{1... | collective-permute-start | bytes 1474568 | tf_op jit(solution)/shard_map/ppermute | solution.py:301
  130.4 64.5 %copy-start.1 = (f32[5,64,16]{2,1,0:T(8,128)S(1)}, f32[5,64,16]{2,1,0:T(8,128)}, u32[]{:S(2)}) copy-start(f32[5,64,16]{2,1,0:T(8,128)} %get-tuple-element.30.picks_ref) | copy-start | bytes 61444

commit v8 on v7

--- a/solution.py
+++ b/solution.py
@@ -75,7 +75,7 @@
         scratch_shapes=[pltpu.SemaphoreType.DMA((count,))],
         compiler_params=pltpu.CompilerParams(vmem_limit_bytes=60 * 1024 * 1024),
         cost_estimate=pl.CostEstimate(flops=0, bytes_accessed=3_000_000, transcendentals=0),
-        name="pack_far" if len(sizes) > len(steps) else "pack_near",
+        name=f"pack_{steps[0]}",
     )(gate, up, down)
 
 
@@ -271,7 +271,8 @@
     ours = (gate_weight[0], up_weight[0], down_weight[0])
     low = quarter + quarter // 2
     to_far_low, to_far_high = pack_weights((2,), (low, 3 * quarter - low), *ours)
-    to_ahead, to_behind, own = pack_weights((1, 3, 0), (3 * quarter,) * 3, *ours)
+    to_ahead, to_behind = pack_weights((1, 3), (3 * quarter,) * 2, *ours)
+    (own,) = pack_weights((0,), (3 * quarter,), *ours)
 
     def shift(block, step):
         pairs = [

time: 196 us -> 196 us (level)
    ppermute x6, waiting for transfers between devices: 17.9 us -> 15.8 us  [shift(): return lax.ppermute(block, 'etp', pairs)]
    pallas_call x2 -> x3, Pallas kernels: 5.18 us -> 6.7 us  [pack_weights(): pl.pallas_call(functools.partial(pack_kernel, steps), out_shape=[jax.Shap...]
  transfers between devices with their start and end apart: 8 -> 8, of which waited for: 3 -> 3; matrix products, arithmetic and copies ran while one was open for 0% -> 0% of each run, Pallas kernels for 3% -> 4%
where the time goes in v8:
time: 196 us; the launch traced here: 195 us
  blocking collectives  108 us (55%)
  starting transfers between devices  53.3 us (27%)
  waiting for transfers between devices  20.3 us (10%)
  Pallas kernels  13.2 us (7%)
    all_to_all x1, blocking collectives, on_device(): lax.all_to_all(summed, 'ep', split_axis=0, concat_axis=0, tiled=True)  51.6 us
    all_to_all x1, starting transfers between devices, on_device(): came = lax.all_to_all(sent, 'ep', split_axis=0, concat_axis=0, tiled=True)  30.4 us
    all_to_all x1, blocking collectives, on_device(): lax.all_to_all(wide, 'etp', 0, 0, tiled=True, axis_index_groups=along_x)  18.8 us
    ppermute x6, starting transfers between devices, shift(): return lax.ppermute(block, 'etp', pairs)  18.3 us
    ppermute x6, waiting for transfers between devices, shift(): return lax.ppermute(block, 'etp', pairs)  15.8 us
    all_to_all x1, blocking collectives, on_device(): lax.all_to_all(partial, 'etp', 0, 0, tiled=True, axis_index_groups=along_y)  12.3 us
    all_to_all x1, blocking collectives, on_device(): lax.all_to_all(back, 'etp', 0, 0, tiled=True, axis_index_groups=along_x)  12.1 us
    all_to_all x1, blocking collectives, on_device(): lax.all_to_all(grads, 'etp', 0, 0, tiled=True, axis_index_groups=along_y)  8.25 us
  transfers between devices with their start and end apart: 8, of which 3 were waited for; matrix products, arithmetic and copies ran while one was open for 0% of the time, Pallas kernels for 4%

profile of v8, /device:TPU:1, one launch (start us, length us, event | category | flops | bytes accessed | tf_op | source)
XLA Modules:
  0.0 195.3 jit_solution(279730299797005835)
XLA Ops:
  0.0 2.5 %dispatch_rows.1 = (bf16[64,2,1152]{2,1,0:T(2,128)(2,1)}, f32[5,64,16]{2,1,0:T(8,128)}) custom-call(s32[8,16]{1,0:T(8,128)} %bitcast.23, f32[8,16]{1,0:T(8,128)} %bitcast.24, bf16[16,448]{1,0:T(8,128)(2,1)} %tokens_any.1, bf16[16,448]{1,0:T(8,128)(2,1)} %grads_any.1), custom_call_target="tpu_custom_call" | custom-call | bytes 500000 | tf_op jit(solution)/shard_map/dispatch_rows/pallas_call | solution.py:127
  2.5 30.4 %all-to-all-start = ((bf16[64,2,1152]{2,1,0:T(2,128)(2,1)}), bf16[64,2,1152]{2,1,0:T(2,128)(2,1)S(1)}, u32[]{:S(2)}, u32[]{:S(2)}) async-start(bf16[64,2,1152]{2,1,0:T(2,128)(2,1)} %get-tuple-element.17), calls=%async_computation | async-start | bytes 589824 | tf_op jit(solution)/shard_map/all_to_all | solution.py:291
  33.0 2.0 %pack_2.1 = (bf16[1344,128]{1,0:T(8,128)(2,1)}, bf16[1344,128]{1,0:T(8,128)(2,1)}) custom-call(bf16[3584,128]{1,0:T(8,128)(2,1)} %bitcast.13, bf16[3584,128]{1,0:T(8,128)(2,1)} %bitcast.16, bf16[128,3584]{1,0:T(8,128)(2,1)} %bitcast.19), custom_call_target="tpu_custom_call" | custom-call | bytes 3000000 | tf_op jit(solution)/shard_map/pack_2/pallas_call | solution.py:70
  35.0 3.2 %collective-permute-start.2 = (bf16[1344,128]{1,0:T(8,128)(2,1)}, bf16[1344,128]{1,0:T(8,128)(2,1)S(1)}, u32[]{:S(2)}, u32[]{:S(2)}) collective-permute-start(bf16[1344,128]{1,0:T(8,128)(2,1)} %get-tuple-element.20), channel_id=1, source_target_pairs={{0,4},{1,5},{2,6},{3,7},{4,8},{5,9},{6,10},{7,11},{8,12},{9,13},{1... | collective-permute-start | bytes 1032200 | tf_op jit(solution)/shard_map/ppermute | solution.py:281
  38.2 3.4 %collective-permute-start.4 = (bf16[1344,128]{1,0:T(8,128)(2,1)}, bf16[1344,128]{1,0:T(8,128)(2,1)S(1)}, u32[]{:S(2)}, u32[]{:S(2)}) collective-permute-start(bf16[1344,128]{1,0:T(8,128)(2,1)} %get-tuple-element.21), channel_id=1, source_target_pairs={{0,12},{1,13},{2,14},{3,15},{4,0},{5,1},{6,2},{7,3},{8,4},{9,5},{1... | collective-permute-start | bytes 1032200 | tf_op jit(solution)/shard_map/ppermute | solution.py:281
  41.6 2.6 %pack_1.1 = (bf16[2688,128]{1,0:T(8,128)(2,1)}, bf16[2688,128]{1,0:T(8,128)(2,1)}) custom-call(bf16[3584,128]{1,0:T(8,128)(2,1)} %bitcast.14, bf16[3584,128]{1,0:T(8,128)(2,1)} %bitcast.17, bf16[128,3584]{1,0:T(8,128)(2,1)} %bitcast.20), custom_call_target="tpu_custom_call" | custom-call | bytes 3000000 | tf_op jit(solution)/shard_map/pack_1/pallas_call | solution.py:70
  44.2 3.4 %collective-permute-start = (bf16[2688,128]{1,0:T(8,128)(2,1)}, bf16[2688,128]{1,0:T(8,128)(2,1)S(1)}, u32[]{:S(2)}, u32[]{:S(2)}) collective-permute-start(bf16[2688,128]{1,0:T(8,128)(2,1)} %get-tuple-element.18), channel_id=1, source_target_pairs={{0,12},{1,13},{2,14},{3,15},{4,0},{5,1},{6,2},{7,3},{8,4},{9,5},{1... | collective-permute-start | bytes 2064392 | tf_op jit(solution)/shard_map/ppermute | solution.py:281
  47.6 1.9 collective-permute-start.1
  49.5 0.0 collective-permute-done.2
  49.5 1.9 collective-permute-start.3
  51.5 0.0 collective-permute-done.4
  51.5 4.6 %collective-permute-start.5 = (bf16[1344,128]{1,0:T(8,128)(2,1)S(1)}, bf16[1344,128]{1,0:T(8,128)(2,1)S(1)}, u32[]{:S(2)}, u32[]{:S(2)}) collective-permute-start(bf16[1344,128]{1,0:T(8,128)(2,1)S(1)} %collective-permute-done.4), channel_id=1, source_target_pairs={{0,12},{1,13},{2,14},{3,15},{4,0},{5,1},{6,2},{7,3},{8,4},{9,5},{1... | collective-permute-start | bytes 1032200 | tf_op jit(solution)/shard_map/ppermute | solution.py:281
  56.1 2.0 %pack_0.1.own = bf16[2688,128]{1,0:T(8,128)(2,1)} custom-call(bf16[3584,128]{1,0:T(8,128)(2,1)} %bitcast.15, bf16[3584,128]{1,0:T(8,128)(2,1)} %bitcast.18, bf16[128,3584]{1,0:T(8,128)(2,1)} %bitcast.21), custom_call_target="tpu_custom_call" | custom-call | bytes 3000000 | tf_op jit(solution)/shard_map/pack_0/pallas_call | solution.py:70
  58.1 15.8 %collective-permute-done.3.far_low = bf16[1344,128]{1,0:T(8,128)(2,1)S(1)} collective-permute-done((bf16[1344,128]{1,0:T(8,128)(2,1)S(1)}, bf16[1344,128]{1,0:T(8,128)(2,1)S(1)}, u32[]{:S(2)}, u32[]{:S(2)}) %collective-permute-start.3) | collective-permute-done | bytes 344096 | tf_op jit(solution)/shard_map/ppermute | solution.py:281
  73.9 0.0 collective-permute-done.5.far_high
  73.9 0.0 collective-permute-done.ahead
  73.9 0.0 collective-permute-done.1.behind
  73.9 3.9 %all-to-all-done = bf16[64,2,1152]{2,1,0:T(2,128)(2,1)S(1)} async-done(((bf16[64,2,1152]{2,1,0:T(2,128)(2,1)}), bf16[64,2,1152]{2,1,0:T(2,128)(2,1)S(1)}, u32[]{:S(2)}, u32[]{:S(2)}) %all-to-all-start) | async-done | bytes 294944 | tf_op jit(solution)/shard_map/all_to_all | solution.py:291
  77.9 0.1 broadcast_in_dim.4
  78.0 0.0 copy-start
  78.0 18.8 %all_to_all.30 = bf16[4,64,2,1152]{3,1,2,0:T(8,128)(2,1)S(1)} all-to-all(bf16[4,64,2,1152]{3,1,2,0:T(8,128)(2,1)S(1)} %broadcast_in_dim.4), channel_id=1, replica_groups={{0,1,2,3},{4,5,6,7},{8,9,10,11},{12,13,14,15},{16,17,18,19},{20,21,22,2..., dimensions={0} | all-to-all | bytes 2359296 | tf_op jit(solution)/shard_map/all_to_all | solution.py:294
  96.8 0.0 copy-done
  96.8 0.9 forward_send.1
  97.8 4.5 %collective-permute-start.6 = (bf16[4,3,160,128]{3,2,1,0:T(8,128)(2,1)S(1)}, bf16[4,3,160,128]{3,2,1,0:T(8,128)(2,1)S(1)}, u32[]{:S(2)}, u32[]{:S(2)}) collective-permute-start(bf16[4,3,160,128]{3,2,1,0:T(8,128)(2,1)S(1)} %forward_send.1), channel_id=1, source_target_pairs={{0,16},{16,0},{32,48},{48,32},{64,80},{80,64},{96,112},{112,96},{1... | collective-permute-start | bytes 1474568 | tf_op jit(solution)/shard_map/ppermute | solution.py:302
  102.3 0.9 forward_keep.1
  103.3 0.5 collective-permute-done.6
  103.8 0.1 add_convert_fusion
  103.9 12.3 %all_to_all.31 = bf16[4,3,160,128]{3,2,1,0:T(8,128)(2,1)S(1)} all-to-all(bf16[4,3,160,128]{3,2,1,0:T(8,128)(2,1)S(1)} %add_convert_fusion), channel_id=1, replica_groups={{0,4,8,12},{1,5,9,13},{2,6,10,14},{3,7,11,15},{16,20,24,28},{17,21,25,2..., dimensions={0} | all-to-all | bytes 983040 | tf_op jit(solution)/shard_map/all_to_all | solution.py:307
  116.2 0.1 convert_reduce_fusion
  116.3 0.1 fusion.2
  116.4 8.3 %all_to_all.32 = bf16[4,2,160,128]{3,2,1,0:T(8,128)(2,1)S(1)} all-to-all(bf16[4,2,160,128]{3,2,1,0:T(8,128)(2,1)S(1)} %broadcast_in_dim.5), channel_id=1, replica_groups={{0,4,8,12},{1,5,9,13},{2,6,10,14},{3,7,11,15},{16,20,24,28},{17,21,25,2..., dimensions={0} | all-to-all | bytes 655360 | tf_op jit(solution)/shard_map/all_to_all | solution.py:313
  124.7 4.8 %all-gather = bf16[8,2,160,128]{3,2,1,0:T(8,128)(2,1)S(1)} all-gather(bf16[4,2,160,128]{3,2,1,0:T(8,128)(2,1)S(1)} %all_to_all.32), channel_id=2, replica_groups={{0,16},{32,48},{64,80},{96,112},{128,144},{160,176},{192,208},{224,240}..., dimensions={0}, use_global_device_ids=true | all-gather | bytes 983040 | tf_op jit(solution)/shard_map/all_gather | solution.py:314
  129.4 0.9 backward_parts.1
  130.4 0.0 copy-start.1
  130.4 12.1 %all_to_all.33.parts_ref = bf16[4,64,1152]{2,1,0:T(8,128)(2,1)S(1)} all-to-all(bf16[4,64,1152]{2,1,0:T(8,128)(2,1)S(1)} %backward_parts.1), channel_id=1, replica_groups={{0,1,2,3},{4,5,6,7},{8,9,10,11},{12,13,14,15},{16,17,18,19},{20,21,22,2..., dimensions={0} | all-to-all | bytes 1179648 | tf_op jit(solution)/shard_map/all_to_all | solution.py:318
  142.5 0.2 gather_rows.1
  142.7 51.6 %all_to_all.34 = bf16[64,2,640]{2,1,0:T(2,128)(2,1)S(1)} all-to-all(bf16[64,2,640]{2,1,0:T(2,128)(2,1)S(1)} %gather_rows.1), channel_id=1, replica_groups=mesh['ep'=64,'etp'=16] {'ep'}, dimensions={0} | all-to-all | bytes 327680 | tf_op jit(solution)/shard_map/all_to_all | solution.py:320
  194.3 0.0 copy-done.1
  194.3 0.9 combine_rows.1
  (4 shorter events, 0.1 us)
Async XLA Ops:
  2.5 75.3 %all-to-all-start = ((bf16[64,2,1152]{2,1,0:T(2,128)(2,1)}), bf16[64,2,1152]{2,1,0:T(2,128)(2,1)S(1)}, u32[]{:S(2)}, u32[]{:S(2)}) async-start(bf16[64,2,1152]{2,1,0:T(2,128)(2,1)} %get-tuple-element.17), calls=%async_computation | async-start | bytes 589824 | tf_op jit(solution)/shard_map/all_to_all | solution.py:291
  35.0 14.5 %collective-permute-start.2 = (bf16[1344,128]{1,0:T(8,128)(2,1)}, bf16[1344,128]{1,0:T(8,128)(2,1)S(1)}, u32[]{:S(2)}, u32[]{:S(2)}) collective-permute-start(bf16[1344,128]{1,0:T(8,128)(2,1)} %get-tuple-element.20), channel_id=1, source_target_pairs={{0,4},{1,5},{2,6},{3,7},{4,8},{5,9},{6,10},{7,11},{8,12},{9,13},{1... | collective-permute-start | bytes 1032200 | tf_op jit(solution)/shard_map/ppermute | solution.py:281
  38.2 13.2 %collective-permute-start.4 = (bf16[1344,128]{1,0:T(8,128)(2,1)}, bf16[1344,128]{1,0:T(8,128)(2,1)S(1)}, u32[]{:S(2)}, u32[]{:S(2)}) collective-permute-start(bf16[1344,128]{1,0:T(8,128)(2,1)} %get-tuple-element.21), channel_id=1, source_target_pairs={{0,12},{1,13},{2,14},{3,15},{4,0},{5,1},{6,2},{7,3},{8,4},{9,5},{1... | collective-permute-start | bytes 1032200 | tf_op jit(solution)/shard_map/ppermute | solution.py:281
  44.2 29.7 %collective-permute-start = (bf16[2688,128]{1,0:T(8,128)(2,1)}, bf16[2688,128]{1,0:T(8,128)(2,1)S(1)}, u32[]{:S(2)}, u32[]{:S(2)}) collective-permute-start(bf16[2688,128]{1,0:T(8,128)(2,1)} %get-tuple-element.18), channel_id=1, source_target_pairs={{0,12},{1,13},{2,14},{3,15},{4,0},{5,1},{6,2},{7,3},{8,4},{9,5},{1... | collective-permute-start | bytes 2064392 | tf_op jit(solution)/shard_map/ppermute | solution.py:281
  47.6 26.3 %collective-permute-start.1 = (bf16[2688,128]{1,0:T(8,128)(2,1)}, bf16[2688,128]{1,0:T(8,128)(2,1)S(1)}, u32[]{:S(2)}, u32[]{:S(2)}) collective-permute-start(bf16[2688,128]{1,0:T(8,128)(2,1)} %get-tuple-element.19), channel_id=1, source_target_pairs={{0,4},{1,5},{2,6},{3,7},{4,8},{5,9},{6,10},{7,11},{8,12},{9,13},{1... | collective-permute-start | bytes 2064392 | tf_op jit(solution)/shard_map/ppermute | solution.py:281
  49.5 24.4 %collective-permute-start.3 = (bf16[1344,128]{1,0:T(8,128)(2,1)S(1)}, bf16[1344,128]{1,0:T(8,128)(2,1)S(1)}, u32[]{:S(2)}, u32[]{:S(2)}) collective-permute-start(bf16[1344,128]{1,0:T(8,128)(2,1)S(1)} %collective-permute-done.2), channel_id=1, source_target_pairs={{0,4},{1,5},{2,6},{3,7},{4,8},{5,9},{6,10},{7,11},{8,12},{9,13},{1... | collective-permute-start | bytes 1032200 | tf_op jit(solution)/shard_map/ppermute | solution.py:281
  51.5 22.4 %collective-permute-start.5 = (bf16[1344,128]{1,0:T(8,128)(2,1)S(1)}, bf16[1344,128]{1,0:T(8,128)(2,1)S(1)}, u32[]{:S(2)}, u32[]{:S(2)}) collective-permute-start(bf16[1344,128]{1,0:T(8,128)(2,1)S(1)} %collective-permute-done.4), channel_id=1, source_target_pairs={{0,12},{1,13},{2,14},{3,15},{4,0},{5,1},{6,2},{7,3},{8,4},{9,5},{1... | collective-permute-start | bytes 1032200 | tf_op jit(solution)/shard_map/ppermute | solution.py:281
  78.0 18.8 %copy-start = (bf16[2688,128]{1,0:T(8,128)(2,1)S(1)}, bf16[2688,128]{1,0:T(8,128)(2,1)}, u32[]{:S(2)}) copy-start(bf16[2688,128]{1,0:T(8,128)(2,1)} %pack_0.1.own) | copy-start | bytes 2064388
  97.8 6.0 %collective-permute-start.6 = (bf16[4,3,160,128]{3,2,1,0:T(8,128)(2,1)S(1)}, bf16[4,3,160,128]{3,2,1,0:T(8,128)(2,1)S(1)}, u32[]{:S(2)}, u32[]{:S(2)}) collective-permute-start(bf16[4,3,160,128]{3,2,1,0:T(8,128)(2,1)S(1)} %forward_send.1), channel_id=1, source_target_pairs={{0,16},{16,0},{32,48},{48,32},{64,80},{80,64},{96,112},{112,96},{1... | collective-permute-start | bytes 1474568 | tf_op jit(solution)/shard_map/ppermute | solution.py:302
  130.4 64.0 %copy-start.1 = (f32[5,64,16]{2,1,0:T(8,128)S(1)}, f32[5,64,16]{2,1,0:T(8,128)}, u32[]{:S(2)}) copy-start(f32[5,64,16]{2,1,0:T(8,128)} %get-tuple-element.28.picks_ref) | copy-start | bytes 61444

commit v9 on v8

--- a/solution.py
+++ b/solution.py
@@ -114,7 +114,7 @@
         pick = jnp.where((rank > s - 0.5) & (rank < s + 0.5), member, 0.0)
         picks_out[s] = pick
         one = mm(pick, tokens, NN)
-        two = mm(pick * weight, grads, NN, lax.Precision.HIGHEST)
+        two = mm(pick, grads, NN) * jnp.sum(pick * weight, axis=1, keepdims=True)
         input_parts.append(jnp.where(even, one[:, :half], one[:, half:]))
         grad_parts.append(jnp.where(even, two[:, :half], two[:, half:]))
     fill = jnp.zeros((sides, sent_out.shape[2] - capacity * half), jnp.float32)

time: 196 us -> 196 us (level)
  no operation moved by 1% of the time
where the time goes in v9:
time: 196 us; the launch traced here: 195 us
  blocking collectives  108 us (55%)
  starting transfers between devices  53.3 us (27%)
  waiting for transfers between devices  20.3 us (10%)
  Pallas kernels  12.8 us (7%)
    all_to_all x1, blocking collectives, on_device(): lax.all_to_all(summed, 'ep', split_axis=0, concat_axis=0, tiled=True)  51.5 us
    all_to_all x1, starting transfers between devices, on_device(): came = lax.all_to_all(sent, 'ep', split_axis=0, concat_axis=0, tiled=True)  30.4 us
    all_to_all x1, blocking collectives, on_device(): lax.all_to_all(wide, 'etp', 0, 0, tiled=True, axis_index_groups=along_x)  18.8 us
    ppermute x6, starting transfers between devices, shift(): return lax.ppermute(block, 'etp', pairs)  18.3 us
    ppermute x6, waiting for transfers between devices, shift(): return lax.ppermute(block, 'etp', pairs)  15.8 us
    all_to_all x1, blocking collectives, on_device(): lax.all_to_all(partial, 'etp', 0, 0, tiled=True, axis_index_groups=along_y)  12.3 us
    all_to_all x1, blocking collectives, on_device(): lax.all_to_all(back, 'etp', 0, 0, tiled=True, axis_index_groups=along_x)  12.2 us
    all_to_all x1, blocking collectives, on_device(): lax.all_to_all(grads, 'etp', 0, 0, tiled=True, axis_index_groups=along_y)  8.25 us
  transfers between devices with their start and end apart: 8, of which 3 were waited for; matrix products, arithmetic and copies ran while one was open for 0% of the time, Pallas kernels for 4%

profile of v9, /device:TPU:1, one launch (start us, length us, event | category | flops | bytes accessed | tf_op | source)
XLA Modules:
  0.0 194.9 jit_solution(12703882442594627681)
XLA Ops:
  0.0 2.2 %dispatch_rows.1 = (bf16[64,2,1152]{2,1,0:T(2,128)(2,1)}, f32[5,64,16]{2,1,0:T(8,128)}) custom-call(s32[8,16]{1,0:T(8,128)} %bitcast.23, f32[8,16]{1,0:T(8,128)} %bitcast.24, bf16[16,448]{1,0:T(8,128)(2,1)} %tokens_any.1, bf16[16,448]{1,0:T(8,128)(2,1)} %grads_any.1), custom_call_target="tpu_custom_call" | custom-call | bytes 500000 | tf_op jit(solution)/shard_map/dispatch_rows/pallas_call | solution.py:127
  2.2 30.4 %all-to-all-start = ((bf16[64,2,1152]{2,1,0:T(2,128)(2,1)}), bf16[64,2,1152]{2,1,0:T(2,128)(2,1)S(1)}, u32[]{:S(2)}, u32[]{:S(2)}) async-start(bf16[64,2,1152]{2,1,0:T(2,128)(2,1)} %get-tuple-element.17), calls=%async_computation | async-start | bytes 589824 | tf_op jit(solution)/shard_map/all_to_all | solution.py:291
  32.6 2.0 %pack_2.1 = (bf16[1344,128]{1,0:T(8,128)(2,1)}, bf16[1344,128]{1,0:T(8,128)(2,1)}) custom-call(bf16[3584,128]{1,0:T(8,128)(2,1)} %bitcast.13, bf16[3584,128]{1,0:T(8,128)(2,1)} %bitcast.16, bf16[128,3584]{1,0:T(8,128)(2,1)} %bitcast.19), custom_call_target="tpu_custom_call" | custom-call | bytes 3000000 | tf_op jit(solution)/shard_map/pack_2/pallas_call | solution.py:70
  34.7 3.2 %collective-permute-start.2 = (bf16[1344,128]{1,0:T(8,128)(2,1)}, bf16[1344,128]{1,0:T(8,128)(2,1)S(1)}, u32[]{:S(2)}, u32[]{:S(2)}) collective-permute-start(bf16[1344,128]{1,0:T(8,128)(2,1)} %get-tuple-element.20), channel_id=1, source_target_pairs={{0,4},{1,5},{2,6},{3,7},{4,8},{5,9},{6,10},{7,11},{8,12},{9,13},{1... | collective-permute-start | bytes 1032200 | tf_op jit(solution)/shard_map/ppermute | solution.py:281
  37.9 3.4 %collective-permute-start.4 = (bf16[1344,128]{1,0:T(8,128)(2,1)}, bf16[1344,128]{1,0:T(8,128)(2,1)S(1)}, u32[]{:S(2)}, u32[]{:S(2)}) collective-permute-start(bf16[1344,128]{1,0:T(8,128)(2,1)} %get-tuple-element.21), channel_id=1, source_target_pairs={{0,12},{1,13},{2,14},{3,15},{4,0},{5,1},{6,2},{7,3},{8,4},{9,5},{1... | collective-permute-start | bytes 1032200 | tf_op jit(solution)/shard_map/ppermute | solution.py:281
  41.2 2.6 %pack_1.1 = (bf16[2688,128]{1,0:T(8,128)(2,1)}, bf16[2688,128]{1,0:T(8,128)(2,1)}) custom-call(bf16[3584,128]{1,0:T(8,128)(2,1)} %bitcast.14, bf16[3584,128]{1,0:T(8,128)(2,1)} %bitcast.17, bf16[128,3584]{1,0:T(8,128)(2,1)} %bitcast.20), custom_call_target="tpu_custom_call" | custom-call | bytes 3000000 | tf_op jit(solution)/shard_map/pack_1/pallas_call | solution.py:70
  43.9 3.4 %collective-permute-start = (bf16[2688,128]{1,0:T(8,128)(2,1)}, bf16[2688,128]{1,0:T(8,128)(2,1)S(1)}, u32[]{:S(2)}, u32[]{:S(2)}) collective-permute-start(bf16[2688,128]{1,0:T(8,128)(2,1)} %get-tuple-element.18), channel_id=1, source_target_pairs={{0,12},{1,13},{2,14},{3,15},{4,0},{5,1},{6,2},{7,3},{8,4},{9,5},{1... | collective-permute-start | bytes 2064392 | tf_op jit(solution)/shard_map/ppermute | solution.py:281
  47.3 1.9 collective-permute-start.1
  49.2 0.0 collective-permute-done.2
  49.2 1.9 collective-permute-start.3
  51.1 0.0 collective-permute-done.4
  51.1 4.6 %collective-permute-start.5 = (bf16[1344,128]{1,0:T(8,128)(2,1)S(1)}, bf16[1344,128]{1,0:T(8,128)(2,1)S(1)}, u32[]{:S(2)}, u32[]{:S(2)}) collective-permute-start(bf16[1344,128]{1,0:T(8,128)(2,1)S(1)} %collective-permute-done.4), channel_id=1, source_target_pairs={{0,12},{1,13},{2,14},{3,15},{4,0},{5,1},{6,2},{7,3},{8,4},{9,5},{1... | collective-permute-start | bytes 1032200 | tf_op jit(solution)/shard_map/ppermute | solution.py:281
  55.7 2.0 %pack_0.1.own = bf16[2688,128]{1,0:T(8,128)(2,1)} custom-call(bf16[3584,128]{1,0:T(8,128)(2,1)} %bitcast.15, bf16[3584,128]{1,0:T(8,128)(2,1)} %bitcast.18, bf16[128,3584]{1,0:T(8,128)(2,1)} %bitcast.21), custom_call_target="tpu_custom_call" | custom-call | bytes 3000000 | tf_op jit(solution)/shard_map/pack_0/pallas_call | solution.py:70
  57.7 15.8 %collective-permute-done.3.far_low = bf16[1344,128]{1,0:T(8,128)(2,1)S(1)} collective-permute-done((bf16[1344,128]{1,0:T(8,128)(2,1)S(1)}, bf16[1344,128]{1,0:T(8,128)(2,1)S(1)}, u32[]{:S(2)}, u32[]{:S(2)}) %collective-permute-start.3) | collective-permute-done | bytes 344096 | tf_op jit(solution)/shard_map/ppermute | solution.py:281
  73.6 0.0 collective-permute-done.5.far_high
  73.6 0.0 collective-permute-done.ahead
  73.6 0.0 collective-permute-done.1.behind
  73.6 3.9 %all-to-all-done = bf16[64,2,1152]{2,1,0:T(2,128)(2,1)S(1)} async-done(((bf16[64,2,1152]{2,1,0:T(2,128)(2,1)}), bf16[64,2,1152]{2,1,0:T(2,128)(2,1)S(1)}, u32[]{:S(2)}, u32[]{:S(2)}) %all-to-all-start) | async-done | bytes 294944 | tf_op jit(solution)/shard_map/all_to_all | solution.py:291
  77.5 0.1 broadcast_in_dim.4
  77.7 0.0 copy-start
  77.7 18.8 %all_to_all.30 = bf16[4,64,2,1152]{3,1,2,0:T(8,128)(2,1)S(1)} all-to-all(bf16[4,64,2,1152]{3,1,2,0:T(8,128)(2,1)S(1)} %broadcast_in_dim.4), channel_id=1, replica_groups={{0,1,2,3},{4,5,6,7},{8,9,10,11},{12,13,14,15},{16,17,18,19},{20,21,22,2..., dimensions={0} | all-to-all | bytes 2359296 | tf_op jit(solution)/shard_map/all_to_all | solution.py:294
  96.5 0.0 copy-done
  96.5 0.9 forward_send.1
  97.4 4.5 %collective-permute-start.6 = (bf16[4,3,160,128]{3,2,1,0:T(8,128)(2,1)S(1)}, bf16[4,3,160,128]{3,2,1,0:T(8,128)(2,1)S(1)}, u32[]{:S(2)}, u32[]{:S(2)}) collective-permute-start(bf16[4,3,160,128]{3,2,1,0:T(8,128)(2,1)S(1)} %forward_send.1), channel_id=1, source_target_pairs={{0,16},{16,0},{32,48},{48,32},{64,80},{80,64},{96,112},{112,96},{1... | collective-permute-start | bytes 1474568 | tf_op jit(solution)/shard_map/ppermute | solution.py:302
  102.0 0.9 forward_keep.1
  102.9 0.5 collective-permute-done.6
  103.4 0.1 add_convert_fusion
  103.5 12.3 %all_to_all.31 = bf16[4,3,160,128]{3,2,1,0:T(8,128)(2,1)S(1)} all-to-all(bf16[4,3,160,128]{3,2,1,0:T(8,128)(2,1)S(1)} %add_convert_fusion), channel_id=1, replica_groups={{0,4,8,12},{1,5,9,13},{2,6,10,14},{3,7,11,15},{16,20,24,28},{17,21,25,2..., dimensions={0} | all-to-all | bytes 983040 | tf_op jit(solution)/shard_map/all_to_all | solution.py:307
  115.9 0.1 convert_reduce_fusion
  115.9 0.1 fusion.2
  116.1 8.3 %all_to_all.32 = bf16[4,2,160,128]{3,2,1,0:T(8,128)(2,1)S(1)} all-to-all(bf16[4,2,160,128]{3,2,1,0:T(8,128)(2,1)S(1)} %broadcast_in_dim.5), channel_id=1, replica_groups={{0,4,8,12},{1,5,9,13},{2,6,10,14},{3,7,11,15},{16,20,24,28},{17,21,25,2..., dimensions={0} | all-to-all | bytes 655360 | tf_op jit(solution)/shard_map/all_to_all | solution.py:313
  124.3 4.8 %all-gather = bf16[8,2,160,128]{3,2,1,0:T(8,128)(2,1)S(1)} all-gather(bf16[4,2,160,128]{3,2,1,0:T(8,128)(2,1)S(1)} %all_to_all.32), channel_id=2, replica_groups={{0,16},{32,48},{64,80},{96,112},{128,144},{160,176},{192,208},{224,240}..., dimensions={0}, use_global_device_ids=true | all-gather | bytes 983040 | tf_op jit(solution)/shard_map/all_gather | solution.py:314
  129.1 0.9 backward_parts.1
  130.0 0.0 copy-start.1
  130.0 12.2 %all_to_all.33.parts_ref = bf16[4,64,1152]{2,1,0:T(8,128)(2,1)S(1)} all-to-all(bf16[4,64,1152]{2,1,0:T(8,128)(2,1)S(1)} %backward_parts.1), channel_id=1, replica_groups={{0,1,2,3},{4,5,6,7},{8,9,10,11},{12,13,14,15},{16,17,18,19},{20,21,22,2..., dimensions={0} | all-to-all | bytes 1179648 | tf_op jit(solution)/shard_map/all_to_all | solution.py:318
  142.2 0.2 gather_rows.1
  142.4 51.5 %all_to_all.34 = bf16[64,2,640]{2,1,0:T(2,128)(2,1)S(1)} all-to-all(bf16[64,2,640]{2,1,0:T(2,128)(2,1)S(1)} %gather_rows.1), channel_id=1, replica_groups=mesh['ep'=64,'etp'=16] {'ep'}, dimensions={0} | all-to-all | bytes 327680 | tf_op jit(solution)/shard_map/all_to_all | solution.py:320
  194.0 0.0 copy-done.1
  194.0 0.9 combine_rows.1
  (4 shorter events, 0.1 us)
Async XLA Ops:
  2.2 75.3 %all-to-all-start = ((bf16[64,2,1152]{2,1,0:T(2,128)(2,1)}), bf16[64,2,1152]{2,1,0:T(2,128)(2,1)S(1)}, u32[]{:S(2)}, u32[]{:S(2)}) async-start(bf16[64,2,1152]{2,1,0:T(2,128)(2,1)} %get-tuple-element.17), calls=%async_computation | async-start | bytes 589824 | tf_op jit(solution)/shard_map/all_to_all | solution.py:291
  34.7 14.5 %collective-permute-start.2 = (bf16[1344,128]{1,0:T(8,128)(2,1)}, bf16[1344,128]{1,0:T(8,128)(2,1)S(1)}, u32[]{:S(2)}, u32[]{:S(2)}) collective-permute-start(bf16[1344,128]{1,0:T(8,128)(2,1)} %get-tuple-element.20), channel_id=1, source_target_pairs={{0,4},{1,5},{2,6},{3,7},{4,8},{5,9},{6,10},{7,11},{8,12},{9,13},{1... | collective-permute-start | bytes 1032200 | tf_op jit(solution)/shard_map/ppermute | solution.py:281
  37.9 13.2 %collective-permute-start.4 = (bf16[1344,128]{1,0:T(8,128)(2,1)}, bf16[1344,128]{1,0:T(8,128)(2,1)S(1)}, u32[]{:S(2)}, u32[]{:S(2)}) collective-permute-start(bf16[1344,128]{1,0:T(8,128)(2,1)} %get-tuple-element.21), channel_id=1, source_target_pairs={{0,12},{1,13},{2,14},{3,15},{4,0},{5,1},{6,2},{7,3},{8,4},{9,5},{1... | collective-permute-start | bytes 1032200 | tf_op jit(solution)/shard_map/ppermute | solution.py:281
  43.9 29.7 %collective-permute-start = (bf16[2688,128]{1,0:T(8,128)(2,1)}, bf16[2688,128]{1,0:T(8,128)(2,1)S(1)}, u32[]{:S(2)}, u32[]{:S(2)}) collective-permute-start(bf16[2688,128]{1,0:T(8,128)(2,1)} %get-tuple-element.18), channel_id=1, source_target_pairs={{0,12},{1,13},{2,14},{3,15},{4,0},{5,1},{6,2},{7,3},{8,4},{9,5},{1... | collective-permute-start | bytes 2064392 | tf_op jit(solution)/shard_map/ppermute | solution.py:281
  47.3 26.3 %collective-permute-start.1 = (bf16[2688,128]{1,0:T(8,128)(2,1)}, bf16[2688,128]{1,0:T(8,128)(2,1)S(1)}, u32[]{:S(2)}, u32[]{:S(2)}) collective-permute-start(bf16[2688,128]{1,0:T(8,128)(2,1)} %get-tuple-element.19), channel_id=1, source_target_pairs={{0,4},{1,5},{2,6},{3,7},{4,8},{5,9},{6,10},{7,11},{8,12},{9,13},{1... | collective-permute-start | bytes 2064392 | tf_op jit(solution)/shard_map/ppermute | solution.py:281
  49.2 24.4 %collective-permute-start.3 = (bf16[1344,128]{1,0:T(8,128)(2,1)S(1)}, bf16[1344,128]{1,0:T(8,128)(2,1)S(1)}, u32[]{:S(2)}, u32[]{:S(2)}) collective-permute-start(bf16[1344,128]{1,0:T(8,128)(2,1)S(1)} %collective-permute-done.2), channel_id=1, source_target_pairs={{0,4},{1,5},{2,6},{3,7},{4,8},{5,9},{6,10},{7,11},{8,12},{9,13},{1... | collective-permute-start | bytes 1032200 | tf_op jit(solution)/shard_map/ppermute | solution.py:281
  51.1 22.4 %collective-permute-start.5 = (bf16[1344,128]{1,0:T(8,128)(2,1)S(1)}, bf16[1344,128]{1,0:T(8,128)(2,1)S(1)}, u32[]{:S(2)}, u32[]{:S(2)}) collective-permute-start(bf16[1344,128]{1,0:T(8,128)(2,1)S(1)} %collective-permute-done.4), channel_id=1, source_target_pairs={{0,12},{1,13},{2,14},{3,15},{4,0},{5,1},{6,2},{7,3},{8,4},{9,5},{1... | collective-permute-start | bytes 1032200 | tf_op jit(solution)/shard_map/ppermute | solution.py:281
  77.7 18.8 %copy-start = (bf16[2688,128]{1,0:T(8,128)(2,1)S(1)}, bf16[2688,128]{1,0:T(8,128)(2,1)}, u32[]{:S(2)}) copy-start(bf16[2688,128]{1,0:T(8,128)(2,1)} %pack_0.1.own) | copy-start | bytes 2064388
  97.4 6.0 %collective-permute-start.6 = (bf16[4,3,160,128]{3,2,1,0:T(8,128)(2,1)S(1)}, bf16[4,3,160,128]{3,2,1,0:T(8,128)(2,1)S(1)}, u32[]{:S(2)}, u32[]{:S(2)}) collective-permute-start(bf16[4,3,160,128]{3,2,1,0:T(8,128)(2,1)S(1)} %forward_send.1), channel_id=1, source_target_pairs={{0,16},{16,0},{32,48},{48,32},{64,80},{80,64},{96,112},{112,96},{1... | collective-permute-start | bytes 1474568 | tf_op jit(solution)/shard_map/ppermute | solution.py:302
  130.0 63.9 %copy-start.1 = (f32[5,64,16]{2,1,0:T(8,128)S(1)}, f32[5,64,16]{2,1,0:T(8,128)}, u32[]{:S(2)}) copy-start(f32[5,64,16]{2,1,0:T(8,128)} %get-tuple-element.28.picks_ref) | copy-start | bytes 61444
